TPU v7x, 256 devices: a whole 4x4x8 slice. The times are simulated.
256 devices in a mesh: replica: 4 (over x_lo, core), shard: 64 (over x_hi, y, z).
Axes of the slice: x: 4 (x_hi: 2, x_lo: 2; x = x_hi * 2 + x_lo), y: 4, z: 8, core: 2. Of those that a mesh axis runs over, the one named last changes fastest.
Arguments:
- tokens: bfloat16 [65536, 18432], P(('replica', 'shard')), may hold values from -24 to 24
- cotangent: bfloat16 [65536, 256], P(('replica', 'shard')), may hold values from -6 to 6
- weight: bfloat16 [18432, 256], P('shard'), may hold values from -0.046875 to 0.046875
- moment_code: bfloat16 [18432, 256], P('shard'), may hold values from -1 to 1
- moment_scale: bfloat16 [18432, 2], P('shard'), may hold values from 0.29882812 to 3
- second_moment: bfloat16 [18432, 256], P('shard'), may hold values from 0.099609375 to 3
Outputs:
- outputs_next: bfloat16 [65536, 256], P(('replica', 'shard'))
- weight_new: bfloat16 [18432, 256], P('shard')
- code_new: bfloat16 [18432, 256], P('shard')
- scale_new: bfloat16 [18432, 2], P('shard')
- second_new: bfloat16 [18432, 256], P('shard')
All inputs are finite; a program needn't handle non-finite values.
Results may differ from a plain program's by a relative error of at most 0.0049.
Values may be sent and summed in bfloat16 or wider, within the bound.
No kernel may reach another device: no remote copies, remote signals or barrier semaphores. Data moves between devices by JAX's collectives and lax.ppermute only.
A program may use at most 128 MiB of HBM per device.

v0:
```python
import math

import jax
import jax.numpy as jnp
from jax import lax
from jax.sharding import PartitionSpec as P


def hadamard_table():
    index = jnp.arange(128, dtype=jnp.int32)
    parity = jnp.zeros((128, 128), jnp.int32)
    for level in range(7):
        left = jnp.bitwise_and(jnp.right_shift(index, level), 1)
        parity = parity + left[:, None] * left[None, :]
    signs = 1 - 2 * jnp.bitwise_and(parity, 1)
    return signs.astype(jnp.float32) / math.sqrt(128.0)


def adam_rows(grad, weight, code, scale, second_old):
    rows, cols = grad.shape
    blocks = cols // 128
    table = hadamard_table()
    stored = (
        code.astype(jnp.float32).reshape(rows, blocks, 128) * scale.astype(jnp.float32)[:, :, None]
    )
    first_old = jnp.einsum("rbk,kj->rbj", stored, table, precision=lax.Precision.HIGHEST).reshape(
        rows, cols
    )
    first = 0.9 * first_old + 0.1 * grad
    second = 0.95 * second_old.astype(jnp.float32) + 0.05 * grad * grad
    weight_new = (weight.astype(jnp.float32) - 0.002 * first / (jnp.sqrt(second) + 1e-08)).astype(
        jnp.bfloat16
    )
    rotated = jnp.einsum(
        "rbk,kj->rbj", first.reshape(rows, blocks, 128), table, precision=lax.Precision.HIGHEST
    )
    scale_new = jnp.max(jnp.abs(rotated), axis=2).astype(jnp.bfloat16)
    scale_back = lax.optimization_barrier(scale_new).astype(jnp.float32)
    code_new = (rotated / (scale_back[:, :, None] + 1e-06)).reshape(rows, cols).astype(jnp.bfloat16)
    return (weight_new, code_new, scale_new, second.astype(jnp.bfloat16))


def per_device(tokens, cotangent, weight, moment_code, moment_scale, second_moment):
    replicas = lax.axis_size("replica")
    shards = lax.axis_size("shard")
    factor = 1.0 / math.sqrt(tokens.shape[0] * replicas * shards)
    contract = (((0,), (0,)), ((), ()))
    summed = lax.psum_scatter(
        lax.dot_general(tokens, cotangent, contract, preferred_element_type=jnp.float32),
        "shard",
        scatter_dimension=0,
        tiled=True,
    )
    grad = lax.psum(summed, "replica") * factor
    weight_new, code_new, scale_new, second_new = adam_rows(
        grad, weight, moment_code, moment_scale, second_moment
    )
    outputs_next = jnp.dot(
        tokens,
        lax.all_gather(weight_new, "shard", axis=0, tiled=True),
        preferred_element_type=jnp.float32,
    )
    return (outputs_next.astype(jnp.bfloat16), weight_new, code_new, scale_new, second_new)


def solution(mesh):
    return jax.shard_map(
        per_device,
        mesh=mesh,
        in_specs=(
            P(("replica", "shard"), None),
            P(("replica", "shard"), None),
            P("shard", None),
            P("shard", None),
            P("shard", None),
            P("shard", None),
        ),
        out_specs=(
            P(("replica", "shard"), None),
            P("shard", None),
            P("shard", None),
            P("shard", None),
            P("shard", None),
        ),
        check_vma=False,
    )
```

profile of v0, /device:TPU:24, one launch (start us, length us, event | category | flops | bytes accessed | tf_op | source)
XLA Modules:
  0.0 1121.9 jit_solution(10863143224817716822)
XLA Ops:
  7.2 0.0 copy-start
  7.2 0.0 reduce-scatter.2.cloned.1.call-start
  7.2 0.8 copy-done
  8.1 12.8 %fusion.18 = f32[18432,256]{1,0:T(8,128)} fusion(bf16[256,18432]{1,0:T(8,128)(2,1)} %param.6, bf16[256,256]{1,0:T(8,128)(2,1)S(1)} %copy-done), kind=kOutput, calls=%fused_computation.37 | convolution fusion | flops 2415919104 | bytes 28442624 | tf_op jit(solution)/shard_map/dot_general | solution.py:49
  20.9 0.0 copy-start.4
  20.9 0.0 copy-start.5
  20.9 0.0 copy-start.1
  20.9 0.0 copy-start.2
  20.9 0.0 reduce-scatter.2.cloned.1.call-update
  20.9 0.0 all-reduce.2.cloned.1.call-start
  21.0 880.1 %reduce-scatter.2.cloned.1.call-done = f32[288,256]{1,0:T(8,128)} async-done(((f32[18432,256]{1,0:T(8,128)}), f32[288,256]{1,0:T(8,128)}) %reduce-scatter.2.cloned.1.call-update) | async-done | bytes 294928 | tf_op jit(solution)/shard_map/reduce_scatter | solution.py:48
  901.1 0.0 all-reduce.2.cloned.1.call-update
  901.1 0.0 all-gather.2.cloned.1.call-start
  901.2 0.0 copy-done.4
  901.2 0.0 copy-done.5
  901.2 0.6 fusion
  901.8 41.7 %all-reduce.2.cloned.1.call-done = f32[288,256]{1,0:T(8,128)} async-done(((f32[288,256]{1,0:T(8,128)}), f32[288,256]{1,0:T(8,128)}) %all-reduce.2.cloned.1.call-update) | async-done | bytes 294928 | tf_op jit(solution)/shard_map/psum | solution.py:54
  943.4 0.0 copy-done.1
  943.4 0.0 copy-done.2
  943.4 1.9 fusion.9
  945.3 0.0 all-gather.2.cloned.1.call-update
  945.4 0.7 abs_reduce_fusion
  946.0 0.0 copy-start.3
  946.1 0.8 copy_bitcast_fusion
  946.9 158.7 %all-gather.2.cloned.1.call-done = bf16[18432,256]{1,0:T(8,128)(2,1)} async-done(((bf16[288,256]{1,0:T(8,128)(2,1)}), bf16[18432,256]{1,0:T(8,128)(2,1)}) %all-gather.2.cloned.1.call-update) | async-done | bytes 9437200 | tf_op jit(solution)/shard_map/all_gather | solution.py:60
  1105.6 9.0 fusion.1
  1114.6 0.0 copy-done.3
  1114.6 0.8 copy.18
  (6 shorter events, 0.0 us)
Async XLA Ops:
  7.2 0.9 copy-start
  7.2 893.9 %reduce-scatter.2.cloned.1.call-start = ((), (), s32[]{:S(2)}) async-start(), calls=%async_computation.1 | async-start | bytes 19169280 | tf_op jit(solution)/shard_map/reduce_scatter | solution.py:48
  20.9 880.3 %copy-start.4 = (bf16[288,2]{0,1:T(2,128)(2,1)S(1)}, bf16[288,2]{0,1:T(2,128)(2,1)}, u32[]{:S(2)}) copy-start(bf16[288,2]{0,1:T(2,128)(2,1)} %param.10) | copy-start | bytes 3460
  20.9 880.3 %copy-start.5 = (bf16[288,256]{1,0:T(8,128)(2,1)S(1)}, bf16[288,256]{1,0:T(8,128)(2,1)}, u32[]{:S(2)}) copy-start(bf16[288,256]{1,0:T(8,128)(2,1)} %param.9) | copy-start | bytes 442372
  20.9 922.5 %copy-start.1 = (bf16[288,256]{1,0:T(8,128)(2,1)S(1)}, bf16[288,256]{1,0:T(8,128)(2,1)}, u32[]{:S(2)}) copy-start(bf16[288,256]{1,0:T(8,128)(2,1)} %param.11) | copy-start | bytes 442372
  20.9 922.5 %copy-start.2 = (bf16[288,256]{1,0:T(8,128)(2,1)S(1)}, bf16[288,256]{1,0:T(8,128)(2,1)}, u32[]{:S(2)}) copy-start(bf16[288,256]{1,0:T(8,128)(2,1)} %param.8) | copy-start | bytes 442372
  20.9 922.5 %all-reduce.2.cloned.1.call-start = ((), (), s32[]{:S(2)}) async-start(), calls=%async_computation.2 | async-start | bytes 589824 | tf_op jit(solution)/shard_map/psum | solution.py:54
  901.1 204.4 %all-gather.2.cloned.1.call-start = ((), (), s32[]{:S(2)}) async-start(), calls=%async_computation.3 | async-start | bytes 9584640 | tf_op jit(solution)/shard_map/all_gather | solution.py:60
  946.0 168.5 %copy-start.3 = (bf16[288,2]{0,1:T(2,128)(2,1)}, bf16[288,2]{0,1:T(2,128)(2,1)S(1)}, u32[]{:S(2)}) copy-start(bf16[288,2]{0,1:T(2,128)(2,1)S(1)} %get-tuple-element.18) | copy-start | bytes 3460
Sparse Core Ops, SparseCore 0:
  21.1 879.9 reduce-scatter.1
  903.7 39.6 all-reduce.1
  947.7 157.7 all-gather.1
where the time goes:
time: 1120 us
  waiting for transfers between devices  1080 us (96%)
  matrix products  23.1 us (2%)
  between operations  13.8 us (1%)
    reduce_scatter x1, waiting for transfers between devices, per_device(): lax.psum_scatter(lax.dot_general(tokens, cotangent, contract, preferred_e...  880 us
    all_gather x1, waiting for transfers between devices, per_device(): lax.all_gather(weight_new, 'shard', axis=0, tiled=True)  159 us
    psum x1, waiting for transfers between devices, per_device(): grad = lax.psum(summed, 'replica') * factor  41.7 us
  transfers between devices with their start and end apart: 3, of which 3 were waited for; matrix products, arithmetic and copies ran while one was open for 0% of the time, Pallas kernels for 0%

commit v1 on v0

v1 whole, which is shorter than its diff:
```python
import math

import jax
import jax.numpy as jnp
from jax import lax
from jax.sharding import Mesh, PartitionSpec as P

AXES = ("xl", "c", "xh", "y", "z")
X = ("xl", "xh")
HALF = 9216
BF = jnp.bfloat16
F32 = jnp.float32


def x_pairs(step):
    where = lambda x: (x % 2) * 2 + x // 2
    return [(where(i), where((i + step) % 4)) for i in range(4)]


def y_pairs(step):
    return [(i, (i + step) % 4) for i in range(4)]


SWAP = [(0, 1), (1, 0)]


def hadamard_table():
    index = jnp.arange(128, dtype=jnp.int32)
    parity = jnp.zeros((128, 128), jnp.int32)
    for level in range(7):
        left = jnp.bitwise_and(jnp.right_shift(index, level), 1)
        parity = parity + left[:, None] * left[None, :]
    signs = 1 - 2 * jnp.bitwise_and(parity, 1)
    return signs.astype(F32) / math.sqrt(128.0)


def rotate(values, table):
    return jnp.einsum("brk,kj->brj", values, table, precision=lax.Precision.HIGHEST)


def adam(grad, weight, code, scale, second_old):
    table = hadamard_table()
    first_old = rotate(code.astype(F32) * scale.astype(F32), table)
    first = 0.9 * first_old + 0.1 * grad
    second = 0.95 * second_old.astype(F32) + 0.05 * grad * grad
    weight_new = (weight.astype(F32) - 0.002 * first / (jnp.sqrt(second) + 1e-08)).astype(BF)
    rotated = rotate(first, table)
    scale_new = jnp.max(jnp.abs(rotated), axis=2, keepdims=True).astype(BF)
    scale_back = lax.optimization_barrier(scale_new).astype(F32)
    code_new = (rotated / (scale_back + 1e-06)).astype(BF)
    return weight_new, code_new, scale_new, second.astype(BF)


def at(array, index, axis):
    return lax.dynamic_index_in_dim(array, index, axis, keepdims=False)


def per_device(tokens, cotangent, weight, code, scale, second_old):
    c = lax.axis_index("c")
    xh = lax.axis_index("xh")
    x = xh * 2 + lax.axis_index("xl")
    y = lax.axis_index("y")

    state = jnp.concatenate([weight, code, second_old, jnp.pad(scale, ((0, 0), (0, 126)))], axis=1)
    state = state.reshape(4, 72, 896)
    got = lax.ppermute(at(state, (x + 2) % 4, 0), "xh", SWAP)
    mine = jnp.where(xh == c, at(state, x, 0), got)

    def blocks(array):
        return array.reshape(72, 2, 128).transpose(1, 0, 2)

    weight_m = blocks(mine[:, :256])
    code_m = blocks(mine[:, 256:512])
    second_m = blocks(mine[:, 512:768])
    scale_m = mine[:, 768:770].T[:, :, None]

    own = lax.dynamic_slice(tokens, (0, c * HALF), (256, HALF))
    other = lax.ppermute(lax.dynamic_slice(tokens, (0, (1 - c) * HALF), (256, HALF)), "c", SWAP)
    cot_other = lax.ppermute(cotangent, "c", SWAP)
    contract = (((0,), (0,)), ((), ()))
    grad = lax.dot_general(own, cotangent, contract, preferred_element_type=F32)
    grad = grad + lax.dot_general(other, cot_other, contract, preferred_element_type=F32)
    grad = grad.reshape(4, 8, 4, 72, 256)

    def reduce_over(term, axis, pairs, place, dim):
        sent = term.astype(BF)
        total = at(term, place, dim)
        for step in (2, 1, 3):
            total = total + lax.ppermute(at(sent, (place + step) % 4, dim), axis, pairs(step)).astype(F32)
        return total

    a = reduce_over(grad[..., :128], X, x_pairs, x, 2)
    b = reduce_over(grad[..., 128:], "y", y_pairs, y, 0)
    a = reduce_over(a, "y", y_pairs, y, 0)
    b = reduce_over(b, X, x_pairs, x, 1)
    ab = lax.all_to_all(jnp.stack([a, b], axis=1), "z", 0, 0, tiled=True)
    grad_m = jnp.sum(ab, axis=0) * (1.0 / 256.0)

    weight_new, code_new, scale_new, second_new = adam(grad_m, weight_m, code_m, scale_m, second_m)

    def rows(array):
        return array.transpose(1, 0, 2).reshape(72, 256)

    def gather(block, axis, pairs, place, dim):
        parts = [block] + [lax.ppermute(block, axis, pairs(step)) for step in (3, 2, 1)]
        twice = jnp.stack(parts + parts, axis=dim)
        return lax.dynamic_slice_in_dim(twice, (4 - place) % 4, 4, dim)

    made = jnp.concatenate(
        [rows(weight_new), rows(code_new), rows(second_new), jnp.pad(scale_new[:, :, 0].T, ((0, 0), (0, 126)))], axis=1
    )
    made = gather(made, X, x_pairs, x, 0)
    made = jnp.where(xh == c, made, lax.ppermute(made, "c", SWAP)).reshape(288, 896)

    ab = lax.all_to_all(jnp.broadcast_to(weight_new[None], (8, 2, 72, 128)), "z", 0, 0, tiled=True)
    a = gather(ab[:, 0], "y", y_pairs, y, 0)
    b = gather(ab[:, 1], X, x_pairs, x, 1)
    a = gather(a, X, x_pairs, x, 2).reshape(HALF, 128)
    b = gather(b, "y", y_pairs, y, 0).reshape(HALF, 128)
    slab = jnp.concatenate([a, b], axis=1)
    part_other = lax.ppermute(jnp.dot(other, slab, preferred_element_type=F32), "c", SWAP)
    outputs = jnp.dot(own, slab, preferred_element_type=F32) + part_other
    return (outputs.astype(BF), made[:, :256], made[:, 256:512], made[:, 768:770], made[:, 512:768])


def solution(mesh):
    split = Mesh(mesh.devices.reshape(2, 2, 2, 4, 8), AXES)
    tokens = P(AXES, None)
    shard = P(("xh", "y", "z"), None)
    return jax.shard_map(
        per_device,
        mesh=split,
        in_specs=(tokens, tokens, shard, shard, shard, shard),
        out_specs=(tokens, shard, shard, shard, shard),
        check_vma=False,
    )
```

time: 1120 us -> 193 us (0.17)
  waiting for transfers between devices: 1080 us -> 93 us
  starting transfers between devices: 0.12 us -> 50.9 us
  local copies, waits for them, and re-layouts: 1.64 us -> 16.2 us
  between operations: 13.8 us -> 1.28 us
    reduce_scatter x1 -> x0, waiting for transfers between devices: 880 us -> none  [per_device(): lax.psum_scatter(lax.dot_general(tokens, cotangent, contract, preferred_e...]
    all_gather x1 -> x0, waiting for transfers between devices: 159 us -> none  [per_device(): lax.all_gather(weight_new, 'shard', axis=0, tiled=True)]
    ppermute x0 -> x32, waiting for transfers between devices: none -> 68.7 us  [the longest x15 45.5 us: gather(): lax.ppermute(block, axis, pairs(step))]
    psum x1 -> x0, waiting for transfers between devices: 41.7 us -> none  [per_device(): grad = lax.psum(summed, 'replica') * factor]
    ppermute x0 -> x32, starting transfers between devices: none -> 39 us  [the longest x15 18.6 us: gather(): lax.ppermute(block, axis, pairs(step))]
    all_to_all x0 -> x2, waiting for transfers between devices: none -> 24.3 us  [the longest x1 17 us: per_device(): ab = lax.all_to_all(jnp.stack([a, b], axis=1), 'z', 0, 0, tiled=True)]
    all_to_all x0 -> x2, starting transfers between devices: none -> 11.9 us  [the longest x1 8.47 us: per_device(): ab = lax.all_to_all(jnp.stack([a, b], axis=1), 'z', 0, 0, tiled=True)]
    dot_general x4 -> x6, matrix products: 23.1 us -> 25.4 us  [the longest x1 7.45 us: per_device(): grad = lax.dot_general(own, cotangent, contract, preferred_element_type=F32)]
  transfers between devices with their start and end apart: 3 -> 34, of which waited for: 3 -> 21; matrix products, arithmetic and copies ran while one was open for 0% -> 13% of each run, Pallas kernels for 0% -> 0%
where the time goes in v1:
time: 193 us; the launch traced here: 192 us
  waiting for transfers between devices  93 us (48%)
  starting transfers between devices  50.9 us (26%)
  matrix products  25.4 us (13%)
  local copies, waits for them, and re-layouts  16.2 us (8%)
  other arithmetic  5.04 us (3%)
    ppermute x15, waiting for transfers between devices, gather(): lax.ppermute(block, axis, pairs(step))  45.5 us
    ppermute x12, waiting for transfers between devices, reduce_over(): lax.ppermute(at(sent, (place + step) % 4, dim), axis, pairs(step))  22.6 us
    ppermute x15, starting transfers between devices, gather(): lax.ppermute(block, axis, pairs(step))  18.6 us
    all_to_all x1, waiting for transfers between devices, per_device(): ab = lax.all_to_all(jnp.stack([a, b], axis=1), 'z', 0, 0, tiled=True)  17 us
    ppermute x12, starting transfers between devices, reduce_over(): lax.ppermute(at(sent, (place + step) % 4, dim), axis, pairs(step))  16.8 us
    all_to_all x1, starting transfers between devices, per_device(): ab = lax.all_to_all(jnp.stack([a, b], axis=1), 'z', 0, 0, tiled=True)  8.47 us
    dot_general x1, matrix products, per_device(): grad = lax.dot_general(own, cotangent, contract, preferred_element_type=F32)  7.45 us
    all_to_all x1, waiting for transfers between devices, per_device(): lax.all_to_all(jnp.broadcast_to(weight_new[None], (8, 2, 72, 128)), 'z',...  7.27 us
  transfers between devices with their start and end apart: 34, of which 21 were waited for; matrix products, arithmetic and copies ran while one was open for 13% of the time, Pallas kernels for 0%

profile of v1, /device:TPU:24, one launch (start us, length us, event | category | flops | bytes accessed | tf_op | source)
XLA Modules:
  0.0 191.8 jit_solution(258350628344322445)
XLA Ops:
  0.6 4.8 %constant_dynamic-slice_fusion.5 = bf16[256,9216]{1,0:T(8,128)(2,1)} fusion(bf16[256,18432]{1,0:T(8,128)(2,1)} %param.6, s32[]{:T(128)S(6)} %select_n.135), kind=kLoop, calls=%fused_computation.127 | loop fusion | bytes 9437188 | tf_op jit(solution)/shard_map/dynamic_slice | solution.py:78
  5.5 0.5 collective-permute-start.2
  6.0 7.4 %fusion.2 = f32[9216,256]{1,0:T(8,128)} fusion(bf16[256,256]{1,0:T(8,128)(2,1)S(1)} %copy-done.6, bf16[256,18432]{1,0:T(8,128)(2,1)} %param.6, s32[]{:T(128)S(6)} %select_n.129), kind=kOutput, calls=%fused_computation.4 | convolution fusion | flops 1207959552 | bytes 14286852 | tf_op jit(solution)/shard_map/dot_general | solution.py:81
  13.6 0.3 collective-permute-done.1
  13.9 6.6 %convolution_add_fusion = f32[9216,256]{1,0:T(8,128)S(1)} fusion(f32[9216,256]{1,0:T(8,128)} %fusion.2, bf16[256,9216]{1,0:T(8,128)(2,1)} %collective-permute-done.1, bf16[256,256]{1,0:T(8,128)(2,1)S(1)} %collective-permute-done.2), kind=kOutput, calls=%fused_computation | convolution fusion | flops 1210318848 | bytes 23724032 | tf_op jit(solution)/shard_map/dot_general | solution.py:82
  20.5 0.9 fusion.55
  21.4 1.2 dynamic-slice_bitcast_fusion.5
  22.7 3.0 %collective-permute-start.3 = (bf16[4,8,72,128]{3,2,1,0:T(8,128)(2,1)S(1)}, bf16[4,8,72,128]{3,2,1,0:T(8,128)(2,1)}, u32[]{:S(2)}, u32[]{:S(2)}) collective-permute-start(bf16[4,8,72,128]{3,2,1,0:T(8,128)(2,1)S(1)} %get-tuple-element.37), channel_id=1, source_target_pairs={{0,32},{128,160},{32,0},{160,128},{1,33},{129,161},{33,1},{161,129... | collective-permute-start | bytes 1769480 | tf_op jit(solution)/shard_map/ppermute | solution.py:89
  25.8 0.7 dynamic-slice_bitcast_fusion.12
  26.4 0.6 collective-permute-start.4
  27.0 2.6 %collective-permute-start.5 = (bf16[4,8,72,128]{3,2,1,0:T(8,128)(2,1)}, bf16[4,8,72,128]{3,2,1,0:T(8,128)(2,1)}, u32[]{:S(2)}, u32[]{:S(2)}) collective-permute-start(bf16[4,8,72,128]{3,2,1,0:T(8,128)(2,1)} %get-tuple-element.38), channel_id=1, source_target_pairs={{0,160},{128,0},{32,128},{160,32},{1,161},{129,1},{33,129},{161,33... | collective-permute-start | bytes 1769480 | tf_op jit(solution)/shard_map/ppermute | solution.py:89
  29.7 1.3 dynamic-slice_bitcast_fusion.2
  31.2 1.8 collective-permute-start.11
  33.0 7.5 %collective-permute-done.3 = bf16[4,8,72,128]{3,2,1,0:T(8,128)(2,1)} collective-permute-done((bf16[4,8,72,128]{3,2,1,0:T(8,128)(2,1)S(1)}, bf16[4,8,72,128]{3,2,1,0:T(8,128)(2,1)}, u32[]{:S(2)}, u32[]{:S(2)}) %collective-permute-start.3) | collective-permute-done | bytes 589856 | tf_op jit(solution)/shard_map/ppermute | solution.py:89
  40.5 1.2 collective-permute-start.9
  41.7 1.3 fusion.54
  43.0 9.3 %collective-permute-done.4 = bf16[4,8,72,128]{3,2,1,0:T(8,128)(2,1)} collective-permute-done((bf16[4,8,72,128]{3,2,1,0:T(8,128)(2,1)}, bf16[4,8,72,128]{3,2,1,0:T(8,128)(2,1)}, u32[]{:S(2)}, u32[]{:S(2)}) %collective-permute-start.4) | collective-permute-done | bytes 589856 | tf_op jit(solution)/shard_map/ppermute | solution.py:89
  52.3 3.0 %collective-permute-start = (bf16[72,896]{1,0:T(8,128)(2,1)}, bf16[72,896]{1,0:T(8,128)(2,1)}, u32[]{:S(2)}, u32[]{:S(2)}) collective-permute-start(bf16[72,896]{1,0:T(8,128)(2,1)} %dynamic-slice_bitcast_fusion.12), channel_id=1, source_target_pairs={{0,32},{32,0},{1,33},{33,1},{2,34},{34,2},{3,35},{35,3},{4,36},{36... | collective-permute-start | bytes 387080 | tf_op jit(solution)/shard_map/ppermute | solution.py:66
  55.3 1.7 fusion.50
  57.1 1.3 collective-permute-start.6
  58.4 2.2 %collective-permute-start.7 = (bf16[8,72,128]{2,1,0:T(8,128)(2,1)S(1)}, bf16[8,72,128]{2,1,0:T(8,128)(2,1)S(1)}, u32[]{:S(2)}, u32[]{:S(2)}) collective-permute-start(bf16[8,72,128]{2,1,0:T(8,128)(2,1)S(1)} %get-tuple-element.45), channel_id=1, source_target_pairs={{0,8},{8,16},{16,24},{24,0},{1,9},{9,17},{17,25},{25,1},{2,10},{10... | collective-permute-start | bytes 442376 | tf_op jit(solution)/shard_map/ppermute | solution.py:89
  60.6 1.7 fusion.52
  62.4 0.5 collective-permute-start.12
  62.9 2.5 %collective-permute-done.6 = bf16[8,72,128]{2,1,0:T(8,128)(2,1)S(1)} collective-permute-done((bf16[8,72,128]{2,1,0:T(8,128)(2,1)S(1)}, bf16[8,72,128]{2,1,0:T(8,128)(2,1)S(1)}, u32[]{:S(2)}, u32[]{:S(2)}) %collective-permute-start.6) | collective-permute-done | bytes 147488 | tf_op jit(solution)/shard_map/ppermute | solution.py:89
  65.5 3.2 %collective-permute-start.14 = (bf16[8,72,128]{2,1,0:T(8,128)(2,1)S(1)}, bf16[8,72,128]{2,1,0:T(8,128)(2,1)S(1)}, u32[]{:S(2)}, u32[]{:S(2)}) collective-permute-start(bf16[8,72,128]{2,1,0:T(8,128)(2,1)S(1)} %get-tuple-element.47), channel_id=1, source_target_pairs={{0,160},{128,0},{32,128},{160,32},{1,161},{129,1},{33,129},{161,33... | collective-permute-start | bytes 442376 | tf_op jit(solution)/shard_map/ppermute | solution.py:89
  68.8 1.8 collective-permute-done.12
  70.5 1.6 collective-permute-done.13
  72.2 0.9 pad_maximum_fusion.7
  73.0 8.5 %all-to-all-start = ((f32[8,2,72,128]{3,2,1,0:T(8,128)}), f32[8,2,72,128]{3,2,1,0:T(8,128)S(1)}, u32[]{:S(2)}, u32[]{:S(2)}) async-start(f32[8,2,72,128]{3,2,1,0:T(8,128)} %pad_maximum_fusion.7), calls=%async_computation | async-start | bytes 1179648 | tf_op jit(solution)/shard_map/all_to_all | solution.py:96
  81.8 17.0 %all-to-all-done = f32[8,2,72,128]{3,2,1,0:T(8,128)S(1)} async-done(((f32[8,2,72,128]{3,2,1,0:T(8,128)}), f32[8,2,72,128]{3,2,1,0:T(8,128)S(1)}, u32[]{:S(2)}, u32[]{:S(2)}) %all-to-all-start) | async-done | bytes 589856 | tf_op jit(solution)/shard_map/all_to_all | solution.py:96
  98.9 0.4 fusion.34
  99.4 0.5 abs_reduce_fusion
  100.1 1.8 collective-permute-start.28
  102.0 1.0 collective-permute-start.30
  102.9 0.8 broadcast_in_dim.2
  103.7 3.4 %all-to-all-start.1 = ((bf16[8,2,72,128]{3,2,1,0:T(8,128)(2,1)}), bf16[8,2,72,128]{3,2,1,0:T(8,128)(2,1)S(1)}, u32[]{:S(2)}, u32[]{:S(2)}) async-start(bf16[8,2,72,128]{3,2,1,0:T(8,128)(2,1)} %broadcast_in_dim.2), calls=%async_computation.1 | async-start | bytes 589824 | tf_op jit(solution)/shard_map/all_to_all | solution.py:115
  107.2 1.3 collective-permute-done.29
  108.5 1.0 collective-permute-done.30
  109.7 0.9 copy-done.1
  110.6 7.3 %all-to-all-done.1 = bf16[8,2,72,128]{3,2,1,0:T(8,128)(2,1)S(1)} async-done(((bf16[8,2,72,128]{3,2,1,0:T(8,128)(2,1)}), bf16[8,2,72,128]{3,2,1,0:T(8,128)(2,1)S(1)}, u32[]{:S(2)}, u32[]{:S(2)}) %all-to-all-start.1) | async-done | bytes 294944 | tf_op jit(solution)/shard_map/all_to_all | solution.py:115
  117.9 2.3 %collective-permute-start.21 = (bf16[8,72,128]{2,1,0:T(8,128)(2,1)S(1)}, bf16[8,72,128]{2,1,0:T(8,128)(2,1)S(1)}, u32[]{:S(2)}, u32[]{:S(2)}) collective-permute-start(bf16[8,72,128]{2,1,0:T(8,128)(2,1)S(1)} %get-tuple-element.54), channel_id=1, source_target_pairs={{0,160},{128,0},{32,128},{160,32},{1,161},{129,1},{33,129},{161,33... | collective-permute-start | bytes 442376 | tf_op jit(solution)/shard_map/ppermute | solution.py:105
  120.2 2.3 %collective-permute-start.22 = (bf16[8,72,128]{2,1,0:T(8,128)(2,1)S(1)}, bf16[8,72,128]{2,1,0:T(8,128)(2,1)S(1)}, u32[]{:S(2)}, u32[]{:S(2)}) collective-permute-start(bf16[8,72,128]{2,1,0:T(8,128)(2,1)S(1)} %get-tuple-element.54), channel_id=1, source_target_pairs={{0,32},{128,160},{32,0},{160,128},{1,33},{129,161},{33,1},{161,129... | collective-permute-start | bytes 442376 | tf_op jit(solution)/shard_map/ppermute | solution.py:105
  122.9 0.8 collective-permute-done.21
  123.6 3.2 %collective-permute-done.22 = bf16[8,72,128]{2,1,0:T(8,128)(2,1)S(1)} collective-permute-done((bf16[8,72,128]{2,1,0:T(8,128)(2,1)S(1)}, bf16[8,72,128]{2,1,0:T(8,128)(2,1)S(1)}, u32[]{:S(2)}, u32[]{:S(2)}) %collective-permute-start.22) | collective-permute-done | bytes 147488 | tf_op jit(solution)/shard_map/ppermute | solution.py:105
  126.9 2.0 %collective-permute-done.23 = bf16[8,72,128]{2,1,0:T(8,128)(2,1)S(1)} collective-permute-done((bf16[8,72,128]{2,1,0:T(8,128)(2,1)S(1)}, bf16[8,72,128]{2,1,0:T(8,128)(2,1)S(1)}, u32[]{:S(2)}, u32[]{:S(2)}) %collective-permute-start.23) | collective-permute-done | bytes 147488 | tf_op jit(solution)/shard_map/ppermute | solution.py:105
  129.0 0.9 collective-permute-start.15
  129.9 4.2 %collective-permute-start.16 = (bf16[8,72,128]{2,1,0:T(8,128)(2,1)S(1)}, bf16[8,72,128]{2,1,0:T(8,128)(2,1)S(1)}, u32[]{:S(2)}, u32[]{:S(2)}) collective-permute-start(bf16[8,72,128]{2,1,0:T(8,128)(2,1)S(1)} %get-tuple-element.52), channel_id=1, source_target_pairs={{0,16},{8,24},{16,0},{24,8},{1,17},{9,25},{17,1},{25,9},{2,18},{10... | collective-permute-start | bytes 442376 | tf_op jit(solution)/shard_map/ppermute | solution.py:105
  134.3 2.1 %collective-permute-start.24 = (bf16[8,4,72,128]{3,2,1,0:T(8,128)(2,1)S(1)}, bf16[8,4,72,128]{3,2,1,0:T(8,128)(2,1)S(1)}, u32[]{:S(2)}, u32[]{:S(2)}) collective-permute-start(bf16[8,4,72,128]{3,2,1,0:T(8,128)(2,1)S(1)} %get-tuple-element.28), channel_id=1, source_target_pairs={{0,24},{8,0},{16,8},{24,16},{1,25},{9,1},{17,9},{25,17},{2,26},{10... | collective-permute-start | bytes 1769480 | tf_op jit(solution)/shard_map/ppermute | solution.py:105
  136.4 0.9 collective-permute-done.15
  137.3 1.0 collective-permute-start.25
  138.4 3.6 %collective-permute-done.16 = bf16[8,72,128]{2,1,0:T(8,128)(2,1)S(1)} collective-permute-done((bf16[8,72,128]{2,1,0:T(8,128)(2,1)S(1)}, bf16[8,72,128]{2,1,0:T(8,128)(2,1)S(1)}, u32[]{:S(2)}, u32[]{:S(2)}) %collective-permute-start.16) | collective-permute-done | bytes 147488 | tf_op jit(solution)/shard_map/ppermute | solution.py:105
  142.0 4.2 %collective-permute-done.17 = bf16[8,72,128]{2,1,0:T(8,128)(2,1)S(1)} collective-permute-done((bf16[8,72,128]{2,1,0:T(8,128)(2,1)S(1)}, bf16[8,72,128]{2,1,0:T(8,128)(2,1)S(1)}, u32[]{:S(2)}, u32[]{:S(2)}) %collective-permute-start.17) | collective-permute-done | bytes 147488 | tf_op jit(solution)/shard_map/ppermute | solution.py:105
  146.5 0.9 collective-permute-start.18
  147.4 7.2 %collective-permute-done.24 = bf16[8,4,72,128]{3,2,1,0:T(8,128)(2,1)S(1)} collective-permute-done((bf16[8,4,72,128]{3,2,1,0:T(8,128)(2,1)S(1)}, bf16[8,4,72,128]{3,2,1,0:T(8,128)(2,1)S(1)}, u32[]{:S(2)}, u32[]{:S(2)}) %collective-permute-start.24) | collective-permute-done | bytes 589856 | tf_op jit(solution)/shard_map/ppermute | solution.py:105
  154.6 1.3 collective-permute-start.19
  156.0 5.6 %collective-permute-done.25 = bf16[8,4,72,128]{3,2,1,0:T(8,128)(2,1)S(1)} collective-permute-done((bf16[8,4,72,128]{3,2,1,0:T(8,128)(2,1)S(1)}, bf16[8,4,72,128]{3,2,1,0:T(8,128)(2,1)S(1)}, u32[]{:S(2)}, u32[]{:S(2)}) %collective-permute-start.25) | collective-permute-done | bytes 589856 | tf_op jit(solution)/shard_map/ppermute | solution.py:105
  161.6 0.4 collective-permute-start.20
  162.9 9.3 %collective-permute-done.19 = bf16[4,8,72,128]{3,2,1,0:T(8,128)(2,1)S(1)} collective-permute-done((bf16[4,8,72,128]{3,2,1,0:T(8,128)(2,1)S(1)}, bf16[4,8,72,128]{3,2,1,0:T(8,128)(2,1)S(1)}, u32[]{:S(2)}, u32[]{:S(2)}) %collective-permute-start.19) | collective-permute-done | bytes 589856 | tf_op jit(solution)/shard_map/ppermute | solution.py:105
  172.3 6.4 %collective-permute-done.20 = bf16[4,8,72,128]{3,2,1,0:T(8,128)(2,1)S(1)} collective-permute-done((bf16[4,8,72,128]{3,2,1,0:T(8,128)(2,1)S(1)}, bf16[4,8,72,128]{3,2,1,0:T(8,128)(2,1)S(1)}, u32[]{:S(2)}, u32[]{:S(2)}) %collective-permute-start.20) | collective-permute-done | bytes 589856 | tf_op jit(solution)/shard_map/ppermute | solution.py:105
  179.4 5.4 %fusion.4 = f32[256,256]{1,0:T(8,128)} fusion(bf16[256,9216]{1,0:T(8,128)(2,1)} %collective-permute-done.1, bf16[9216,128]{1,0:T(8,128)(2,1)S(1)} %bitcast.263, bf16[9216,128]{1,0:T(8,128)(2,1)S(1)} %bitcast.265), kind=kOutput, calls=%fused_computation.6 | convolution fusion | flops 1217396736 | bytes 9699328 | tf_op jit(solution)/shard_map/dot_general | solution.py:121
  184.9 0.7 copy.73
  185.6 0.8 fusion.56
  186.3 0.3 collective-permute-done.27
  186.7 5.1 %fusion.14 = bf16[256,256]{1,0:T(8,128)(2,1)} fusion(f32[256,256]{1,0:T(8,128)} %collective-permute-done.27, bf16[9216,128]{1,0:T(8,128)(2,1)S(1)} %bitcast.264, bf16[9216,128]{1,0:T(8,128)(2,1)} %bitcast.266, bf16[256,18432]{1,0:T(8,128)(2,1)} %param.6, s32[]{:T(128)S(6)} %select_n.129), kind=kOutput, calls=%fused_computation.18 | convolution fusion | flops 1217527808 | bytes 9830404 | tf_op jit(solution)/shard_map/dot_general | solution.py:122
  (106 shorter events, 4.2 us)
Async XLA Ops:
  0.6 4.8 %copy-start.6 = (bf16[256,256]{1,0:T(8,128)(2,1)S(1)}, bf16[256,256]{1,0:T(8,128)(2,1)}, u32[]{:S(2)}) copy-start(bf16[256,256]{1,0:T(8,128)(2,1)} %param.7) | copy-start | bytes 393220
  5.5 8.4 %collective-permute-start.1 = (bf16[256,9216]{1,0:T(8,128)(2,1)}, bf16[256,9216]{1,0:T(8,128)(2,1)}, u32[]{:S(2)}, u32[]{:S(2)}) collective-permute-start(bf16[256,9216]{1,0:T(8,128)(2,1)} %constant_dynamic-slice_fusion.5), channel_id=1, source_target_pairs={{0,64},{64,0},{1,65},{65,1},{2,66},{66,2},{3,67},{67,3},{4,68},{68... | collective-permute-start | bytes 14155784 | tf_op jit(solution)/shard_map/ppermute | solution.py:78
  5.5 8.1 %collective-permute-start.2 = (bf16[256,256]{1,0:T(8,128)(2,1)S(1)}, bf16[256,256]{1,0:T(8,128)(2,1)S(1)}, u32[]{:S(2)}, u32[]{:S(2)}) collective-permute-start(bf16[256,256]{1,0:T(8,128)(2,1)S(1)} %copy-done.6), channel_id=1, source_target_pairs={{0,64},{64,0},{1,65},{65,1},{2,66},{66,2},{3,67},{67,3},{4,68},{68... | collective-permute-start | bytes 393224 | tf_op jit(solution)/shard_map/ppermute | solution.py:79
  6.0 7.5 %copy-start.7 = (bf16[288,2]{0,1:T(2,128)(2,1)S(1)}, bf16[288,2]{0,1:T(2,128)(2,1)}, u32[]{:S(2)}) copy-start(bf16[288,2]{0,1:T(2,128)(2,1)} %param.10) | copy-start | bytes 3460
  20.5 5.2 %copy-start.3 = (bf16[288,256]{1,0:T(8,128)(2,1)S(1)}, bf16[288,256]{1,0:T(8,128)(2,1)}, u32[]{:S(2)}) copy-start(bf16[288,256]{1,0:T(8,128)(2,1)} %param.11) | copy-start | bytes 442372
  20.5 5.2 %copy-start.4 = (bf16[288,256]{1,0:T(8,128)(2,1)S(1)}, bf16[288,256]{1,0:T(8,128)(2,1)}, u32[]{:S(2)}) copy-start(bf16[288,256]{1,0:T(8,128)(2,1)} %param.9) | copy-start | bytes 442372
  20.5 5.2 %copy-start.5 = (bf16[288,256]{1,0:T(8,128)(2,1)S(1)}, bf16[288,256]{1,0:T(8,128)(2,1)}, u32[]{:S(2)}) copy-start(bf16[288,256]{1,0:T(8,128)(2,1)} %param.8) | copy-start | bytes 442372
  22.7 17.8 %collective-permute-start.3 = (bf16[4,8,72,128]{3,2,1,0:T(8,128)(2,1)S(1)}, bf16[4,8,72,128]{3,2,1,0:T(8,128)(2,1)}, u32[]{:S(2)}, u32[]{:S(2)}) collective-permute-start(bf16[4,8,72,128]{3,2,1,0:T(8,128)(2,1)S(1)} %get-tuple-element.37), channel_id=1, source_target_pairs={{0,32},{128,160},{32,0},{160,128},{1,33},{129,161},{33,1},{161,129... | collective-permute-start | bytes 1769480 | tf_op jit(solution)/shard_map/ppermute | solution.py:89
  26.4 25.8 %collective-permute-start.4 = (bf16[4,8,72,128]{3,2,1,0:T(8,128)(2,1)}, bf16[4,8,72,128]{3,2,1,0:T(8,128)(2,1)}, u32[]{:S(2)}, u32[]{:S(2)}) collective-permute-start(bf16[4,8,72,128]{3,2,1,0:T(8,128)(2,1)} %get-tuple-element.39), channel_id=1, source_target_pairs={{0,128},{128,32},{32,160},{160,0},{1,129},{129,33},{33,161},{161,1... | collective-permute-start | bytes 1769480 | tf_op jit(solution)/shard_map/ppermute | solution.py:89
  27.0 28.3 %collective-permute-start.5 = (bf16[4,8,72,128]{3,2,1,0:T(8,128)(2,1)}, bf16[4,8,72,128]{3,2,1,0:T(8,128)(2,1)}, u32[]{:S(2)}, u32[]{:S(2)}) collective-permute-start(bf16[4,8,72,128]{3,2,1,0:T(8,128)(2,1)} %get-tuple-element.38), channel_id=1, source_target_pairs={{0,160},{128,0},{32,128},{160,32},{1,161},{129,1},{33,129},{161,33... | collective-permute-start | bytes 1769480 | tf_op jit(solution)/shard_map/ppermute | solution.py:89
  31.0 27.4 %collective-permute-start.10 = (bf16[8,4,72,128]{3,2,1,0:T(8,128)(2,1)}, bf16[8,4,72,128]{3,2,1,0:T(8,128)(2,1)}, u32[]{:S(2)}, u32[]{:S(2)}) collective-permute-start(bf16[8,4,72,128]{3,2,1,0:T(8,128)(2,1)} %get-tuple-element.42), channel_id=1, source_target_pairs={{0,8},{8,16},{16,24},{24,0},{1,9},{9,17},{17,25},{25,1},{2,10},{10... | collective-permute-start | bytes 1769480 | tf_op jit(solution)/shard_map/ppermute | solution.py:89
  31.2 29.4 %collective-permute-start.11 = (bf16[8,4,72,128]{3,2,1,0:T(8,128)(2,1)}, bf16[8,4,72,128]{3,2,1,0:T(8,128)(2,1)}, u32[]{:S(2)}, u32[]{:S(2)}) collective-permute-start(bf16[8,4,72,128]{3,2,1,0:T(8,128)(2,1)} %get-tuple-element.41), channel_id=1, source_target_pairs={{0,24},{8,0},{16,8},{24,16},{1,25},{9,1},{17,9},{25,17},{2,26},{10... | collective-permute-start | bytes 1769480 | tf_op jit(solution)/shard_map/ppermute | solution.py:89
  40.5 20.1 %collective-permute-start.9 = (bf16[8,4,72,128]{3,2,1,0:T(8,128)(2,1)}, bf16[8,4,72,128]{3,2,1,0:T(8,128)(2,1)}, u32[]{:S(2)}, u32[]{:S(2)}) collective-permute-start(bf16[8,4,72,128]{3,2,1,0:T(8,128)(2,1)} %get-tuple-element.40), channel_id=1, source_target_pairs={{0,16},{8,24},{16,0},{24,8},{1,17},{9,25},{17,1},{25,9},{2,18},{10... | collective-permute-start | bytes 1769480 | tf_op jit(solution)/shard_map/ppermute | solution.py:89
  52.3 29.2 %collective-permute-start = (bf16[72,896]{1,0:T(8,128)(2,1)}, bf16[72,896]{1,0:T(8,128)(2,1)}, u32[]{:S(2)}, u32[]{:S(2)}) collective-permute-start(bf16[72,896]{1,0:T(8,128)(2,1)} %dynamic-slice_bitcast_fusion.12), channel_id=1, source_target_pairs={{0,32},{32,0},{1,33},{33,1},{2,34},{34,2},{3,35},{35,3},{4,36},{36... | collective-permute-start | bytes 387080 | tf_op jit(solution)/shard_map/ppermute | solution.py:66
  57.1 8.3 %collective-permute-start.6 = (bf16[8,72,128]{2,1,0:T(8,128)(2,1)S(1)}, bf16[8,72,128]{2,1,0:T(8,128)(2,1)S(1)}, u32[]{:S(2)}, u32[]{:S(2)}) collective-permute-start(bf16[8,72,128]{2,1,0:T(8,128)(2,1)S(1)} %get-tuple-element.43), channel_id=1, source_target_pairs={{0,16},{8,24},{16,0},{24,8},{1,17},{9,25},{17,1},{25,9},{2,18},{10... | collective-permute-start | bytes 442376 | tf_op jit(solution)/shard_map/ppermute | solution.py:89
  58.4 7.0 %collective-permute-start.7 = (bf16[8,72,128]{2,1,0:T(8,128)(2,1)S(1)}, bf16[8,72,128]{2,1,0:T(8,128)(2,1)S(1)}, u32[]{:S(2)}, u32[]{:S(2)}) collective-permute-start(bf16[8,72,128]{2,1,0:T(8,128)(2,1)S(1)} %get-tuple-element.45), channel_id=1, source_target_pairs={{0,8},{8,16},{16,24},{24,0},{1,9},{9,17},{17,25},{25,1},{2,10},{10... | collective-permute-start | bytes 442376 | tf_op jit(solution)/shard_map/ppermute | solution.py:89
  60.6 8.1 %collective-permute-start.8 = (bf16[8,72,128]{2,1,0:T(8,128)(2,1)S(1)}, bf16[8,72,128]{2,1,0:T(8,128)(2,1)S(1)}, u32[]{:S(2)}, u32[]{:S(2)}) collective-permute-start(bf16[8,72,128]{2,1,0:T(8,128)(2,1)S(1)} %get-tuple-element.44), channel_id=1, source_target_pairs={{0,24},{8,0},{16,8},{24,16},{1,25},{9,1},{17,9},{25,17},{2,26},{10... | collective-permute-start | bytes 442376 | tf_op jit(solution)/shard_map/ppermute | solution.py:89
  62.4 8.1 %collective-permute-start.12 = (bf16[8,72,128]{2,1,0:T(8,128)(2,1)S(1)}, bf16[8,72,128]{2,1,0:T(8,128)(2,1)S(1)}, u32[]{:S(2)}, u32[]{:S(2)}) collective-permute-start(bf16[8,72,128]{2,1,0:T(8,128)(2,1)S(1)} %get-tuple-element.46), channel_id=1, source_target_pairs={{0,32},{128,160},{32,0},{160,128},{1,33},{129,161},{33,1},{161,129... | collective-permute-start | bytes 442376 | tf_op jit(solution)/shard_map/ppermute | solution.py:89
  65.4 6.6 %collective-permute-start.13 = (bf16[8,72,128]{2,1,0:T(8,128)(2,1)S(1)}, bf16[8,72,128]{2,1,0:T(8,128)(2,1)S(1)}, u32[]{:S(2)}, u32[]{:S(2)}) collective-permute-start(bf16[8,72,128]{2,1,0:T(8,128)(2,1)S(1)} %get-tuple-element.48), channel_id=1, source_target_pairs={{0,128},{128,32},{32,160},{160,0},{1,129},{129,33},{33,161},{161,1... | collective-permute-start | bytes 442376 | tf_op jit(solution)/shard_map/ppermute | solution.py:89
  65.5 6.6 %collective-permute-start.14 = (bf16[8,72,128]{2,1,0:T(8,128)(2,1)S(1)}, bf16[8,72,128]{2,1,0:T(8,128)(2,1)S(1)}, u32[]{:S(2)}, u32[]{:S(2)}) collective-permute-start(bf16[8,72,128]{2,1,0:T(8,128)(2,1)S(1)} %get-tuple-element.47), channel_id=1, source_target_pairs={{0,160},{128,0},{32,128},{160,32},{1,161},{129,1},{33,129},{161,33... | collective-permute-start | bytes 442376 | tf_op jit(solution)/shard_map/ppermute | solution.py:89
  73.0 25.8 %all-to-all-start = ((f32[8,2,72,128]{3,2,1,0:T(8,128)}), f32[8,2,72,128]{3,2,1,0:T(8,128)S(1)}, u32[]{:S(2)}, u32[]{:S(2)}) async-start(f32[8,2,72,128]{3,2,1,0:T(8,128)} %pad_maximum_fusion.7), calls=%async_computation | async-start | bytes 1179648 | tf_op jit(solution)/shard_map/all_to_all | solution.py:96
  100.1 7.0 %collective-permute-start.28 = (bf16[72,896]{1,0:T(8,128)(2,1)S(1)}, bf16[72,896]{1,0:T(8,128)(2,1)S(1)}, u32[]{:S(2)}, u32[]{:S(2)}) collective-permute-start(bf16[72,896]{1,0:T(8,128)(2,1)S(1)} %fusion.25), channel_id=1, source_target_pairs={{0,160},{128,0},{32,128},{160,32},{1,161},{129,1},{33,129},{161,33... | collective-permute-start | bytes 387080 | tf_op jit(solution)/shard_map/ppermute | solution.py:105
  102.0 6.6 %collective-permute-start.29 = (bf16[72,896]{1,0:T(8,128)(2,1)S(1)}, bf16[72,896]{1,0:T(8,128)(2,1)S(1)}, u32[]{:S(2)}, u32[]{:S(2)}) collective-permute-start(bf16[72,896]{1,0:T(8,128)(2,1)S(1)} %fusion.25), channel_id=1, source_target_pairs={{0,32},{128,160},{32,0},{160,128},{1,33},{129,161},{33,1},{161,129... | collective-permute-start | bytes 387080 | tf_op jit(solution)/shard_map/ppermute | solution.py:105
  102.0 7.5 %collective-permute-start.30 = (bf16[72,896]{1,0:T(8,128)(2,1)S(1)}, bf16[72,896]{1,0:T(8,128)(2,1)S(1)}, u32[]{:S(2)}, u32[]{:S(2)}) collective-permute-start(bf16[72,896]{1,0:T(8,128)(2,1)S(1)} %fusion.25), channel_id=1, source_target_pairs={{0,128},{128,32},{32,160},{160,0},{1,129},{129,33},{33,161},{161,1... | collective-permute-start | bytes 387080 | tf_op jit(solution)/shard_map/ppermute | solution.py:105
  103.7 14.2 %all-to-all-start.1 = ((bf16[8,2,72,128]{3,2,1,0:T(8,128)(2,1)}), bf16[8,2,72,128]{3,2,1,0:T(8,128)(2,1)S(1)}, u32[]{:S(2)}, u32[]{:S(2)}) async-start(bf16[8,2,72,128]{3,2,1,0:T(8,128)(2,1)} %broadcast_in_dim.2), calls=%async_computation.1 | async-start | bytes 589824 | tf_op jit(solution)/shard_map/all_to_all | solution.py:115
  109.6 1.0 copy-start.1
  110.6 74.2 %collective-permute-start.31 = (bf16[4,72,896]{2,1,0:T(8,128)(2,1)S(1)}, bf16[4,72,896]{2,1,0:T(8,128)(2,1)S(1)}, u32[]{:S(2)}, u32[]{:S(2)}) collective-permute-start(bf16[4,72,896]{2,1,0:T(8,128)(2,1)S(1)} %constant_dynamic-slice_fusion), channel_id=1, source_target_pairs={{0,64},{64,0},{1,65},{65,1},{2,66},{66,2},{3,67},{67,3},{4,68},{68... | collective-permute-start | bytes 1548296 | tf_op jit(solution)/shard_map/ppermute | solution.py:113
  117.9 5.7 %collective-permute-start.21 = (bf16[8,72,128]{2,1,0:T(8,128)(2,1)S(1)}, bf16[8,72,128]{2,1,0:T(8,128)(2,1)S(1)}, u32[]{:S(2)}, u32[]{:S(2)}) collective-permute-start(bf16[8,72,128]{2,1,0:T(8,128)(2,1)S(1)} %get-tuple-element.54), channel_id=1, source_target_pairs={{0,160},{128,0},{32,128},{160,32},{1,161},{129,1},{33,129},{161,33... | collective-permute-start | bytes 442376 | tf_op jit(solution)/shard_map/ppermute | solution.py:105
  120.2 6.6 %collective-permute-start.22 = (bf16[8,72,128]{2,1,0:T(8,128)(2,1)S(1)}, bf16[8,72,128]{2,1,0:T(8,128)(2,1)S(1)}, u32[]{:S(2)}, u32[]{:S(2)}) collective-permute-start(bf16[8,72,128]{2,1,0:T(8,128)(2,1)S(1)} %get-tuple-element.54), channel_id=1, source_target_pairs={{0,32},{128,160},{32,0},{160,128},{1,33},{129,161},{33,1},{161,129... | collective-permute-start | bytes 442376 | tf_op jit(solution)/shard_map/ppermute | solution.py:105
  122.6 6.4 %collective-permute-start.23 = (bf16[8,72,128]{2,1,0:T(8,128)(2,1)S(1)}, bf16[8,72,128]{2,1,0:T(8,128)(2,1)S(1)}, u32[]{:S(2)}, u32[]{:S(2)}) collective-permute-start(bf16[8,72,128]{2,1,0:T(8,128)(2,1)S(1)} %get-tuple-element.54), channel_id=1, source_target_pairs={{0,128},{128,32},{32,160},{160,0},{1,129},{129,33},{33,161},{161,1... | collective-permute-start | bytes 442376 | tf_op jit(solution)/shard_map/ppermute | solution.py:105
  129.0 8.4 %collective-permute-start.15 = (bf16[8,72,128]{2,1,0:T(8,128)(2,1)S(1)}, bf16[8,72,128]{2,1,0:T(8,128)(2,1)S(1)}, u32[]{:S(2)}, u32[]{:S(2)}) collective-permute-start(bf16[8,72,128]{2,1,0:T(8,128)(2,1)S(1)} %get-tuple-element.52), channel_id=1, source_target_pairs={{0,24},{8,0},{16,8},{24,16},{1,25},{9,1},{17,9},{25,17},{2,26},{10... | collective-permute-start | bytes 442376 | tf_op jit(solution)/shard_map/ppermute | solution.py:105
  129.9 12.1 %collective-permute-start.16 = (bf16[8,72,128]{2,1,0:T(8,128)(2,1)S(1)}, bf16[8,72,128]{2,1,0:T(8,128)(2,1)S(1)}, u32[]{:S(2)}, u32[]{:S(2)}) collective-permute-start(bf16[8,72,128]{2,1,0:T(8,128)(2,1)S(1)} %get-tuple-element.52), channel_id=1, source_target_pairs={{0,16},{8,24},{16,0},{24,8},{1,17},{9,25},{17,1},{25,9},{2,18},{10... | collective-permute-start | bytes 442376 | tf_op jit(solution)/shard_map/ppermute | solution.py:105
  134.1 12.1 %collective-permute-start.17 = (bf16[8,72,128]{2,1,0:T(8,128)(2,1)S(1)}, bf16[8,72,128]{2,1,0:T(8,128)(2,1)S(1)}, u32[]{:S(2)}, u32[]{:S(2)}) collective-permute-start(bf16[8,72,128]{2,1,0:T(8,128)(2,1)S(1)} %get-tuple-element.52), channel_id=1, source_target_pairs={{0,8},{8,16},{16,24},{24,0},{1,9},{9,17},{17,25},{25,1},{2,10},{10... | collective-permute-start | bytes 442376 | tf_op jit(solution)/shard_map/ppermute | solution.py:105
  134.3 20.3 %collective-permute-start.24 = (bf16[8,4,72,128]{3,2,1,0:T(8,128)(2,1)S(1)}, bf16[8,4,72,128]{3,2,1,0:T(8,128)(2,1)S(1)}, u32[]{:S(2)}, u32[]{:S(2)}) collective-permute-start(bf16[8,4,72,128]{3,2,1,0:T(8,128)(2,1)S(1)} %get-tuple-element.28), channel_id=1, source_target_pairs={{0,24},{8,0},{16,8},{24,16},{1,25},{9,1},{17,9},{25,17},{2,26},{10... | collective-permute-start | bytes 1769480 | tf_op jit(solution)/shard_map/ppermute | solution.py:105
  137.3 24.2 %collective-permute-start.25 = (bf16[8,4,72,128]{3,2,1,0:T(8,128)(2,1)S(1)}, bf16[8,4,72,128]{3,2,1,0:T(8,128)(2,1)S(1)}, u32[]{:S(2)}, u32[]{:S(2)}) collective-permute-start(bf16[8,4,72,128]{3,2,1,0:T(8,128)(2,1)S(1)} %get-tuple-element.28), channel_id=1, source_target_pairs={{0,16},{8,24},{16,0},{24,8},{1,17},{9,25},{17,1},{25,9},{2,18},{10... | collective-permute-start | bytes 1769480 | tf_op jit(solution)/shard_map/ppermute | solution.py:105
  142.0 20.1 %collective-permute-start.26 = (bf16[8,4,72,128]{3,2,1,0:T(8,128)(2,1)S(1)}, bf16[8,4,72,128]{3,2,1,0:T(8,128)(2,1)S(1)}, u32[]{:S(2)}, u32[]{:S(2)}) collective-permute-start(bf16[8,4,72,128]{3,2,1,0:T(8,128)(2,1)S(1)} %get-tuple-element.28), channel_id=1, source_target_pairs={{0,8},{8,16},{16,24},{24,0},{1,9},{9,17},{17,25},{25,1},{2,10},{10... | collective-permute-start | bytes 1769480 | tf_op jit(solution)/shard_map/ppermute | solution.py:105
  146.5 16.3 %collective-permute-start.18 = (bf16[4,8,72,128]{3,2,1,0:T(8,128)(2,1)S(1)}, bf16[4,8,72,128]{3,2,1,0:T(8,128)(2,1)S(1)}, u32[]{:S(2)}, u32[]{:S(2)}) collective-permute-start(bf16[4,8,72,128]{3,2,1,0:T(8,128)(2,1)S(1)} %get-tuple-element.26), channel_id=1, source_target_pairs={{0,160},{128,0},{32,128},{160,32},{1,161},{129,1},{33,129},{161,33... | collective-permute-start | bytes 1769480 | tf_op jit(solution)/shard_map/ppermute | solution.py:105
  154.6 17.5 %collective-permute-start.19 = (bf16[4,8,72,128]{3,2,1,0:T(8,128)(2,1)S(1)}, bf16[4,8,72,128]{3,2,1,0:T(8,128)(2,1)S(1)}, u32[]{:S(2)}, u32[]{:S(2)}) collective-permute-start(bf16[4,8,72,128]{3,2,1,0:T(8,128)(2,1)S(1)} %get-tuple-element.26), channel_id=1, source_target_pairs={{0,32},{128,160},{32,0},{160,128},{1,33},{129,161},{33,1},{161,129... | collective-permute-start | bytes 1769480 | tf_op jit(solution)/shard_map/ppermute | solution.py:105
  161.6 17.1 %collective-permute-start.20 = (bf16[4,8,72,128]{3,2,1,0:T(8,128)(2,1)S(1)}, bf16[4,8,72,128]{3,2,1,0:T(8,128)(2,1)S(1)}, u32[]{:S(2)}, u32[]{:S(2)}) collective-permute-start(bf16[4,8,72,128]{3,2,1,0:T(8,128)(2,1)S(1)} %get-tuple-element.26), channel_id=1, source_target_pairs={{0,128},{128,32},{32,160},{160,0},{1,129},{129,33},{33,161},{161,1... | collective-permute-start | bytes 1769480 | tf_op jit(solution)/shard_map/ppermute | solution.py:105
  179.4 5.4 %copy-start = (bf16[4,8,4,72,128]{4,3,2,1,0:T(8,128)(2,1)}, bf16[4,8,4,72,128]{4,3,2,1,0:T(8,128)(2,1)S(1)}, u32[]{:S(2)}) copy-start(bf16[4,8,4,72,128]{4,3,2,1,0:T(8,128)(2,1)S(1)} %constant_dynamic-slice_fusion.3) | copy-start | bytes 7077892
  179.4 5.4 %copy-start.2 = (bf16[8,72,896]{2,1,0:T(8,128)(2,1)S(1)}, bf16[8,72,896]{2,1,0:T(8,128)(2,1)}, u32[]{:S(2)}) copy-start(bf16[8,72,896]{2,1,0:T(8,128)(2,1)} %copy-done.1) | copy-start | bytes 3096580
  184.8 1.9 collective-permute-start.27

commit v2 on v0

v2 whole, which is shorter than its diff:
```python
import itertools
import math

import jax
import jax.numpy as jnp
from jax import lax
from jax.experimental import pallas as pl
from jax.experimental.pallas import tpu as pltpu
from jax.sharding import Mesh, PartitionSpec as P

AXES = ("xl", "c", "xh", "y", "z")
PLANE = ("xl", "c", "xh", "y")
BF = jnp.bfloat16
F32 = jnp.float32
SWAP = [(0, 1), (1, 0)]


def flat(x, c, y):
    return ((x % 2 * 2 + c) * 2 + x // 2) * 4 + y


def line_pairs(first, step):
    pairs = []
    for x in range(4):
        for c in range(2):
            for y in range(4):
                along_x = (c == 0) == first
                to = flat((x + step) % 4, c, y) if along_x else flat(x, c, (y + step) % 4)
                pairs.append((flat(x, c, y), to))
    return pairs


def home_pairs():
    pairs = []
    for c in range(2):
        for p in range(4):
            owners = [(p, c, q) if c == 0 else (q, c, p) for q in range(4)]
            holders = [(2 * c + i, core, p) for i in range(2) for core in range(2)]

            def hops(order):
                apart = lambda a, b: min((a - b) % 4, (b - a) % 4)
                pair = zip(owners, order)
                each = [apart(o[0], h[0]) + apart(o[2], h[2]) + (0.1 if o[1] != h[1] else 0) for o, h in pair]
                return sum(each) + 0.01 * max(each)

            best = min(itertools.permutations(holders), key=hops)
            pairs += [(flat(*owners[q]), flat(*best[q]), q) for q in range(4)]
    return pairs


def hadamard_table():
    index = jnp.arange(128, dtype=jnp.int32)
    parity = jnp.zeros((128, 128), jnp.int32)
    for level in range(7):
        left = jnp.bitwise_and(jnp.right_shift(index, level), 1)
        parity = parity + left[:, None] * left[None, :]
    signs = 1 - 2 * jnp.bitwise_and(parity, 1)
    return signs.astype(F32) / math.sqrt(128.0)


def call(kernel, out_shape, scratch=(), in_specs=None):
    options = {} if in_specs is None else {"in_specs": in_specs}
    return pl.pallas_call(
        kernel,
        out_shape=out_shape,
        scratch_shapes=scratch,
        compiler_params=pltpu.CompilerParams(vmem_limit_bytes=16 << 20),
        cost_estimate=pl.CostEstimate(flops=1000, bytes_accessed=1000, transcendentals=0),
        **options,
    )


def shaped(shape, dtype):
    return jax.ShapeDtypeStruct(shape, dtype)


def after(value, *others):
    return lax.optimization_barrier((value, *others))[0]


SCALAR = pl.BlockSpec(memory_space=pltpu.SMEM)
VMEM = pl.BlockSpec(memory_space=pltpu.VMEM)


def gradient_rows(own, other, cot_own, cot_other, rows, dtype, added=()):
    contract = (((0,), (0,)), ((), ()))
    size = rows.stop - rows.start

    def kernel(own_ref, other_ref, cot_own_ref, cot_other_ref, *refs):
        for i in range(0, size, 384):
            part = pl.ds(rows.start + i, 384)
            term = lax.dot_general(own_ref[:, part], cot_own_ref[...], contract, preferred_element_type=F32)
            term += lax.dot_general(other_ref[:, part], cot_other_ref[...], contract, preferred_element_type=F32)
            for ref in refs[:-1]:
                term += ref[pl.ds(i, 384), :].astype(F32)
            refs[-1][pl.ds(i, 384), :] = term.astype(dtype)

    return call(kernel, shaped((size, 256), dtype))(own, other, cot_own, cot_other, *added)


def sum_and_split(total, upper, lower, q):
    def kernel(q_ref, total_ref, a_ref, b_ref, d_ref, e_ref, keep_ref, one_ref, two_ref, three_ref, value_ref):
        for z in range(8):
            rows, local = pl.ds(z * 288, 288), pl.ds(z % 4 * 288, 288)
            f_ref, g_ref = (a_ref, b_ref) if z < 4 else (d_ref, e_ref)
            value_ref[rows, :] = total_ref[rows, :] + f_ref[local, :].astype(F32) + g_ref[local, :].astype(F32)
            for step, ref in enumerate((keep_ref, one_ref, two_ref, three_ref)):
                at = pl.multiple_of(z * 288 + (q_ref[0] + step) % 4 * 72, 8)
                ref[z] = value_ref[pl.ds(at, 72), :].astype(ref.dtype)

    return call(
        kernel,
        [shaped((8, 72, 256), F32)] + [shaped((8, 72, 256), BF)] * 3,
        [pltpu.VMEM((2304, 256), F32)],
        [SCALAR] + [VMEM] * 5,
    )(q.reshape(1), total, *upper, *lower)


def sum_rows(keep, terms):
    def kernel(keep_ref, a_ref, b_ref, d_ref, out_ref):
        out_ref[...] = (
            keep_ref[...] + a_ref[...].astype(F32) + b_ref[...].astype(F32) + d_ref[...].astype(F32)
        ).astype(BF)

    return call(kernel, shaped((8, 72, 256), BF))(keep, *terms)


def adam(terms, state, table):
    def kernel(terms_ref, state_ref, table_ref, copies_ref, made_ref):
        grad = terms_ref[0].astype(F32)
        for z in range(1, 8):
            grad += terms_ref[z].astype(F32)
        grad *= 1.0 / 256.0
        table = table_ref[...]

        def rotate(block):
            return jnp.dot(block, table, precision=lax.Precision.HIGHEST, preferred_element_type=F32)

        second = 0.95 * state_ref[2].astype(F32) + 0.05 * grad * grad
        code = state_ref[1].astype(F32)
        weight = state_ref[0].astype(F32)
        scale = state_ref[3].astype(F32)
        scales = []
        for block in range(2):
            at = slice(128 * block, 128 * block + 128)
            first_old = rotate(code[:, at] * scale[:, block : block + 1])
            first = 0.9 * first_old + 0.1 * grad[:, at]
            weight_new = (weight[:, at] - 0.002 * first / (jnp.sqrt(second[:, at]) + 1e-08)).astype(BF)
            for z in range(8):
                copies_ref[z, :, at] = weight_new
            rotated = rotate(first)
            scales.append(jnp.max(jnp.abs(rotated), axis=1, keepdims=True).astype(BF).astype(F32))
            made_ref[0, :, at] = (rotated / (scales[block] + 1e-06)).astype(BF)
        made_ref[1] = second.astype(BF)
        column = lax.broadcasted_iota(jnp.int32, (72, 256), 1)
        made_ref[2] = jnp.where(column % 2 == 0, scales[0], scales[1]).astype(BF)

    return call(kernel, [shaped((8, 72, 256), BF), shaped((3, 72, 256), BF)])(terms, state, table)


def both_cores(*arrays):
    part = sum(a.reshape(-1, 256)[:16, :128] for a in arrays)
    return lax.ppermute(part, "c", SWAP)


def join(parts, q, z, ready):
    def kernel(place_ref, a_ref, b_ref, d_ref, e_ref, ready_ref, upper_ref, lower_ref, home_ref):
        column = lax.broadcasted_iota(jnp.int32, (72, 256), 1)
        scales = jnp.zeros((72, 256), F32)
        for step, ref in enumerate((a_ref, b_ref, d_ref, e_ref)):
            quarter = (place_ref[0] + step) % 4
            upper_ref[:, quarter] = ref[:4]
            lower_ref[:, quarter] = ref[4:8]
            home_ref[quarter] = ref[place_ref[1]]
            home_ref[4 + quarter] = ref[8]
            home_ref[8 + quarter] = ref[9]
            scales = jnp.where(column // 2 == quarter, ref[10].astype(F32), scales)
        home_ref[12] = scales.astype(BF)

    return call(
        kernel,
        [shaped((4, 4, 72, 256), BF)] * 2 + [shaped((13, 72, 256), BF)],
        (),
        [SCALAR] + [VMEM] * 5,
    )(jnp.stack([q, z]), *parts, ready)


def unpack(home):
    def kernel(home_ref, weight_ref, code_ref, second_ref, scale_ref):
        weight_ref[...] = home_ref[:4]
        code_ref[...] = home_ref[4:8]
        second_ref[...] = home_ref[8:12]
        for quarter in range(4):
            scale_ref[quarter] = home_ref[12][:, 2 * quarter : 2 * quarter + 2]

    return call(kernel, [shaped((4, 72, 256), BF)] * 3 + [shaped((4, 72, 2), BF)])(home)


def outputs_chunk(own, other, upper, lower, total):
    def kernel(own_ref, other_ref, upper_ref, lower_ref, *refs):
        for half, ref in ((slice(0, 256), own_ref), (slice(256, 512), other_ref)):
            value = jnp.dot(ref[:, :1152], upper_ref[...], preferred_element_type=F32)
            value += jnp.dot(ref[:, 1152:], lower_ref[...], preferred_element_type=F32)
            refs[-1][half] = value if total is None else refs[0][half] + value

    given = [] if total is None else [total]
    return call(kernel, shaped((512, 256), F32))(own, other, upper, lower, *given)


def per_device(tokens, cotangent, weight, code, scale, second_old):
    xl = lax.axis_index("xl")
    c = lax.axis_index("c")
    x = lax.axis_index("xh") * 2 + xl
    y = lax.axis_index("y")
    p = jnp.where(c == 0, x, y)
    q = jnp.where(c == 0, y, x)

    home = home_pairs()

    def taken(place, *behind):
        return lax.dynamic_slice(tokens, (0, after(place, *behind) * 2304), (256, 2304))

    def sent(step, *behind):
        return taken((1 - c) * 4 + (q + step) % 4, *behind)

    def kept(step, *behind):
        return taken(c * 4 + (p + step) % 4, *behind)

    def swap(chunk):
        return lax.ppermute(chunk, "c", SWAP)

    def pass_on(rows, step):
        return lax.ppermute(rows, PLANE, line_pairs(True, step))

    def rows_of(step, rows, *added, dtype=BF):
        return gradient_rows(own[step], other[step], cotangent, cot_other, rows, dtype, added)

    upper, lower, both = slice(0, 1152), slice(1152, 2304), slice(0, 2304)
    own, other = {}, {}
    cot_other = swap(cotangent)
    chunk = sent(2)
    other[2] = swap(after(chunk, cot_other))
    quarter = [0] * 32
    for _, holder, which in home:
        quarter[holder] = which
    here = ((xl * 2 + c) * 2 + lax.axis_index("xh")) * 4 + y
    at = after(jnp.asarray(quarter, jnp.int32)[here], chunk) * 72
    state = [weight, code, second_old, jnp.pad(scale, ((0, 0), (0, 254)))]
    state = jnp.stack([lax.dynamic_slice(a, (at, 0), (72, 256)) for a in state])
    state = lax.ppermute(state, PLANE, [(b, a) for a, b, _ in home])
    taken_here = [kept(step, chunk) for step in (2, 1, 3, 0)]
    taken_there = [sent(step, chunk) for step in (1, 3, 0)]
    *taken_here, one, three, zero = lax.optimization_barrier((*taken_here, *taken_there))
    own = dict(zip((2, 1, 3, 0), taken_here))
    other[1], other[3], other[0] = swap(one), swap(three), swap(zero)
    from_left, from_right = pass_on(rows_of(2, upper), 1), pass_on(rows_of(2, lower), 3)
    own[1] = after(own[1], state)
    left_lower = pass_on(rows_of(1, lower), 1)
    right_upper = pass_on(rows_of(3, upper), 3)
    left_upper = pass_on(rows_of(1, upper, from_left), 1)
    right_lower = pass_on(rows_of(3, lower, from_right), 3)
    total = rows_of(0, both, dtype=F32)

    keep, *pieces = sum_and_split(total, (left_upper, right_upper), (left_lower, right_lower), q)
    got = [lax.ppermute(pieces[step - 1], PLANE, line_pairs(False, step)) for step in (1, 3, 2)]
    grad = lax.all_to_all(sum_rows(keep, got), "z", 0, 0, tiled=True)
    copies, made = adam(grad, state, hadamard_table())

    slab = lax.all_to_all(copies, "z", 0, 0, tiled=True)
    slab = jnp.concatenate([slab, made])
    got = {step: lax.ppermute(slab, PLANE, line_pairs(False, step)) for step in (1, 3, 2)}
    upper, lower, made = join([slab, got[3], got[2], got[1]], q, lax.axis_index("z"), both_cores(*got.values()))
    upper, lower = upper.reshape(1152, 256), lower.reshape(1152, 256)
    left_upper, right_lower = pass_on(upper, 1), pass_on(lower, 3)
    left_lower, right_upper = pass_on(lower, 1), pass_on(upper, 3)

    for step in range(4):
        own[step] = kept(step, copies)
    out = outputs_chunk(own[0], other[0], upper, lower, None)
    made = lax.ppermute(after(made, out), PLANE, [(a, b) for a, b, _ in home])
    upper, lower = pass_on(left_upper, 1), pass_on(right_lower, 3)
    out = outputs_chunk(own[3], other[3], left_upper, left_lower, out)
    out = outputs_chunk(own[1], other[1], right_upper, right_lower, out)
    out = outputs_chunk(own[2], other[2], upper, lower, out)
    weight_new, code_new, second_new, scale_new = unpack(made)
    outputs = (out[:256] + lax.ppermute(out[256:], "c", SWAP)).astype(BF)
    rows = lambda a: a.reshape(288, a.shape[2])
    return (outputs, rows(weight_new), rows(code_new), rows(scale_new), rows(second_new))


def solution(mesh):
    split = Mesh(mesh.devices.reshape(2, 2, 2, 4, 8), AXES)
    tokens = P(AXES, None)
    shard = P(("xh", "y", "z"), None)
    return jax.shard_map(
        per_device,
        mesh=split,
        in_specs=(tokens, tokens, shard, shard, shard, shard),
        out_specs=(tokens, shard, shard, shard, shard),
        check_vma=False,
    )
```

time: 1120 us -> 159 us (0.14)
  waiting for transfers between devices: 1080 us -> 61.9 us
  starting transfers between devices: 0.12 us -> 45 us
  matrix products: 23.1 us -> 0 us
  Pallas kernels: 0 us -> 18.6 us
  local copies, waits for them, and re-layouts: 1.64 us -> 16.5 us
  blocking collectives: 0 us -> 13.2 us
  between operations: 13.8 us -> 1.68 us
    reduce_scatter x1 -> x0, waiting for transfers between devices: 880 us -> none  [per_device(): lax.psum_scatter(lax.dot_general(tokens, cotangent, contract, preferred_e...]
    all_gather x1 -> x0, waiting for transfers between devices: 159 us -> none  [per_device(): lax.all_gather(weight_new, 'shard', axis=0, tiled=True)]
    ppermute x0 -> x27, waiting for transfers between devices: none -> 51.1 us  [the longest x12 18.2 us: pass_on(): return lax.ppermute(rows, PLANE, line_pairs(True, step))]
    psum x1 -> x0, waiting for transfers between devices: 41.7 us -> none  [per_device(): grad = lax.psum(summed, 'replica') * factor]
    ppermute x0 -> x27, starting transfers between devices: none -> 36.6 us  [the longest x12 22.7 us: pass_on(): return lax.ppermute(rows, PLANE, line_pairs(True, step))]
    dot_general x4 -> x0, matrix products: 23.1 us -> none  [the longest x1 12.8 us: per_device(): lax.dot_general(tokens, cotangent, contract, preferred_element_type=jnp.f...]
    pallas_call x0 -> x16, Pallas kernels: none -> 18.6 us  [the longest x4 6.99 us: outputs_chunk(): call(kernel, shaped((512, 256), F32))(own, other, upper, lower, *given)]
    all_to_all x0 -> x1, blocking collectives: none -> 13.2 us  [per_device(): slab = lax.all_to_all(copies, 'z', 0, 0, tiled=True)]
  transfers between devices with their start and end apart: 3 -> 28, of which waited for: 3 -> 14; matrix products, arithmetic and copies ran while one was open for 0% -> 9% of each run, Pallas kernels for 0% -> 9%
where the time goes in v2:
time: 159 us
  waiting for transfers between devices  61.9 us (39%)
  starting transfers between devices  45 us (28%)
  Pallas kernels  18.6 us (12%)
  local copies, waits for them, and re-layouts  16.5 us (10%)
  blocking collectives  13.2 us (8%)
  between operations  1.68 us (1%)
  other arithmetic  1.67 us (1%)
    ppermute x12, starting transfers between devices, pass_on(): return lax.ppermute(rows, PLANE, line_pairs(True, step))  22.7 us
    ppermute x12, waiting for transfers between devices, pass_on(): return lax.ppermute(rows, PLANE, line_pairs(True, step))  18.2 us
    all_to_all x1, blocking collectives, per_device(): slab = lax.all_to_all(copies, 'z', 0, 0, tiled=True)  13.2 us
    dynamic_slice x3, local copies, waits for them, and re-layouts, taken(): lax.dynamic_slice(tokens, (0, after(place, *behind) * 2304), (256, 2304))  11.9 us
    ppermute x3, waiting for transfers between devices, per_device(): lax.ppermute(slab, PLANE, line_pairs(False, step))  11.5 us
    all_to_all x1, waiting for transfers between devices, per_device(): grad = lax.all_to_all(sum_rows(keep, got), 'z', 0, 0, tiled=True)  10.8 us
    ppermute x1, waiting for transfers between devices, per_device(): made = lax.ppermute(after(made, out), PLANE, [(a, b) for a, b, _ in home])  9.07 us
    all_to_all x1, starting transfers between devices, per_device(): grad = lax.all_to_all(sum_rows(keep, got), 'z', 0, 0, tiled=True)  8.46 us
  transfers between devices with their start and end apart: 28, of which 14 were waited for; matrix products, arithmetic and copies ran while one was open for 9% of the time, Pallas kernels for 9%

profile of v2, /device:TPU:24, one launch (start us, length us, event | category | flops | bytes accessed | tf_op | source)
XLA Modules:
  0.0 158.5 jit_solution(3949890424714059139)
XLA Ops:
  0.6 0.1 collective-permute-start.1
  0.8 2.4 %constant_dynamic-slice_fusion.11 = bf16[256,2304]{1,0:T(8,128)(2,1)} fusion(bf16[256,18432]{1,0:T(8,128)(2,1)} %param.7, s32[]{:T(128)S(6)} %select_n.98), kind=kLoop, calls=%fused_computation.23 | loop fusion | bytes 2359300 | tf_op jit(solution)/shard_map/dynamic_slice | solution.py:221
  3.2 0.5 collective-permute-start.4
  3.7 6.9 %constant_dynamic-slice_fusion.4 = (bf16[256,2304]{1,0:T(8,128)(2,1)}, bf16[256,2304]{1,0:T(8,128)(2,1)}, bf16[256,2304]{1,0:T(8,128)(2,1)}, bf16[256,2304]{1,0:...) fusion(bf16[256,18432]{1,0:T(8,128)(2,1)} %param.7, ...), kind=kLoop, calls=%fused_computation.16 | loop fusion | bytes 16515100 | tf_op jit(solution)/shard_map/dynamic_slice | solution.py:221
  10.7 0.5 collective-permute-start.3
  11.1 0.6 dynamic_slice.59
  12.4 0.1 copy.12
  12.6 0.8 dynamic-slice_bitcast_fusion
  13.4 3.5 %collective-permute-start.2 = (bf16[4,72,256]{2,1,0:T(8,128)(2,1)S(1)}, bf16[4,72,256]{2,1,0:T(8,128)(2,1)S(1)}, u32[]{:S(2)}, u32[]{:S(2)}) collective-permute-start(bf16[4,72,256]{2,1,0:T(8,128)(2,1)S(1)} %pad_maximum_fusion), channel_id=1, source_target_pairs={{192,0},{128,8},{0,16},{64,24},{8,128},{72,136},{200,144},{136,152... | collective-permute-start | bytes 442376 | tf_op jit(solution)/shard_map/ppermute | solution.py:250
  16.9 1.3 copy-done.1
  18.2 0.5 shard_map.115
  18.8 0.5 shard_map.111
  19.4 3.4 %collective-permute-done.2.state_ref = bf16[4,72,256]{2,1,0:T(8,128)(2,1)S(1)} collective-permute-done((bf16[4,72,256]{2,1,0:T(8,128)(2,1)S(1)}, bf16[4,72,256]{2,1,0:T(8,128)(2,1)S(1)}, u32[]{:S(2)}, u32[]{:S(2)}) %collective-permute-start.2) | collective-permute-done | bytes 147488 | tf_op jit(solution)/shard_map/ppermute | solution.py:250
  22.7 0.7 collective-permute-start.5
  23.4 0.5 shard_map.114
  24.0 3.1 %collective-permute-start.9 = (bf16[1152,256]{1,0:T(8,128)(2,1)S(1)}, bf16[1152,256]{1,0:T(8,128)(2,1)S(1)}, u32[]{:S(2)}, u32[]{:S(2)}) collective-permute-start(bf16[1152,256]{1,0:T(8,128)(2,1)S(1)} %shard_map.114), channel_id=1, source_target_pairs={{0,128},{8,136},{16,144},{24,152},{64,72},{72,80},{80,88},{88,64},... | collective-permute-start | bytes 1769480 | tf_op jit(solution)/shard_map/ppermute | solution.py:233
  27.0 1.8 %shard_map.113 = bf16[1152,256]{1,0:T(8,128)(2,1)S(1)} custom-call(bf16[256,2304]{1,0:T(8,128)(2,1)S(1)} %copy-done.3, bf16[256,2304]{1,0:T(8,128)(2,1)} %collective-permute-done.7.other_ref, bf16[256,256]{1,0:T(8,128)(2,1)S(1)} %copy-done.4, bf16[256,256]{1,0:T(8,128)(2,1)S(1)} %collective-permute-done.1.cot_other_ref), custom_call_target="tpu_custom_call" | custom-call | flops 1000 | bytes 1000 | tf_op jit(solution)/shard_map/pallas_call | solution.py:98
  28.8 0.3 collective-permute-start.8
  29.1 1.8 %shard_map.116 = bf16[1152,256]{1,0:T(8,128)(2,1)S(1)} custom-call(bf16[256,2304]{1,0:T(8,128)(2,1)S(1)} %copy-done.3, bf16[256,2304]{1,0:T(8,128)(2,1)} %collective-permute-done.7.other_ref, bf16[256,256]{1,0:T(8,128)(2,1)S(1)} %copy-done.4, bf16[256,256]{1,0:T(8,128)(2,1)S(1)} %collective-permute-done.1.cot_other_ref, ...), custom_call_target="tpu_custom_call" | custom-call | flops 1000 | bytes 1000 | tf_op jit(solution)/shard_map/pallas_call | solution.py:98
  31.0 3.7 %collective-permute-start.11 = (bf16[1152,256]{1,0:T(8,128)(2,1)S(1)}, bf16[1152,256]{1,0:T(8,128)(2,1)S(1)}, u32[]{:S(2)}, u32[]{:S(2)}) collective-permute-start(bf16[1152,256]{1,0:T(8,128)(2,1)S(1)} %shard_map.116), channel_id=1, source_target_pairs={{0,160},{8,168},{16,176},{24,184},{64,88},{72,64},{80,72},{88,80},... | collective-permute-start | bytes 1769480 | tf_op jit(solution)/shard_map/ppermute | solution.py:233
  34.6 0.5 shard_map.112
  35.2 0.3 collective-permute-start.6
  35.5 0.8 shard_map.110.total_ref
  36.3 0.2 copy-done.5
  36.5 3.7 %collective-permute-done.9.d_ref = bf16[1152,256]{1,0:T(8,128)(2,1)S(1)} collective-permute-done((bf16[1152,256]{1,0:T(8,128)(2,1)S(1)}, bf16[1152,256]{1,0:T(8,128)(2,1)S(1)}, u32[]{:S(2)}, u32[]{:S(2)}) %collective-permute-start.9) | collective-permute-done | bytes 589856 | tf_op jit(solution)/shard_map/ppermute | solution.py:233
  40.2 4.9 %collective-permute-done.11.e_ref = bf16[1152,256]{1,0:T(8,128)(2,1)S(1)} collective-permute-done((bf16[1152,256]{1,0:T(8,128)(2,1)S(1)}, bf16[1152,256]{1,0:T(8,128)(2,1)S(1)}, u32[]{:S(2)}, u32[]{:S(2)}) %collective-permute-start.11) | collective-permute-done | bytes 589856 | tf_op jit(solution)/shard_map/ppermute | solution.py:233
  45.1 1.4 collective-permute-done.6.a_ref
  46.5 0.5 shard_map.117
  47.1 2.4 %collective-permute-start.12 = (bf16[8,72,256]{2,1,0:T(8,128)(2,1)S(1)}, bf16[8,72,256]{2,1,0:T(8,128)(2,1)S(1)}, u32[]{:S(2)}, u32[]{:S(2)}) collective-permute-start(bf16[8,72,256]{2,1,0:T(8,128)(2,1)S(1)} %get-tuple-element.58), channel_id=1, source_target_pairs={{0,8},{8,16},{16,24},{24,0},{64,192},{72,200},{80,208},{88,216},{1... | collective-permute-start | bytes 884744 | tf_op jit(solution)/shard_map/ppermute | solution.py:265
  49.4 4.4 %collective-permute-start.14 = (bf16[8,72,256]{2,1,0:T(8,128)(2,1)S(1)}, bf16[8,72,256]{2,1,0:T(8,128)(2,1)S(1)}, u32[]{:S(2)}, u32[]{:S(2)}) collective-permute-start(bf16[8,72,256]{2,1,0:T(8,128)(2,1)S(1)} %get-tuple-element.60), channel_id=1, source_target_pairs={{0,16},{8,24},{16,0},{24,8},{64,96},{72,104},{80,112},{88,120},{12... | collective-permute-start | bytes 884744 | tf_op jit(solution)/shard_map/ppermute | solution.py:265
  53.9 3.5 %collective-permute-done.13.b_ref = bf16[8,72,256]{2,1,0:T(8,128)(2,1)S(1)} collective-permute-done((bf16[8,72,256]{2,1,0:T(8,128)(2,1)S(1)}, bf16[8,72,256]{2,1,0:T(8,128)(2,1)S(1)}, u32[]{:S(2)}, u32[]{:S(2)}) %collective-permute-start.13) | collective-permute-done | bytes 294944 | tf_op jit(solution)/shard_map/ppermute | solution.py:265
  57.4 4.4 %collective-permute-done.14.d_ref = bf16[8,72,256]{2,1,0:T(8,128)(2,1)S(1)} collective-permute-done((bf16[8,72,256]{2,1,0:T(8,128)(2,1)S(1)}, bf16[8,72,256]{2,1,0:T(8,128)(2,1)S(1)}, u32[]{:S(2)}, u32[]{:S(2)}) %collective-permute-start.14) | collective-permute-done | bytes 294944 | tf_op jit(solution)/shard_map/ppermute | solution.py:265
  61.7 0.8 shard_map.118
  62.6 8.5 %all-to-all-start = ((bf16[8,72,256]{2,1,0:T(8,128)(2,1)}), bf16[8,72,256]{2,1,0:T(8,128)(2,1)S(1)}, u32[]{:S(2)}, u32[]{:S(2)}) async-start(bf16[8,72,256]{2,1,0:T(8,128)(2,1)} %shard_map.118), calls=%async_computation | async-start | bytes 589824 | tf_op jit(solution)/shard_map/all_to_all | solution.py:266
  71.1 0.2 convert_multiply_fusion.table_ref
  71.3 10.8 %all-to-all-done.terms_ref = bf16[8,72,256]{2,1,0:T(8,128)(2,1)S(1)} async-done(((bf16[8,72,256]{2,1,0:T(8,128)(2,1)}), bf16[8,72,256]{2,1,0:T(8,128)(2,1)S(1)}, u32[]{:S(2)}, u32[]{:S(2)}) %all-to-all-start) | async-done | bytes 294944 | tf_op jit(solution)/shard_map/all_to_all | solution.py:266
  82.1 0.7 shard_map.119
  82.8 13.2 %all_to_all.10 = bf16[8,72,256]{2,1,0:T(8,128)(2,1)S(1)} all-to-all(bf16[8,72,256]{2,1,0:T(8,128)(2,1)S(1)} %get-tuple-element.61), channel_id=1, replica_groups=mesh['xl'=2,'c'=2,'xh'=2,'y'=4,'z'=8] {'z'}, dimensions={0} | all-to-all | bytes 589824 | tf_op jit(solution)/shard_map/all_to_all | solution.py:269
  96.1 2.0 %collective-permute-start.15 = (bf16[11,72,256]{2,1,0:T(8,128)(2,1)S(1)}, bf16[11,72,256]{2,1,0:T(8,128)(2,1)}, u32[]{:S(2)}, u32[]{:S(2)}) collective-permute-start(bf16[11,72,256]{2,1,0:T(8,128)(2,1)S(1)} %constant_dynamic-update-slice_fusion.a_ref), channel_id=1, source_target_pairs={{0,24},{8,0},{16,8},{24,16},{64,224},{72,232},{80,240},{88,248},{1... | collective-permute-start | bytes 1216520 | tf_op jit(solution)/shard_map/ppermute | solution.py:271
  98.1 0.2 collective-permute-start.16
  98.3 5.7 %collective-permute-done.17.e_ref = bf16[11,72,256]{2,1,0:T(8,128)(2,1)S(1)} collective-permute-done((bf16[11,72,256]{2,1,0:T(8,128)(2,1)S(1)}, bf16[11,72,256]{2,1,0:T(8,128)(2,1)S(1)}, u32[]{:S(2)}, u32[]{:S(2)}) %collective-permute-start.17) | collective-permute-done | bytes 405536 | tf_op jit(solution)/shard_map/ppermute | solution.py:271
  104.0 5.8 %collective-permute-done.15.b_ref = bf16[11,72,256]{2,1,0:T(8,128)(2,1)} collective-permute-done((bf16[11,72,256]{2,1,0:T(8,128)(2,1)S(1)}, bf16[11,72,256]{2,1,0:T(8,128)(2,1)}, u32[]{:S(2)}, u32[]{:S(2)}) %collective-permute-start.15) | collective-permute-done | bytes 405536 | tf_op jit(solution)/shard_map/ppermute | solution.py:271
  109.8 0.7 slice_add_fusion.1
  110.5 1.1 collective-permute-done.18.ready_ref
  111.6 2.3 %shard_map.120 = (bf16[4,4,72,256]{3,2,1,0:T(8,128)(2,1)}, bf16[4,4,72,256]{3,2,1,0:T(8,128)(2,1)}, bf16[13,72,256]{2,1,0:T(8,128)(2,1)S(1)}) custom-call(s32[2]{0:T(128)S(1)} %pad_add_fusion.place_ref, bf16[11,72,256]{2,1,0:T(8,128)(2,1)S(1)} %constant_dynamic-update-slice_fusion.a_ref, bf16[11,72,256]{2,1,0:T(8,128)(2,1)} %collective-permute-done.15.b_ref, ...), custom_call_target="tpu_custom_call" | custom-call | flops 1000 | bytes 1000 | tf_op jit(solution)/shard_map/pallas_call | solution.py:180
  113.9 0.8 copy-done.8
  114.7 0.8 collective-permute-start.19
  115.5 7.1 %collective-permute-start.21 = (bf16[1152,256]{1,0:T(8,128)(2,1)}, bf16[1152,256]{1,0:T(8,128)(2,1)}, u32[]{:S(2)}, u32[]{:S(2)}) collective-permute-start(bf16[1152,256]{1,0:T(8,128)(2,1)} %bitcast.11.lower_ref), channel_id=1, source_target_pairs={{0,160},{8,168},{16,176},{24,184},{64,88},{72,64},{80,72},{88,80},... | collective-permute-start | bytes 1769480 | tf_op jit(solution)/shard_map/ppermute | solution.py:233
  122.7 3.2 %collective-permute-start.23 = (bf16[1152,256]{1,0:T(8,128)(2,1)}, bf16[1152,256]{1,0:T(8,128)(2,1)S(1)}, u32[]{:S(2)}, u32[]{:S(2)}) collective-permute-start(bf16[1152,256]{1,0:T(8,128)(2,1)} %bitcast.10.upper_ref), channel_id=1, source_target_pairs={{0,160},{8,168},{16,176},{24,184},{64,88},{72,64},{80,72},{88,80},... | collective-permute-start | bytes 1769480 | tf_op jit(solution)/shard_map/ppermute | solution.py:233
  125.9 4.8 %collective-permute-done.19.upper_ref = bf16[1152,256]{1,0:T(8,128)(2,1)S(1)} collective-permute-done((bf16[1152,256]{1,0:T(8,128)(2,1)}, bf16[1152,256]{1,0:T(8,128)(2,1)S(1)}, u32[]{:S(2)}, u32[]{:S(2)}) %collective-permute-start.19) | collective-permute-done | bytes 589856 | tf_op jit(solution)/shard_map/ppermute | solution.py:233
  130.7 3.3 %collective-permute-start.22 = (bf16[1152,256]{1,0:T(8,128)(2,1)}, bf16[1152,256]{1,0:T(8,128)(2,1)S(1)}, u32[]{:S(2)}, u32[]{:S(2)}) collective-permute-start(bf16[1152,256]{1,0:T(8,128)(2,1)} %collective-permute-done.21.lower_ref), channel_id=1, source_target_pairs={{0,160},{8,168},{16,176},{24,184},{64,88},{72,64},{80,72},{88,80},... | collective-permute-start | bytes 1769480 | tf_op jit(solution)/shard_map/ppermute | solution.py:233
  134.1 2.6 %constant_dynamic-slice_fusion = (bf16[256,2304]{1,0:T(8,128)(2,1)S(1)}, bf16[256,2304]{1,0:T(8,128)(2,1)S(1)}, bf16[256,2304]{1,0:T(8,128)(2,1)S(1)}, bf16[256,2304]{1,0:T(8,128)(2,1)S(1)}) fusion(bf16[256,18432]{1,0:T(8,128)(2,1)} %param.7, s32[]{:T(128)S(6)} %select_n.117, s32[]{:T(128)S(6)} %select_n.115, s32[]{:T(128)S(6)} %select_n.114, s32[]{:T(128)S(6)} %select_n.116), kind=kLoop, calls=%fused_computation.12 | loop fusion | bytes 9437200 | tf_op jit(solution)/shard_map/dynamic_slice | solution.py:221
  136.7 2.1 %shard_map.121.refs_0_ = f32[512,256]{1,0:T(8,128)S(1)} custom-call(bf16[256,2304]{1,0:T(8,128)(2,1)S(1)} %get-tuple-element.80.own_ref, bf16[256,2304]{1,0:T(8,128)(2,1)S(1)} %copy-done.6, bf16[1152,256]{1,0:T(8,128)(2,1)} %bitcast.10.upper_ref, bf16[1152,256]{1,0:T(8,128)(2,1)} %bitcast.11.lower_ref), custom_call_target="tpu_custom_call" | custom-call | flops 1000 | bytes 1000 | tf_op jit(solution)/shard_map/pallas_call | solution.py:207
  138.9 0.1 collective-permute-start.26
  139.0 2.1 %shard_map.122.refs_0_ = f32[512,256]{1,0:T(8,128)S(1)} custom-call(bf16[256,2304]{1,0:T(8,128)(2,1)S(1)} %get-tuple-element.83.own_ref, bf16[256,2304]{1,0:T(8,128)(2,1)} %collective-permute-done.7.other_ref, bf16[1152,256]{1,0:T(8,128)(2,1)S(1)} %collective-permute-done.19.upper_ref, bf16[1152,256]{1,0:T(8,128)(2,1)S(1)} %collective-permute-done.24.lower_ref, ...), custom_call_target="tpu_custom_call" | custom-call | flops 1000 | bytes 1000 | tf_op jit(solution)/shard_map/pallas_call | solution.py:207
  141.1 1.9 %shard_map.123.refs_0_ = f32[512,256]{1,0:T(8,128)S(1)} custom-call(bf16[256,2304]{1,0:T(8,128)(2,1)S(1)} %get-tuple-element.81.own_ref, bf16[256,2304]{1,0:T(8,128)(2,1)S(1)} %collective-permute-done.3.other_ref, bf16[1152,256]{1,0:T(8,128)(2,1)S(1)} %collective-permute-done.23.upper_ref, bf16[1152,256]{1,0:T(8,128)(2,1)} %collective-permute-done.21.lower_ref, ...), custom_call_target="tpu_custom_call" | custom-call | flops 1000 | bytes 1000 | tf_op jit(solution)/shard_map/pallas_call | solution.py:207
  143.0 0.3 collective-permute-done.20.upper_ref
  143.4 3.0 %collective-permute-done.22.lower_ref = bf16[1152,256]{1,0:T(8,128)(2,1)S(1)} collective-permute-done((bf16[1152,256]{1,0:T(8,128)(2,1)}, bf16[1152,256]{1,0:T(8,128)(2,1)S(1)}, u32[]{:S(2)}, u32[]{:S(2)}) %collective-permute-start.22) | collective-permute-done | bytes 589856 | tf_op jit(solution)/shard_map/ppermute | solution.py:233
  146.4 0.8 shard_map.124
  147.2 0.1 collective-permute-start.25
  147.3 9.1 %collective-permute-done.26.home_ref = bf16[13,72,256]{2,1,0:T(8,128)(2,1)S(1)} collective-permute-done((bf16[13,72,256]{2,1,0:T(8,128)(2,1)S(1)}, bf16[13,72,256]{2,1,0:T(8,128)(2,1)S(1)}, u32[]{:S(2)}, u32[]{:S(2)}) %collective-permute-start.26) | collective-permute-done | bytes 479264 | tf_op jit(solution)/shard_map/ppermute | solution.py:280
  156.4 0.8 shard_map.125
  157.2 0.7 copy.13
  157.8 0.7 fusion
  (54 shorter events, 0.6 us)
Async XLA Ops:
  0.6 11.9 %copy-start = (bf16[288,256]{1,0:T(8,128)(2,1)S(1)}, bf16[288,256]{1,0:T(8,128)(2,1)}, u32[]{:S(2)}) copy-start(bf16[288,256]{1,0:T(8,128)(2,1)} %param.9) | copy-start | bytes 442372
  0.6 2.5 %collective-permute-start.1 = (bf16[256,256]{1,0:T(8,128)(2,1)}, bf16[256,256]{1,0:T(8,128)(2,1)S(1)}, u32[]{:S(2)}, u32[]{:S(2)}) collective-permute-start(bf16[256,256]{1,0:T(8,128)(2,1)} %cot_own_ref.13), channel_id=1, source_target_pairs={{0,64},{64,0},{1,65},{65,1},{2,66},{66,2},{3,67},{67,3},{4,68},{68... | collective-permute-start | bytes 393224 | tf_op jit(solution)/shard_map/ppermute | solution.py:230
  3.2 7.9 %copy-start.11 = (s32[32]{0:T(128)S(1)}, s32[32]{0:T(128)}, u32[]{:S(2)}) copy-start(s32[32]{0:T(128)} %constant.104.clone) | copy-start | bytes 388
  3.2 9.2 %copy-start.10 = (bf16[288,2]{0,1:T(2,128)(2,1)S(1)}, bf16[288,2]{0,1:T(2,128)(2,1)}, u32[]{:S(2)}) copy-start(bf16[288,2]{0,1:T(2,128)(2,1)} %param.11) | copy-start | bytes 3460
  3.2 13.7 %copy-start.4 = (bf16[256,256]{1,0:T(8,128)(2,1)S(1)}, bf16[256,256]{1,0:T(8,128)(2,1)}, u32[]{:S(2)}) copy-start(bf16[256,256]{1,0:T(8,128)(2,1)} %cot_own_ref.13) | copy-start | bytes 393220
  3.2 13.7 %collective-permute-start.4 = (bf16[256,2304]{1,0:T(8,128)(2,1)}, bf16[256,2304]{1,0:T(8,128)(2,1)S(1)}, u32[]{:S(2)}, u32[]{:S(2)}) collective-permute-start(bf16[256,2304]{1,0:T(8,128)(2,1)} %constant_dynamic-slice_fusion.11), channel_id=1, source_target_pairs={{0,64},{64,0},{1,65},{65,1},{2,66},{66,2},{3,67},{67,3},{4,68},{68... | collective-permute-start | bytes 3538952 | tf_op jit(solution)/shard_map/ppermute | solution.py:230
  10.6 16.4 %collective-permute-start.7 = (bf16[256,2304]{1,0:T(8,128)(2,1)}, bf16[256,2304]{1,0:T(8,128)(2,1)}, u32[]{:S(2)}, u32[]{:S(2)}) collective-permute-start(bf16[256,2304]{1,0:T(8,128)(2,1)} %get-tuple-element.56), channel_id=1, source_target_pairs={{0,64},{64,0},{1,65},{65,1},{2,66},{66,2},{3,67},{67,3},{4,68},{68... | collective-permute-start | bytes 3538952 | tf_op jit(solution)/shard_map/ppermute | solution.py:230
  10.7 12.8 %collective-permute-start.3 = (bf16[256,2304]{1,0:T(8,128)(2,1)}, bf16[256,2304]{1,0:T(8,128)(2,1)S(1)}, u32[]{:S(2)}, u32[]{:S(2)}) collective-permute-start(bf16[256,2304]{1,0:T(8,128)(2,1)} %get-tuple-element.52), channel_id=1, source_target_pairs={{0,64},{64,0},{1,65},{65,1},{2,66},{66,2},{3,67},{67,3},{4,68},{68... | collective-permute-start | bytes 3538952 | tf_op jit(solution)/shard_map/ppermute | solution.py:230
  13.4 9.3 %collective-permute-start.2 = (bf16[4,72,256]{2,1,0:T(8,128)(2,1)S(1)}, bf16[4,72,256]{2,1,0:T(8,128)(2,1)S(1)}, u32[]{:S(2)}, u32[]{:S(2)}) collective-permute-start(bf16[4,72,256]{2,1,0:T(8,128)(2,1)S(1)} %pad_maximum_fusion), channel_id=1, source_target_pairs={{192,0},{128,8},{0,16},{64,24},{8,128},{72,136},{200,144},{136,152... | collective-permute-start | bytes 442376 | tf_op jit(solution)/shard_map/ppermute | solution.py:250
  16.9 18.5 %collective-permute-start = (bf16[256,2304]{1,0:T(8,128)(2,1)}, bf16[256,2304]{1,0:T(8,128)(2,1)S(1)}, u32[]{:S(2)}, u32[]{:S(2)}) collective-permute-start(bf16[256,2304]{1,0:T(8,128)(2,1)} %get-tuple-element.48), channel_id=1, source_target_pairs={{0,64},{64,0},{1,65},{65,1},{2,66},{66,2},{3,67},{67,3},{4,68},{68... | collective-permute-start | bytes 3538952 | tf_op jit(solution)/shard_map/ppermute | solution.py:230
  16.9 1.3 copy-start.1
  18.7 4.7 %copy-start.2 = (bf16[256,2304]{1,0:T(8,128)(2,1)S(1)}, bf16[256,2304]{1,0:T(8,128)(2,1)}, u32[]{:S(2)}) copy-start(bf16[256,2304]{1,0:T(8,128)(2,1)} %get-tuple-element.51.own_ref) | copy-start | bytes 3538948
  18.7 10.4 %collective-permute-start.10 = (bf16[1152,256]{1,0:T(8,128)(2,1)S(1)}, bf16[1152,256]{1,0:T(8,128)(2,1)S(1)}, u32[]{:S(2)}, u32[]{:S(2)}) collective-permute-start(bf16[1152,256]{1,0:T(8,128)(2,1)S(1)} %shard_map.115), channel_id=1, source_target_pairs={{0,160},{8,168},{16,176},{24,184},{64,88},{72,64},{80,72},{88,80},... | collective-permute-start | bytes 1769480 | tf_op jit(solution)/shard_map/ppermute | solution.py:233
  19.3 7.7 %copy-start.3 = (bf16[256,2304]{1,0:T(8,128)(2,1)S(1)}, bf16[256,2304]{1,0:T(8,128)(2,1)}, u32[]{:S(2)}) copy-start(bf16[256,2304]{1,0:T(8,128)(2,1)} %get-tuple-element.55.own_ref) | copy-start | bytes 3538948
  22.7 11.9 %collective-permute-start.5 = (bf16[1152,256]{1,0:T(8,128)(2,1)S(1)}, bf16[1152,256]{1,0:T(8,128)(2,1)S(1)}, u32[]{:S(2)}, u32[]{:S(2)}) collective-permute-start(bf16[1152,256]{1,0:T(8,128)(2,1)S(1)} %shard_map.111), channel_id=1, source_target_pairs={{0,128},{8,136},{16,144},{24,152},{64,72},{72,80},{80,88},{88,64},... | collective-permute-start | bytes 1769480 | tf_op jit(solution)/shard_map/ppermute | solution.py:233
  24.0 16.2 %collective-permute-start.9 = (bf16[1152,256]{1,0:T(8,128)(2,1)S(1)}, bf16[1152,256]{1,0:T(8,128)(2,1)S(1)}, u32[]{:S(2)}, u32[]{:S(2)}) collective-permute-start(bf16[1152,256]{1,0:T(8,128)(2,1)S(1)} %shard_map.114), channel_id=1, source_target_pairs={{0,128},{8,136},{16,144},{24,152},{64,72},{72,80},{80,88},{88,64},... | collective-permute-start | bytes 1769480 | tf_op jit(solution)/shard_map/ppermute | solution.py:233
  28.8 11.3 %collective-permute-start.8 = (bf16[1152,256]{1,0:T(8,128)(2,1)S(1)}, bf16[1152,256]{1,0:T(8,128)(2,1)S(1)}, u32[]{:S(2)}, u32[]{:S(2)}) collective-permute-start(bf16[1152,256]{1,0:T(8,128)(2,1)S(1)} %shard_map.113), channel_id=1, source_target_pairs={{0,160},{8,168},{16,176},{24,184},{64,88},{72,64},{80,72},{88,80},... | collective-permute-start | bytes 1769480 | tf_op jit(solution)/shard_map/ppermute | solution.py:233
  30.9 4.5 %copy-start.7 = (bf16[256,2304]{1,0:T(8,128)(2,1)S(1)}, bf16[256,2304]{1,0:T(8,128)(2,1)}, u32[]{:S(2)}) copy-start(bf16[256,2304]{1,0:T(8,128)(2,1)} %get-tuple-element.47.own_ref) | copy-start | bytes 3538948
  31.0 14.1 %collective-permute-start.11 = (bf16[1152,256]{1,0:T(8,128)(2,1)S(1)}, bf16[1152,256]{1,0:T(8,128)(2,1)S(1)}, u32[]{:S(2)}, u32[]{:S(2)}) collective-permute-start(bf16[1152,256]{1,0:T(8,128)(2,1)S(1)} %shard_map.116), channel_id=1, source_target_pairs={{0,160},{8,168},{16,176},{24,184},{64,88},{72,64},{80,72},{88,80},... | collective-permute-start | bytes 1769480 | tf_op jit(solution)/shard_map/ppermute | solution.py:233
  35.2 11.4 %collective-permute-start.6 = (bf16[1152,256]{1,0:T(8,128)(2,1)S(1)}, bf16[1152,256]{1,0:T(8,128)(2,1)S(1)}, u32[]{:S(2)}, u32[]{:S(2)}) collective-permute-start(bf16[1152,256]{1,0:T(8,128)(2,1)S(1)} %shard_map.112), channel_id=1, source_target_pairs={{0,128},{8,136},{16,144},{24,152},{64,72},{72,80},{80,88},{88,64},... | collective-permute-start | bytes 1769480 | tf_op jit(solution)/shard_map/ppermute | solution.py:233
  35.4 1.0 copy-start.5
  47.1 6.8 %collective-permute-start.12 = (bf16[8,72,256]{2,1,0:T(8,128)(2,1)S(1)}, bf16[8,72,256]{2,1,0:T(8,128)(2,1)S(1)}, u32[]{:S(2)}, u32[]{:S(2)}) collective-permute-start(bf16[8,72,256]{2,1,0:T(8,128)(2,1)S(1)} %get-tuple-element.58), channel_id=1, source_target_pairs={{0,8},{8,16},{16,24},{24,0},{64,192},{72,200},{80,208},{88,216},{1... | collective-permute-start | bytes 884744 | tf_op jit(solution)/shard_map/ppermute | solution.py:265
  49.4 7.9 %collective-permute-start.13 = (bf16[8,72,256]{2,1,0:T(8,128)(2,1)S(1)}, bf16[8,72,256]{2,1,0:T(8,128)(2,1)S(1)}, u32[]{:S(2)}, u32[]{:S(2)}) collective-permute-start(bf16[8,72,256]{2,1,0:T(8,128)(2,1)S(1)} %get-tuple-element.59), channel_id=1, source_target_pairs={{0,24},{8,0},{16,8},{24,16},{64,224},{72,232},{80,240},{88,248},{1... | collective-permute-start | bytes 884744 | tf_op jit(solution)/shard_map/ppermute | solution.py:265
  49.4 12.3 %collective-permute-start.14 = (bf16[8,72,256]{2,1,0:T(8,128)(2,1)S(1)}, bf16[8,72,256]{2,1,0:T(8,128)(2,1)S(1)}, u32[]{:S(2)}, u32[]{:S(2)}) collective-permute-start(bf16[8,72,256]{2,1,0:T(8,128)(2,1)S(1)} %get-tuple-element.60), channel_id=1, source_target_pairs={{0,16},{8,24},{16,0},{24,8},{64,96},{72,104},{80,112},{88,120},{12... | collective-permute-start | bytes 884744 | tf_op jit(solution)/shard_map/ppermute | solution.py:265
  62.6 19.5 %all-to-all-start = ((bf16[8,72,256]{2,1,0:T(8,128)(2,1)}), bf16[8,72,256]{2,1,0:T(8,128)(2,1)S(1)}, u32[]{:S(2)}, u32[]{:S(2)}) async-start(bf16[8,72,256]{2,1,0:T(8,128)(2,1)} %shard_map.118), calls=%async_computation | async-start | bytes 589824 | tf_op jit(solution)/shard_map/all_to_all | solution.py:266
  96.0 8.0 %collective-permute-start.17 = (bf16[11,72,256]{2,1,0:T(8,128)(2,1)S(1)}, bf16[11,72,256]{2,1,0:T(8,128)(2,1)S(1)}, u32[]{:S(2)}, u32[]{:S(2)}) collective-permute-start(bf16[11,72,256]{2,1,0:T(8,128)(2,1)S(1)} %constant_dynamic-update-slice_fusion.a_ref), channel_id=1, source_target_pairs={{0,8},{8,16},{16,24},{24,0},{64,192},{72,200},{80,208},{88,216},{1... | collective-permute-start | bytes 1216520 | tf_op jit(solution)/shard_map/ppermute | solution.py:271
  96.1 13.6 %collective-permute-start.15 = (bf16[11,72,256]{2,1,0:T(8,128)(2,1)S(1)}, bf16[11,72,256]{2,1,0:T(8,128)(2,1)}, u32[]{:S(2)}, u32[]{:S(2)}) collective-permute-start(bf16[11,72,256]{2,1,0:T(8,128)(2,1)S(1)} %constant_dynamic-update-slice_fusion.a_ref), channel_id=1, source_target_pairs={{0,24},{8,0},{16,8},{24,16},{64,224},{72,232},{80,240},{88,248},{1... | collective-permute-start | bytes 1216520 | tf_op jit(solution)/shard_map/ppermute | solution.py:271
  98.1 11.6 %collective-permute-start.16 = (bf16[11,72,256]{2,1,0:T(8,128)(2,1)S(1)}, bf16[11,72,256]{2,1,0:T(8,128)(2,1)}, u32[]{:S(2)}, u32[]{:S(2)}) collective-permute-start(bf16[11,72,256]{2,1,0:T(8,128)(2,1)S(1)} %constant_dynamic-update-slice_fusion.a_ref), channel_id=1, source_target_pairs={{0,16},{8,24},{16,0},{24,8},{64,96},{72,104},{80,112},{88,120},{12... | collective-permute-start | bytes 1216520 | tf_op jit(solution)/shard_map/ppermute | solution.py:271
  110.5 1.2 collective-permute-start.18
  113.9 0.8 copy-start.8
  114.7 16.0 %collective-permute-start.19 = (bf16[1152,256]{1,0:T(8,128)(2,1)}, bf16[1152,256]{1,0:T(8,128)(2,1)S(1)}, u32[]{:S(2)}, u32[]{:S(2)}) collective-permute-start(bf16[1152,256]{1,0:T(8,128)(2,1)} %bitcast.10.upper_ref), channel_id=1, source_target_pairs={{0,128},{8,136},{16,144},{24,152},{64,72},{72,80},{80,88},{88,64},... | collective-permute-start | bytes 1769480 | tf_op jit(solution)/shard_map/ppermute | solution.py:233
  115.5 15.2 %collective-permute-start.21 = (bf16[1152,256]{1,0:T(8,128)(2,1)}, bf16[1152,256]{1,0:T(8,128)(2,1)}, u32[]{:S(2)}, u32[]{:S(2)}) collective-permute-start(bf16[1152,256]{1,0:T(8,128)(2,1)} %bitcast.11.lower_ref), channel_id=1, source_target_pairs={{0,160},{8,168},{16,176},{24,184},{64,88},{72,64},{80,72},{88,80},... | collective-permute-start | bytes 1769480 | tf_op jit(solution)/shard_map/ppermute | solution.py:233
  122.6 14.1 %copy-start.6 = (bf16[256,2304]{1,0:T(8,128)(2,1)S(1)}, bf16[256,2304]{1,0:T(8,128)(2,1)}, u32[]{:S(2)}) copy-start(bf16[256,2304]{1,0:T(8,128)(2,1)} %copy-done.5) | copy-start | bytes 3538948
  122.6 16.3 %collective-permute-start.24 = (bf16[1152,256]{1,0:T(8,128)(2,1)}, bf16[1152,256]{1,0:T(8,128)(2,1)S(1)}, u32[]{:S(2)}, u32[]{:S(2)}) collective-permute-start(bf16[1152,256]{1,0:T(8,128)(2,1)} %bitcast.11.lower_ref), channel_id=1, source_target_pairs={{0,128},{8,136},{16,144},{24,152},{64,72},{72,80},{80,88},{88,64},... | collective-permute-start | bytes 1769480 | tf_op jit(solution)/shard_map/ppermute | solution.py:233
  122.7 18.5 %collective-permute-start.23 = (bf16[1152,256]{1,0:T(8,128)(2,1)}, bf16[1152,256]{1,0:T(8,128)(2,1)S(1)}, u32[]{:S(2)}, u32[]{:S(2)}) collective-permute-start(bf16[1152,256]{1,0:T(8,128)(2,1)} %bitcast.10.upper_ref), channel_id=1, source_target_pairs={{0,160},{8,168},{16,176},{24,184},{64,88},{72,64},{80,72},{88,80},... | collective-permute-start | bytes 1769480 | tf_op jit(solution)/shard_map/ppermute | solution.py:233
  130.7 12.6 %collective-permute-start.20 = (bf16[1152,256]{1,0:T(8,128)(2,1)S(1)}, bf16[1152,256]{1,0:T(8,128)(2,1)S(1)}, u32[]{:S(2)}, u32[]{:S(2)}) collective-permute-start(bf16[1152,256]{1,0:T(8,128)(2,1)S(1)} %collective-permute-done.19.upper_ref), channel_id=1, source_target_pairs={{0,128},{8,136},{16,144},{24,152},{64,72},{72,80},{80,88},{88,64},... | collective-permute-start | bytes 1769480 | tf_op jit(solution)/shard_map/ppermute | solution.py:233
  130.7 15.6 %collective-permute-start.22 = (bf16[1152,256]{1,0:T(8,128)(2,1)}, bf16[1152,256]{1,0:T(8,128)(2,1)S(1)}, u32[]{:S(2)}, u32[]{:S(2)}) collective-permute-start(bf16[1152,256]{1,0:T(8,128)(2,1)} %collective-permute-done.21.lower_ref), channel_id=1, source_target_pairs={{0,160},{8,168},{16,176},{24,184},{64,88},{72,64},{80,72},{88,80},... | collective-permute-start | bytes 1769480 | tf_op jit(solution)/shard_map/ppermute | solution.py:233
  136.7 2.2 %copy-start.9 = (bf16[13,72,256]{2,1,0:T(8,128)(2,1)S(1)}, bf16[13,72,256]{2,1,0:T(8,128)(2,1)}, u32[]{:S(2)}) copy-start(bf16[13,72,256]{2,1,0:T(8,128)(2,1)} %copy-done.8) | copy-start | bytes 1437700
  138.9 17.5 %collective-permute-start.26 = (bf16[13,72,256]{2,1,0:T(8,128)(2,1)S(1)}, bf16[13,72,256]{2,1,0:T(8,128)(2,1)S(1)}, u32[]{:S(2)}, u32[]{:S(2)}) collective-permute-start(bf16[13,72,256]{2,1,0:T(8,128)(2,1)S(1)} %copy-done.9), channel_id=1, source_target_pairs={{0,192},{8,128},{16,0},{24,64},{128,8},{136,72},{144,200},{152,136... | collective-permute-start | bytes 1437704 | tf_op jit(solution)/shard_map/ppermute | solution.py:280
  147.2 10.6 %collective-permute-start.25 = (f32[256,256]{1,0:T(8,128)S(1)}, f32[256,256]{1,0:T(8,128)S(1)}, u32[]{:S(2)}, u32[]{:S(2)}) collective-permute-start(f32[256,256]{1,0:T(8,128)S(1)} %slice.24), channel_id=1, source_target_pairs={{0,64},{64,0},{1,65},{65,1},{2,66},{66,2},{3,67},{67,3},{4,68},{68... | collective-permute-start | bytes 786440 | tf_op jit(solution)/shard_map/ppermute | solution.py:286

commit v3 on v2

--- a/solution.py
+++ b/solution.py
@@ -80,9 +80,10 @@
 
 SCALAR = pl.BlockSpec(memory_space=pltpu.SMEM)
 VMEM = pl.BlockSpec(memory_space=pltpu.VMEM)
-
-
-def gradient_rows(own, other, cot_own, cot_other, rows, dtype, added=()):
+ANY = pl.BlockSpec(memory_space=pl.ANY)
+
+
+def gradient_rows(own, other, cot_own, cot_other, rows, dtype, added=(), behind=()):
     contract = (((0,), (0,)), ((), ()))
     size = rows.stop - rows.start
 
@@ -91,11 +92,12 @@
             part = pl.ds(rows.start + i, 384)
             term = lax.dot_general(own_ref[:, part], cot_own_ref[...], contract, preferred_element_type=F32)
             term += lax.dot_general(other_ref[:, part], cot_other_ref[...], contract, preferred_element_type=F32)
-            for ref in refs[:-1]:
+            for ref in refs[: len(added)]:
                 term += ref[pl.ds(i, 384), :].astype(F32)
             refs[-1][pl.ds(i, 384), :] = term.astype(dtype)
 
-    return call(kernel, shaped((size, 256), dtype))(own, other, cot_own, cot_other, *added)
+    specs = [VMEM] * (4 + len(added)) + [ANY] * len(behind)
+    return call(kernel, shaped((size, 256), dtype), (), specs)(own, other, cot_own, cot_other, *added, *behind)
 
 
 def sum_and_split(total, upper, lower, q):
@@ -158,9 +160,19 @@
     return call(kernel, [shaped((8, 72, 256), BF), shaped((3, 72, 256), BF)])(terms, state, table)
 
 
+def stacked(slab, made):
+    def kernel(slab_ref, made_ref, out_ref):
+        out_ref[:8] = slab_ref[...]
+        out_ref[8:] = made_ref[...]
+
+    return call(kernel, shaped((11, 72, 256), BF))(slab, made)
+
+
 def both_cores(*arrays):
-    part = sum(a.reshape(-1, 256)[:16, :128] for a in arrays)
-    return lax.ppermute(part, "c", SWAP)
+    def kernel(*refs):
+        refs[-1][...] = jnp.zeros((16, 128), BF)
+
+    return lax.ppermute(call(kernel, shaped((16, 128), BF), (), [ANY] * len(arrays))(*arrays), "c", SWAP)
 
 
 def join(parts, q, z, ready):
@@ -181,7 +193,7 @@
         kernel,
         [shaped((4, 4, 72, 256), BF)] * 2 + [shaped((13, 72, 256), BF)],
         (),
-        [SCALAR] + [VMEM] * 5,
+        [SCALAR] + [VMEM] * 4 + [ANY],
     )(jnp.stack([q, z]), *parts, ready)
 
 
@@ -232,19 +244,20 @@
     def pass_on(rows, step):
         return lax.ppermute(rows, PLANE, line_pairs(True, step))
 
-    def rows_of(step, rows, *added, dtype=BF):
-        return gradient_rows(own[step], other[step], cotangent, cot_other, rows, dtype, added)
+    def rows_of(step, rows, *added, dtype=BF, behind=()):
+        return gradient_rows(own[step], other[step], cotangent, cot_other, rows, dtype, added, behind)
 
     upper, lower, both = slice(0, 1152), slice(1152, 2304), slice(0, 2304)
     own, other = {}, {}
     cot_other = swap(cotangent)
     chunk = sent(2)
     other[2] = swap(after(chunk, cot_other))
-    quarter = [0] * 32
+    words = [0] * 4
     for _, holder, which in home:
-        quarter[holder] = which
-    here = ((xl * 2 + c) * 2 + lax.axis_index("xh")) * 4 + y
-    at = after(jnp.asarray(quarter, jnp.int32)[here], chunk) * 72
+        words[holder // 8] += which << (holder % 8 * 2)
+    word = jnp.where(xl == 0, jnp.where(c == 0, words[0], words[1]), jnp.where(c == 0, words[2], words[3]))
+    at = lax.shift_right_logical(word, 2 * (lax.axis_index("xh") * 4 + y)) % 4
+    at = after(at, chunk) * 72
     state = [weight, code, second_old, jnp.pad(scale, ((0, 0), (0, 254)))]
     state = jnp.stack([lax.dynamic_slice(a, (at, 0), (72, 256)) for a in state])
     state = lax.ppermute(state, PLANE, [(b, a) for a, b, _ in home])
@@ -254,30 +267,31 @@
     own = dict(zip((2, 1, 3, 0), taken_here))
     other[1], other[3], other[0] = swap(one), swap(three), swap(zero)
     from_left, from_right = pass_on(rows_of(2, upper), 1), pass_on(rows_of(2, lower), 3)
-    own[1] = after(own[1], state)
     left_lower = pass_on(rows_of(1, lower), 1)
     right_upper = pass_on(rows_of(3, upper), 3)
     left_upper = pass_on(rows_of(1, upper, from_left), 1)
     right_lower = pass_on(rows_of(3, lower, from_right), 3)
-    total = rows_of(0, both, dtype=F32)
+    total = rows_of(0, both, dtype=F32, behind=(state,))
 
     keep, *pieces = sum_and_split(total, (left_upper, right_upper), (left_lower, right_lower), q)
     got = [lax.ppermute(pieces[step - 1], PLANE, line_pairs(False, step)) for step in (1, 3, 2)]
-    grad = lax.all_to_all(sum_rows(keep, got), "z", 0, 0, tiled=True)
+    grad = sum_rows(keep, got)
+    own = [kept(step, grad) for step in range(4)]
+    grad = lax.all_to_all(grad, "z", 0, 0, tiled=True)
+    state, *own = lax.optimization_barrier((state, *own))
     copies, made = adam(grad, state, hadamard_table())
 
     slab = lax.all_to_all(copies, "z", 0, 0, tiled=True)
-    slab = jnp.concatenate([slab, made])
+    slab = stacked(slab, made)
     got = {step: lax.ppermute(slab, PLANE, line_pairs(False, step)) for step in (1, 3, 2)}
-    upper, lower, made = join([slab, got[3], got[2], got[1]], q, lax.axis_index("z"), both_cores(*got.values()))
+    parts = [slab, got[3], got[2], got[1]]
+    upper, lower, made = join(parts, q, lax.axis_index("z"), both_cores(*got.values()))
     upper, lower = upper.reshape(1152, 256), lower.reshape(1152, 256)
     left_upper, right_lower = pass_on(upper, 1), pass_on(lower, 3)
     left_lower, right_upper = pass_on(lower, 1), pass_on(upper, 3)
 
-    for step in range(4):
-        own[step] = kept(step, copies)
     out = outputs_chunk(own[0], other[0], upper, lower, None)
-    made = lax.ppermute(after(made, out), PLANE, [(a, b) for a, b, _ in home])
+    made = lax.ppermute(made, PLANE, [(a, b) for a, b, _ in home])
     upper, lower = pass_on(left_upper, 1), pass_on(right_lower, 3)
     out = outputs_chunk(own[3], other[3], left_upper, left_lower, out)
     out = outputs_chunk(own[1], other[1], right_upper, right_lower, out)

time: 159 us -> 148 us (0.931)
  waiting for transfers between devices: 61.9 us -> 52.7 us
  starting transfers between devices: 45 us -> 42.1 us
    all_to_all x1, waiting for transfers between devices: 10.8 us -> 6.06 us  [per_device(): grad = lax.all_to_all(grad, 'z', 0, 0, tiled=True)]
    ppermute x2, waiting for transfers between devices: 10.2 us -> 5.64 us  [the longest x1 4.55 us: per_device(): made = lax.ppermute(made, PLANE, [(a, b) for a, b, _ in home])]
    ppermute x1, starting transfers between devices: 0.09 us -> 3.8 us  [per_device(): outputs = (out[:256] + lax.ppermute(out[256:], 'c', SWAP)).astype(BF)]
    ppermute x1, waiting for transfers between devices: 3.38 us -> 0.01 us  [per_device(): state = lax.ppermute(state, PLANE, [(b, a) for a, b, _ in home])]
    pallas_call x7 -> x9, Pallas kernels: 6.46 us -> 9.8 us  [the longest x7 9.77 us: gradient_rows(): call(kernel, shaped((size, 256), dtype), (), specs)]
    ppermute x3, starting transfers between devices: 6.82 us -> 3.68 us  [per_device(): lax.ppermute(pieces[step - 1], PLANE, line_pairs(False, step))]
    ppermute x12, starting transfers between devices: 22.7 us -> 19.8 us  [pass_on(): return lax.ppermute(rows, PLANE, line_pairs(True, step))]
    ppermute x12, waiting for transfers between devices: 18.2 us -> 20.9 us  [pass_on(): return lax.ppermute(rows, PLANE, line_pairs(True, step))]
  transfers between devices with their start and end apart: 28 -> 28, of which waited for: 14 -> 15; matrix products, arithmetic and copies ran while one was open for 9% -> 11% of each run, Pallas kernels for 9% -> 11%
where the time goes in v3:
time: 148 us
  waiting for transfers between devices  52.7 us (36%)
  starting transfers between devices  42.1 us (28%)
  Pallas kernels  19.9 us (13%)
  local copies, waits for them, and re-layouts  17.8 us (12%)
  blocking collectives  13.2 us (9%)
    ppermute x12, waiting for transfers between devices, pass_on(): return lax.ppermute(rows, PLANE, line_pairs(True, step))  20.9 us
    ppermute x12, starting transfers between devices, pass_on(): return lax.ppermute(rows, PLANE, line_pairs(True, step))  19.8 us
    dynamic_slice x3, local copies, waits for them, and re-layouts, taken(): lax.dynamic_slice(tokens, (0, after(place, *behind) * 2304), (256, 2304))  13.6 us
    all_to_all x1, blocking collectives, per_device(): slab = lax.all_to_all(copies, 'z', 0, 0, tiled=True)  13.2 us
    ppermute x3, waiting for transfers between devices, per_device(): lax.ppermute(slab, PLANE, line_pairs(False, step))  11.6 us
    pallas_call x7, Pallas kernels, gradient_rows(): call(kernel, shaped((size, 256), dtype), (), specs)  9.77 us
    ppermute x3, waiting for transfers between devices, per_device(): lax.ppermute(pieces[step - 1], PLANE, line_pairs(False, step))  8.45 us
    all_to_all x1, starting transfers between devices, per_device(): grad = lax.all_to_all(grad, 'z', 0, 0, tiled=True)  7.86 us
  transfers between devices with their start and end apart: 28, of which 15 were waited for; matrix products, arithmetic and copies ran while one was open for 11% of the time, Pallas kernels for 11%

profile of v3, /device:TPU:24, one launch (start us, length us, event | category | flops | bytes accessed | tf_op | source)
XLA Modules:
  0.0 147.7 jit_solution(15261689839614918604)
XLA Ops:
  0.6 0.1 collective-permute-start.2
  0.8 2.4 %constant_dynamic-slice_fusion.11 = bf16[256,2304]{1,0:T(8,128)(2,1)} fusion(bf16[256,18432]{1,0:T(8,128)(2,1)} %param.6, s32[]{:T(128)S(6)} %select_n.112), kind=kLoop, calls=%fused_computation.19 | loop fusion | bytes 2359300 | tf_op jit(solution)/shard_map/dynamic_slice | solution.py:233
  3.1 0.5 collective-permute-start.4
  3.6 6.7 %constant_dynamic-slice_fusion.4 = (bf16[256,2304]{1,0:T(8,128)(2,1)}, bf16[256,2304]{1,0:T(8,128)(2,1)}, bf16[256,2304]{1,0:T(8,128)(2,1)}, bf16[256,2304]{1,0:...) fusion(bf16[256,18432]{1,0:T(8,128)(2,1)} %param.6, ...), kind=kLoop, calls=%fused_computation.12 | loop fusion | bytes 16515100 | tf_op jit(solution)/shard_map/dynamic_slice | solution.py:233
  10.4 0.5 collective-permute-start.7
  10.9 1.3 copy-done.1
  12.1 1.4 shard_map.102
  13.5 1.5 %collective-permute-start.5 = (bf16[1152,256]{1,0:T(8,128)(2,1)}, bf16[1152,256]{1,0:T(8,128)(2,1)}, u32[]{:S(2)}, u32[]{:S(2)}) collective-permute-start(bf16[1152,256]{1,0:T(8,128)(2,1)} %shard_map.102), channel_id=1, source_target_pairs={{0,128},{8,136},{16,144},{24,152},{64,72},{72,80},{80,88},{88,64},... | collective-permute-start | bytes 1769480 | tf_op jit(solution)/shard_map/ppermute | solution.py:245
  15.0 0.5 shard_map.106
  15.5 1.8 %collective-permute-start.10 = (bf16[1152,256]{1,0:T(8,128)(2,1)S(1)}, bf16[1152,256]{1,0:T(8,128)(2,1)}, u32[]{:S(2)}, u32[]{:S(2)}) collective-permute-start(bf16[1152,256]{1,0:T(8,128)(2,1)S(1)} %shard_map.106), channel_id=1, source_target_pairs={{0,160},{8,168},{16,176},{24,184},{64,88},{72,64},{80,72},{88,80},... | collective-permute-start | bytes 1769480 | tf_op jit(solution)/shard_map/ppermute | solution.py:245
  17.4 0.1 copy.11
  17.6 0.8 dynamic-slice_bitcast_fusion
  18.4 2.3 %collective-permute-start = (bf16[4,72,256]{2,1,0:T(8,128)(2,1)S(1)}, bf16[4,72,256]{2,1,0:T(8,128)(2,1)S(1)}, u32[]{:S(2)}, u32[]{:S(2)}) collective-permute-start(bf16[4,72,256]{2,1,0:T(8,128)(2,1)S(1)} %pad_maximum_fusion), channel_id=1, source_target_pairs={{192,0},{128,8},{0,16},{64,24},{8,128},{72,136},{200,144},{136,152... | collective-permute-start | bytes 442376 | tf_op jit(solution)/shard_map/ppermute | solution.py:263
  20.7 1.3 copy-done.3
  22.0 0.5 shard_map.105
  22.5 0.4 collective-permute-start.9
  23.0 1.8 %shard_map.104 = bf16[1152,256]{1,0:T(8,128)(2,1)S(1)} custom-call(bf16[256,2304]{1,0:T(8,128)(2,1)S(1)} %copy-done.2, bf16[256,2304]{1,0:T(8,128)(2,1)} %collective-permute-done.7.other_ref, bf16[256,256]{1,0:T(8,128)(2,1)S(1)} %copy-done.4, bf16[256,256]{1,0:T(8,128)(2,1)S(1)} %collective-permute-done.2.cot_other_ref), custom_call_target="tpu_custom_call" | custom-call | flops 1000 | bytes 1000 | tf_op jit(solution)/shard_map/pallas_call | solution.py:100
  24.7 1.7 %collective-permute-done.5.refs_0_ = bf16[1152,256]{1,0:T(8,128)(2,1)} collective-permute-done((bf16[1152,256]{1,0:T(8,128)(2,1)}, bf16[1152,256]{1,0:T(8,128)(2,1)}, u32[]{:S(2)}, u32[]{:S(2)}) %collective-permute-start.5) | collective-permute-done | bytes 589856 | tf_op jit(solution)/shard_map/ppermute | solution.py:245
  26.5 1.2 collective-permute-start.8
  27.7 1.6 %shard_map.103 = bf16[1152,256]{1,0:T(8,128)(2,1)S(1)} custom-call(bf16[256,2304]{1,0:T(8,128)(2,1)S(1)} %copy-done.3, bf16[256,2304]{1,0:T(8,128)(2,1)S(1)} %collective-permute-done.3.other_ref, bf16[256,256]{1,0:T(8,128)(2,1)S(1)} %copy-done.4, bf16[256,256]{1,0:T(8,128)(2,1)S(1)} %collective-permute-done.2.cot_other_ref, ...), custom_call_target="tpu_custom_call" | custom-call | flops 1000 | bytes 1000 | tf_op jit(solution)/shard_map/pallas_call | solution.py:100
  29.3 0.2 collective-permute-done.10.refs_0_
  29.5 0.7 collective-permute-start.6
  30.2 1.9 %shard_map.107 = bf16[1152,256]{1,0:T(8,128)(2,1)S(1)} custom-call(bf16[256,2304]{1,0:T(8,128)(2,1)S(1)} %copy-done.2, bf16[256,2304]{1,0:T(8,128)(2,1)} %collective-permute-done.7.other_ref, bf16[256,256]{1,0:T(8,128)(2,1)S(1)} %copy-done.4, bf16[256,256]{1,0:T(8,128)(2,1)S(1)} %collective-permute-done.2.cot_other_ref, ...), custom_call_target="tpu_custom_call" | custom-call | flops 1000 | bytes 1000 | tf_op jit(solution)/shard_map/pallas_call | solution.py:100
  32.2 3.3 %collective-permute-start.11 = (bf16[1152,256]{1,0:T(8,128)(2,1)S(1)}, bf16[1152,256]{1,0:T(8,128)(2,1)S(1)}, u32[]{:S(2)}, u32[]{:S(2)}) collective-permute-start(bf16[1152,256]{1,0:T(8,128)(2,1)S(1)} %shard_map.107), channel_id=1, source_target_pairs={{0,160},{8,168},{16,176},{24,184},{64,88},{72,64},{80,72},{88,80},... | collective-permute-start | bytes 1769480 | tf_op jit(solution)/shard_map/ppermute | solution.py:245
  35.5 2.1 %shard_map.101.total_ref = f32[2304,256]{1,0:T(8,128)S(1)} custom-call(bf16[256,2304]{1,0:T(8,128)(2,1)S(1)} %copy-done.9, bf16[256,2304]{1,0:T(8,128)(2,1)} %collective-permute-done.1.other_ref, bf16[256,256]{1,0:T(8,128)(2,1)S(1)} %copy-done.4, bf16[256,256]{1,0:T(8,128)(2,1)S(1)} %collective-permute-done.2.cot_other_ref, ...), custom_call_target="tpu_custom_call" | custom-call | flops 1000 | bytes 1000 | tf_op jit(solution)/shard_map/pallas_call | solution.py:100
  37.6 3.5 %collective-permute-done.6.a_ref = bf16[1152,256]{1,0:T(8,128)(2,1)S(1)} collective-permute-done((bf16[1152,256]{1,0:T(8,128)(2,1)S(1)}, bf16[1152,256]{1,0:T(8,128)(2,1)S(1)}, u32[]{:S(2)}, u32[]{:S(2)}) %collective-permute-start.6) | collective-permute-done | bytes 589856 | tf_op jit(solution)/shard_map/ppermute | solution.py:245
  41.1 2.6 %collective-permute-done.11.e_ref = bf16[1152,256]{1,0:T(8,128)(2,1)S(1)} collective-permute-done((bf16[1152,256]{1,0:T(8,128)(2,1)S(1)}, bf16[1152,256]{1,0:T(8,128)(2,1)S(1)}, u32[]{:S(2)}, u32[]{:S(2)}) %collective-permute-start.11) | collective-permute-done | bytes 589856 | tf_op jit(solution)/shard_map/ppermute | solution.py:245
  43.7 0.5 shard_map.108
  44.2 1.0 collective-permute-start.12
  45.3 1.1 collective-permute-start.13
  46.4 1.6 %collective-permute-start.14 = (bf16[8,72,256]{2,1,0:T(8,128)(2,1)S(1)}, bf16[8,72,256]{2,1,0:T(8,128)(2,1)S(1)}, u32[]{:S(2)}, u32[]{:S(2)}) collective-permute-start(bf16[8,72,256]{2,1,0:T(8,128)(2,1)S(1)} %get-tuple-element.62), channel_id=1, source_target_pairs={{0,16},{8,24},{16,0},{24,8},{64,96},{72,104},{80,112},{88,120},{12... | collective-permute-start | bytes 884744 | tf_op jit(solution)/shard_map/ppermute | solution.py:277
  47.9 3.1 %collective-permute-done.12.a_ref = bf16[8,72,256]{2,1,0:T(8,128)(2,1)S(1)} collective-permute-done((bf16[8,72,256]{2,1,0:T(8,128)(2,1)S(1)}, bf16[8,72,256]{2,1,0:T(8,128)(2,1)S(1)}, u32[]{:S(2)}, u32[]{:S(2)}) %collective-permute-start.12) | collective-permute-done | bytes 294944 | tf_op jit(solution)/shard_map/ppermute | solution.py:277
  51.1 5.3 %collective-permute-done.13.b_ref = bf16[8,72,256]{2,1,0:T(8,128)(2,1)S(1)} collective-permute-done((bf16[8,72,256]{2,1,0:T(8,128)(2,1)S(1)}, bf16[8,72,256]{2,1,0:T(8,128)(2,1)S(1)}, u32[]{:S(2)}, u32[]{:S(2)}) %collective-permute-start.13) | collective-permute-done | bytes 294944 | tf_op jit(solution)/shard_map/ppermute | solution.py:277
  56.4 0.8 shard_map.109
  57.2 7.9 %all-to-all-start = ((bf16[8,72,256]{2,1,0:T(8,128)(2,1)}), bf16[8,72,256]{2,1,0:T(8,128)(2,1)S(1)}, u32[]{:S(2)}, u32[]{:S(2)}) async-start(bf16[8,72,256]{2,1,0:T(8,128)(2,1)} %shard_map.109), calls=%async_computation | async-start | bytes 589824 | tf_op jit(solution)/shard_map/all_to_all | solution.py:280
  65.1 0.2 convert_multiply_fusion.table_ref
  65.3 4.5 %constant_dynamic-slice_fusion = (bf16[256,2304]{1,0:T(8,128)(2,1)}, bf16[256,2304]{1,0:T(8,128)(2,1)}, bf16[256,2304]{1,0:T(8,128)(2,1)}, bf16[256,2304]{1,0:T(8,128)(2,1)}) fusion(bf16[256,18432]{1,0:T(8,128)(2,1)} %param.6, s32[]{:T(128)S(6)} %select_n.132, s32[]{:T(128)S(6)} %select_n.130, s32[]{:T(128)S(6)} %select_n.129, s32[]{:T(128)S(6)} %select_n.131), kind=kLoop, calls=%fused_computation.8 | loop fusion | bytes 9437200 | tf_op jit(solution)/shard_map/dynamic_slice | solution.py:233
  69.9 6.1 %all-to-all-done.terms_ref = bf16[8,72,256]{2,1,0:T(8,128)(2,1)S(1)} async-done(((bf16[8,72,256]{2,1,0:T(8,128)(2,1)}), bf16[8,72,256]{2,1,0:T(8,128)(2,1)S(1)}, u32[]{:S(2)}, u32[]{:S(2)}) %all-to-all-start) | async-done | bytes 294944 | tf_op jit(solution)/shard_map/all_to_all | solution.py:280
  75.9 0.7 shard_map.110
  76.7 13.2 %all_to_all.10.slab_ref = bf16[8,72,256]{2,1,0:T(8,128)(2,1)S(1)} all-to-all(bf16[8,72,256]{2,1,0:T(8,128)(2,1)S(1)} %get-tuple-element.69), channel_id=1, replica_groups=mesh['xl'=2,'c'=2,'xh'=2,'y'=4,'z'=8] {'z'}, dimensions={0} | all-to-all | bytes 589824 | tf_op jit(solution)/shard_map/all_to_all | solution.py:284
  89.9 1.2 collective-permute-start.17
  91.1 1.2 collective-permute-start.16
  92.3 1.0 collective-permute-start.15
  93.3 4.5 %collective-permute-done.17.refs_0_.e_ref = bf16[11,72,256]{2,1,0:T(8,128)(2,1)S(1)} collective-permute-done((bf16[11,72,256]{2,1,0:T(8,128)(2,1)S(1)}, bf16[11,72,256]{2,1,0:T(8,128)(2,1)S(1)}, u32[]{:S(2)}, u32[]{:S(2)}) %collective-permute-start.17) | collective-permute-done | bytes 405536 | tf_op jit(solution)/shard_map/ppermute | solution.py:286
  97.9 2.8 %collective-permute-done.16.refs_2_.d_ref = bf16[11,72,256]{2,1,0:T(8,128)(2,1)} collective-permute-done((bf16[11,72,256]{2,1,0:T(8,128)(2,1)S(1)}, bf16[11,72,256]{2,1,0:T(8,128)(2,1)}, u32[]{:S(2)}, u32[]{:S(2)}) %collective-permute-start.16) | collective-permute-done | bytes 405536 | tf_op jit(solution)/shard_map/ppermute | solution.py:286
  100.7 4.2 %collective-permute-done.15.refs_1_.b_ref = bf16[11,72,256]{2,1,0:T(8,128)(2,1)} collective-permute-done((bf16[11,72,256]{2,1,0:T(8,128)(2,1)S(1)}, bf16[11,72,256]{2,1,0:T(8,128)(2,1)}, u32[]{:S(2)}, u32[]{:S(2)}) %collective-permute-start.15) | collective-permute-done | bytes 405536 | tf_op jit(solution)/shard_map/ppermute | solution.py:286
  105.0 1.1 collective-permute-done.18.ready_ref
  106.1 1.3 shard_map.113
  107.3 3.8 %collective-permute-start.21 = (bf16[1152,256]{1,0:T(8,128)(2,1)S(1)}, bf16[1152,256]{1,0:T(8,128)(2,1)S(1)}, u32[]{:S(2)}, u32[]{:S(2)}) collective-permute-start(bf16[1152,256]{1,0:T(8,128)(2,1)S(1)} %bitcast.18), channel_id=1, source_target_pairs={{0,160},{8,168},{16,176},{24,184},{64,88},{72,64},{80,72},{88,80},... | collective-permute-start | bytes 1769480 | tf_op jit(solution)/shard_map/ppermute | solution.py:245
  111.1 3.3 %collective-permute-start.23 = (bf16[1152,256]{1,0:T(8,128)(2,1)S(1)}, bf16[1152,256]{1,0:T(8,128)(2,1)S(1)}, u32[]{:S(2)}, u32[]{:S(2)}) collective-permute-start(bf16[1152,256]{1,0:T(8,128)(2,1)S(1)} %bitcast.16), channel_id=1, source_target_pairs={{0,160},{8,168},{16,176},{24,184},{64,88},{72,64},{80,72},{88,80},... | collective-permute-start | bytes 1769480 | tf_op jit(solution)/shard_map/ppermute | solution.py:245
  114.4 4.1 %collective-permute-done.21.lower_ref = bf16[1152,256]{1,0:T(8,128)(2,1)S(1)} collective-permute-done((bf16[1152,256]{1,0:T(8,128)(2,1)S(1)}, bf16[1152,256]{1,0:T(8,128)(2,1)S(1)}, u32[]{:S(2)}, u32[]{:S(2)}) %collective-permute-start.21) | collective-permute-done | bytes 589856 | tf_op jit(solution)/shard_map/ppermute | solution.py:245
  118.5 3.7 %collective-permute-start.22 = (bf16[1152,256]{1,0:T(8,128)(2,1)S(1)}, bf16[1152,256]{1,0:T(8,128)(2,1)S(1)}, u32[]{:S(2)}, u32[]{:S(2)}) collective-permute-start(bf16[1152,256]{1,0:T(8,128)(2,1)S(1)} %collective-permute-done.21.lower_ref), channel_id=1, source_target_pairs={{0,160},{8,168},{16,176},{24,184},{64,88},{72,64},{80,72},{88,80},... | collective-permute-start | bytes 1769480 | tf_op jit(solution)/shard_map/ppermute | solution.py:245
  122.2 0.1 collective-permute-start.26
  122.3 2.2 %shard_map.114.refs_0_ = f32[512,256]{1,0:T(8,128)S(1)} custom-call(bf16[256,2304]{1,0:T(8,128)(2,1)S(1)} %copy-done.8, bf16[256,2304]{1,0:T(8,128)(2,1)} %collective-permute-done.1.other_ref, bf16[1152,256]{1,0:T(8,128)(2,1)S(1)} %bitcast.17, bf16[1152,256]{1,0:T(8,128)(2,1)S(1)} %bitcast.20), custom_call_target="tpu_custom_call" | custom-call | flops 1000 | bytes 1000 | tf_op jit(solution)/shard_map/pallas_call | solution.py:219
  124.5 4.0 %collective-permute-done.24.lower_ref = bf16[1152,256]{1,0:T(8,128)(2,1)S(1)} collective-permute-done((bf16[1152,256]{1,0:T(8,128)(2,1)S(1)}, bf16[1152,256]{1,0:T(8,128)(2,1)S(1)}, u32[]{:S(2)}, u32[]{:S(2)}) %collective-permute-start.24) | collective-permute-done | bytes 589856 | tf_op jit(solution)/shard_map/ppermute | solution.py:245
  128.5 2.1 %shard_map.115.refs_0_ = f32[512,256]{1,0:T(8,128)S(1)} custom-call(bf16[256,2304]{1,0:T(8,128)(2,1)S(1)} %copy-done.7, bf16[256,2304]{1,0:T(8,128)(2,1)} %collective-permute-done.7.other_ref, bf16[1152,256]{1,0:T(8,128)(2,1)S(1)} %collective-permute-done.19.upper_ref, bf16[1152,256]{1,0:T(8,128)(2,1)S(1)} %collective-permute-done.24.lower_ref, ...), custom_call_target="tpu_custom_call" | custom-call | flops 1000 | bytes 1000 | tf_op jit(solution)/shard_map/pallas_call | solution.py:219
  130.7 0.8 shard_map.116.refs_0_
  131.5 4.8 %collective-permute-done.22.lower_ref = bf16[1152,256]{1,0:T(8,128)(2,1)S(1)} collective-permute-done((bf16[1152,256]{1,0:T(8,128)(2,1)S(1)}, bf16[1152,256]{1,0:T(8,128)(2,1)S(1)}, u32[]{:S(2)}, u32[]{:S(2)}) %collective-permute-start.22) | collective-permute-done | bytes 589856 | tf_op jit(solution)/shard_map/ppermute | solution.py:245
  136.3 0.8 shard_map.117
  137.2 3.8 %collective-permute-start.25 = (f32[256,256]{1,0:T(8,128)S(1)}, f32[256,256]{1,0:T(8,128)S(1)}, u32[]{:S(2)}, u32[]{:S(2)}) collective-permute-start(f32[256,256]{1,0:T(8,128)S(1)} %slice.9), channel_id=1, source_target_pairs={{0,64},{64,0},{1,65},{65,1},{2,66},{66,2},{3,67},{67,3},{4,68},{68... | collective-permute-start | bytes 786440 | tf_op jit(solution)/shard_map/ppermute | solution.py:300
  141.0 4.6 %collective-permute-done.26.home_ref = bf16[13,72,256]{2,1,0:T(8,128)(2,1)S(1)} collective-permute-done((bf16[13,72,256]{2,1,0:T(8,128)(2,1)S(1)}, bf16[13,72,256]{2,1,0:T(8,128)(2,1)S(1)}, u32[]{:S(2)}, u32[]{:S(2)}) %collective-permute-start.26) | collective-permute-done | bytes 479264 | tf_op jit(solution)/shard_map/ppermute | solution.py:294
  145.5 0.8 shard_map.118
  146.3 0.7 copy.12
  147.0 0.7 fusion
  (50 shorter events, 0.5 us)
Async XLA Ops:
  0.6 16.9 %copy-start = (bf16[288,256]{1,0:T(8,128)(2,1)S(1)}, bf16[288,256]{1,0:T(8,128)(2,1)}, u32[]{:S(2)}) copy-start(bf16[288,256]{1,0:T(8,128)(2,1)} %param.8) | copy-start | bytes 442372
  0.6 2.5 %collective-permute-start.2 = (bf16[256,256]{1,0:T(8,128)(2,1)}, bf16[256,256]{1,0:T(8,128)(2,1)S(1)}, u32[]{:S(2)}, u32[]{:S(2)}) collective-permute-start(bf16[256,256]{1,0:T(8,128)(2,1)} %cot_own_ref.13), channel_id=1, source_target_pairs={{0,64},{64,0},{1,65},{65,1},{2,66},{66,2},{3,67},{67,3},{4,68},{68... | collective-permute-start | bytes 393224 | tf_op jit(solution)/shard_map/ppermute | solution.py:242
  3.1 7.7 %copy-start.4 = (bf16[256,256]{1,0:T(8,128)(2,1)S(1)}, bf16[256,256]{1,0:T(8,128)(2,1)}, u32[]{:S(2)}) copy-start(bf16[256,256]{1,0:T(8,128)(2,1)} %cot_own_ref.13) | copy-start | bytes 393220
  3.1 7.7 %collective-permute-start.4 = (bf16[256,2304]{1,0:T(8,128)(2,1)}, bf16[256,2304]{1,0:T(8,128)(2,1)S(1)}, u32[]{:S(2)}, u32[]{:S(2)}) collective-permute-start(bf16[256,2304]{1,0:T(8,128)(2,1)} %constant_dynamic-slice_fusion.11), channel_id=1, source_target_pairs={{0,64},{64,0},{1,65},{65,1},{2,66},{66,2},{3,67},{67,3},{4,68},{68... | collective-permute-start | bytes 3538952 | tf_op jit(solution)/shard_map/ppermute | solution.py:242
  10.3 8.1 %collective-permute-start.3 = (bf16[256,2304]{1,0:T(8,128)(2,1)}, bf16[256,2304]{1,0:T(8,128)(2,1)S(1)}, u32[]{:S(2)}, u32[]{:S(2)}) collective-permute-start(bf16[256,2304]{1,0:T(8,128)(2,1)} %get-tuple-element.54), channel_id=1, source_target_pairs={{0,64},{64,0},{1,65},{65,1},{2,66},{66,2},{3,67},{67,3},{4,68},{68... | collective-permute-start | bytes 3538952 | tf_op jit(solution)/shard_map/ppermute | solution.py:242
  10.4 12.1 %collective-permute-start.7 = (bf16[256,2304]{1,0:T(8,128)(2,1)}, bf16[256,2304]{1,0:T(8,128)(2,1)}, u32[]{:S(2)}, u32[]{:S(2)}) collective-permute-start(bf16[256,2304]{1,0:T(8,128)(2,1)} %get-tuple-element.58), channel_id=1, source_target_pairs={{0,64},{64,0},{1,65},{65,1},{2,66},{66,2},{3,67},{67,3},{4,68},{68... | collective-permute-start | bytes 3538952 | tf_op jit(solution)/shard_map/ppermute | solution.py:242
  10.8 24.7 %collective-permute-start.1 = (bf16[256,2304]{1,0:T(8,128)(2,1)}, bf16[256,2304]{1,0:T(8,128)(2,1)}, u32[]{:S(2)}, u32[]{:S(2)}) collective-permute-start(bf16[256,2304]{1,0:T(8,128)(2,1)} %get-tuple-element.52), channel_id=1, source_target_pairs={{0,64},{64,0},{1,65},{65,1},{2,66},{66,2},{3,67},{67,3},{4,68},{68... | collective-permute-start | bytes 3538952 | tf_op jit(solution)/shard_map/ppermute | solution.py:242
  10.9 1.3 copy-start.1
  13.5 3.8 %copy-start.10 = (bf16[288,2]{0,1:T(2,128)(2,1)S(1)}, bf16[288,2]{0,1:T(2,128)(2,1)}, u32[]{:S(2)}) copy-start(bf16[288,2]{0,1:T(2,128)(2,1)} %param.10) | copy-start | bytes 3460
  13.5 13.0 %collective-permute-start.5 = (bf16[1152,256]{1,0:T(8,128)(2,1)}, bf16[1152,256]{1,0:T(8,128)(2,1)}, u32[]{:S(2)}, u32[]{:S(2)}) collective-permute-start(bf16[1152,256]{1,0:T(8,128)(2,1)} %shard_map.102), channel_id=1, source_target_pairs={{0,128},{8,136},{16,144},{24,152},{64,72},{72,80},{80,88},{88,64},... | collective-permute-start | bytes 1769480 | tf_op jit(solution)/shard_map/ppermute | solution.py:245
  15.5 14.0 %collective-permute-start.10 = (bf16[1152,256]{1,0:T(8,128)(2,1)S(1)}, bf16[1152,256]{1,0:T(8,128)(2,1)}, u32[]{:S(2)}, u32[]{:S(2)}) collective-permute-start(bf16[1152,256]{1,0:T(8,128)(2,1)S(1)} %shard_map.106), channel_id=1, source_target_pairs={{0,160},{8,168},{16,176},{24,184},{64,88},{72,64},{80,72},{88,80},... | collective-permute-start | bytes 1769480 | tf_op jit(solution)/shard_map/ppermute | solution.py:245
  18.4 4.6 %copy-start.2 = (bf16[256,2304]{1,0:T(8,128)(2,1)S(1)}, bf16[256,2304]{1,0:T(8,128)(2,1)}, u32[]{:S(2)}) copy-start(bf16[256,2304]{1,0:T(8,128)(2,1)} %get-tuple-element.57.own_ref) | copy-start | bytes 3538948
  18.4 13.8 %collective-permute-start = (bf16[4,72,256]{2,1,0:T(8,128)(2,1)S(1)}, bf16[4,72,256]{2,1,0:T(8,128)(2,1)S(1)}, u32[]{:S(2)}, u32[]{:S(2)}) collective-permute-start(bf16[4,72,256]{2,1,0:T(8,128)(2,1)S(1)} %pad_maximum_fusion), channel_id=1, source_target_pairs={{192,0},{128,8},{0,16},{64,24},{8,128},{72,136},{200,144},{136,152... | collective-permute-start | bytes 442376 | tf_op jit(solution)/shard_map/ppermute | solution.py:263
  20.7 1.3 copy-start.3
  22.5 15.1 %collective-permute-start.9 = (bf16[1152,256]{1,0:T(8,128)(2,1)S(1)}, bf16[1152,256]{1,0:T(8,128)(2,1)S(1)}, u32[]{:S(2)}, u32[]{:S(2)}) collective-permute-start(bf16[1152,256]{1,0:T(8,128)(2,1)S(1)} %shard_map.105), channel_id=1, source_target_pairs={{0,128},{8,136},{16,144},{24,152},{64,72},{72,80},{80,88},{88,64},... | collective-permute-start | bytes 1769480 | tf_op jit(solution)/shard_map/ppermute | solution.py:245
  26.5 11.1 %collective-permute-start.8 = (bf16[1152,256]{1,0:T(8,128)(2,1)S(1)}, bf16[1152,256]{1,0:T(8,128)(2,1)S(1)}, u32[]{:S(2)}, u32[]{:S(2)}) collective-permute-start(bf16[1152,256]{1,0:T(8,128)(2,1)S(1)} %shard_map.104), channel_id=1, source_target_pairs={{0,160},{8,168},{16,176},{24,184},{64,88},{72,64},{80,72},{88,80},... | collective-permute-start | bytes 1769480 | tf_op jit(solution)/shard_map/ppermute | solution.py:245
  29.3 6.2 %copy-start.9 = (bf16[256,2304]{1,0:T(8,128)(2,1)S(1)}, bf16[256,2304]{1,0:T(8,128)(2,1)}, u32[]{:S(2)}) copy-start(bf16[256,2304]{1,0:T(8,128)(2,1)} %get-tuple-element.51.own_ref) | copy-start | bytes 3538948
  29.5 11.7 %collective-permute-start.6 = (bf16[1152,256]{1,0:T(8,128)(2,1)S(1)}, bf16[1152,256]{1,0:T(8,128)(2,1)S(1)}, u32[]{:S(2)}, u32[]{:S(2)}) collective-permute-start(bf16[1152,256]{1,0:T(8,128)(2,1)S(1)} %shard_map.103), channel_id=1, source_target_pairs={{0,128},{8,136},{16,144},{24,152},{64,72},{72,80},{80,88},{88,64},... | collective-permute-start | bytes 1769480 | tf_op jit(solution)/shard_map/ppermute | solution.py:245
  32.2 11.5 %collective-permute-start.11 = (bf16[1152,256]{1,0:T(8,128)(2,1)S(1)}, bf16[1152,256]{1,0:T(8,128)(2,1)S(1)}, u32[]{:S(2)}, u32[]{:S(2)}) collective-permute-start(bf16[1152,256]{1,0:T(8,128)(2,1)S(1)} %shard_map.107), channel_id=1, source_target_pairs={{0,160},{8,168},{16,176},{24,184},{64,88},{72,64},{80,72},{88,80},... | collective-permute-start | bytes 1769480 | tf_op jit(solution)/shard_map/ppermute | solution.py:245
  44.2 6.8 %collective-permute-start.12 = (bf16[8,72,256]{2,1,0:T(8,128)(2,1)S(1)}, bf16[8,72,256]{2,1,0:T(8,128)(2,1)S(1)}, u32[]{:S(2)}, u32[]{:S(2)}) collective-permute-start(bf16[8,72,256]{2,1,0:T(8,128)(2,1)S(1)} %get-tuple-element.60), channel_id=1, source_target_pairs={{0,8},{8,16},{16,24},{24,0},{64,192},{72,200},{80,208},{88,216},{1... | collective-permute-start | bytes 884744 | tf_op jit(solution)/shard_map/ppermute | solution.py:277
  45.3 11.1 %collective-permute-start.13 = (bf16[8,72,256]{2,1,0:T(8,128)(2,1)S(1)}, bf16[8,72,256]{2,1,0:T(8,128)(2,1)S(1)}, u32[]{:S(2)}, u32[]{:S(2)}) collective-permute-start(bf16[8,72,256]{2,1,0:T(8,128)(2,1)S(1)} %get-tuple-element.61), channel_id=1, source_target_pairs={{0,24},{8,0},{16,8},{24,16},{64,224},{72,232},{80,240},{88,248},{1... | collective-permute-start | bytes 884744 | tf_op jit(solution)/shard_map/ppermute | solution.py:277
  46.4 10.0 %collective-permute-start.14 = (bf16[8,72,256]{2,1,0:T(8,128)(2,1)S(1)}, bf16[8,72,256]{2,1,0:T(8,128)(2,1)S(1)}, u32[]{:S(2)}, u32[]{:S(2)}) collective-permute-start(bf16[8,72,256]{2,1,0:T(8,128)(2,1)S(1)} %get-tuple-element.62), channel_id=1, source_target_pairs={{0,16},{8,24},{16,0},{24,8},{64,96},{72,104},{80,112},{88,120},{12... | collective-permute-start | bytes 884744 | tf_op jit(solution)/shard_map/ppermute | solution.py:277
  57.2 18.7 %all-to-all-start = ((bf16[8,72,256]{2,1,0:T(8,128)(2,1)}), bf16[8,72,256]{2,1,0:T(8,128)(2,1)S(1)}, u32[]{:S(2)}, u32[]{:S(2)}) async-start(bf16[8,72,256]{2,1,0:T(8,128)(2,1)} %shard_map.109), calls=%async_computation | async-start | bytes 589824 | tf_op jit(solution)/shard_map/all_to_all | solution.py:280
  89.9 8.0 %collective-permute-start.17 = (bf16[11,72,256]{2,1,0:T(8,128)(2,1)S(1)}, bf16[11,72,256]{2,1,0:T(8,128)(2,1)S(1)}, u32[]{:S(2)}, u32[]{:S(2)}) collective-permute-start(bf16[11,72,256]{2,1,0:T(8,128)(2,1)S(1)} %shard_map.111.a_ref), channel_id=1, source_target_pairs={{0,8},{8,16},{16,24},{24,0},{64,192},{72,200},{80,208},{88,216},{1... | collective-permute-start | bytes 1216520 | tf_op jit(solution)/shard_map/ppermute | solution.py:286
  91.1 9.6 %collective-permute-start.16 = (bf16[11,72,256]{2,1,0:T(8,128)(2,1)S(1)}, bf16[11,72,256]{2,1,0:T(8,128)(2,1)}, u32[]{:S(2)}, u32[]{:S(2)}) collective-permute-start(bf16[11,72,256]{2,1,0:T(8,128)(2,1)S(1)} %shard_map.111.a_ref), channel_id=1, source_target_pairs={{0,16},{8,24},{16,0},{24,8},{64,96},{72,104},{80,112},{88,120},{12... | collective-permute-start | bytes 1216520 | tf_op jit(solution)/shard_map/ppermute | solution.py:286
  92.3 12.6 %collective-permute-start.15 = (bf16[11,72,256]{2,1,0:T(8,128)(2,1)S(1)}, bf16[11,72,256]{2,1,0:T(8,128)(2,1)}, u32[]{:S(2)}, u32[]{:S(2)}) collective-permute-start(bf16[11,72,256]{2,1,0:T(8,128)(2,1)S(1)} %shard_map.111.a_ref), channel_id=1, source_target_pairs={{0,24},{8,0},{16,8},{24,16},{64,224},{72,232},{80,240},{88,248},{1... | collective-permute-start | bytes 1216520 | tf_op jit(solution)/shard_map/ppermute | solution.py:286
  93.3 29.0 %copy-start.8 = (bf16[256,2304]{1,0:T(8,128)(2,1)S(1)}, bf16[256,2304]{1,0:T(8,128)(2,1)}, u32[]{:S(2)}) copy-start(bf16[256,2304]{1,0:T(8,128)(2,1)} %get-tuple-element.75.own_ref) | copy-start | bytes 3538948
  104.9 1.2 collective-permute-start.18
  107.3 11.2 %collective-permute-start.21 = (bf16[1152,256]{1,0:T(8,128)(2,1)S(1)}, bf16[1152,256]{1,0:T(8,128)(2,1)S(1)}, u32[]{:S(2)}, u32[]{:S(2)}) collective-permute-start(bf16[1152,256]{1,0:T(8,128)(2,1)S(1)} %bitcast.18), channel_id=1, source_target_pairs={{0,160},{8,168},{16,176},{24,184},{64,88},{72,64},{80,72},{88,80},... | collective-permute-start | bytes 1769480 | tf_op jit(solution)/shard_map/ppermute | solution.py:245
  111.1 11.1 %collective-permute-start.19 = (bf16[1152,256]{1,0:T(8,128)(2,1)S(1)}, bf16[1152,256]{1,0:T(8,128)(2,1)S(1)}, u32[]{:S(2)}, u32[]{:S(2)}) collective-permute-start(bf16[1152,256]{1,0:T(8,128)(2,1)S(1)} %bitcast.15), channel_id=1, source_target_pairs={{0,128},{8,136},{16,144},{24,152},{64,72},{72,80},{80,88},{88,64},... | collective-permute-start | bytes 1769480 | tf_op jit(solution)/shard_map/ppermute | solution.py:245
  111.1 17.4 %collective-permute-start.24 = (bf16[1152,256]{1,0:T(8,128)(2,1)S(1)}, bf16[1152,256]{1,0:T(8,128)(2,1)S(1)}, u32[]{:S(2)}, u32[]{:S(2)}) collective-permute-start(bf16[1152,256]{1,0:T(8,128)(2,1)S(1)} %bitcast.19), channel_id=1, source_target_pairs={{0,128},{8,136},{16,144},{24,152},{64,72},{72,80},{80,88},{88,64},... | collective-permute-start | bytes 1769480 | tf_op jit(solution)/shard_map/ppermute | solution.py:245
  111.1 19.5 %collective-permute-start.23 = (bf16[1152,256]{1,0:T(8,128)(2,1)S(1)}, bf16[1152,256]{1,0:T(8,128)(2,1)S(1)}, u32[]{:S(2)}, u32[]{:S(2)}) collective-permute-start(bf16[1152,256]{1,0:T(8,128)(2,1)S(1)} %bitcast.16), channel_id=1, source_target_pairs={{0,160},{8,168},{16,176},{24,184},{64,88},{72,64},{80,72},{88,80},... | collective-permute-start | bytes 1769480 | tf_op jit(solution)/shard_map/ppermute | solution.py:245
  118.5 17.8 %collective-permute-start.22 = (bf16[1152,256]{1,0:T(8,128)(2,1)S(1)}, bf16[1152,256]{1,0:T(8,128)(2,1)S(1)}, u32[]{:S(2)}, u32[]{:S(2)}) collective-permute-start(bf16[1152,256]{1,0:T(8,128)(2,1)S(1)} %collective-permute-done.21.lower_ref), channel_id=1, source_target_pairs={{0,160},{8,168},{16,176},{24,184},{64,88},{72,64},{80,72},{88,80},... | collective-permute-start | bytes 1769480 | tf_op jit(solution)/shard_map/ppermute | solution.py:245
  122.2 14.1 %collective-permute-start.20 = (bf16[1152,256]{1,0:T(8,128)(2,1)S(1)}, bf16[1152,256]{1,0:T(8,128)(2,1)S(1)}, u32[]{:S(2)}, u32[]{:S(2)}) collective-permute-start(bf16[1152,256]{1,0:T(8,128)(2,1)S(1)} %collective-permute-done.19.upper_ref), channel_id=1, source_target_pairs={{0,128},{8,136},{16,144},{24,152},{64,72},{72,80},{80,88},{88,64},... | collective-permute-start | bytes 1769480 | tf_op jit(solution)/shard_map/ppermute | solution.py:245
  122.2 6.3 %copy-start.7 = (bf16[256,2304]{1,0:T(8,128)(2,1)S(1)}, bf16[256,2304]{1,0:T(8,128)(2,1)}, u32[]{:S(2)}) copy-start(bf16[256,2304]{1,0:T(8,128)(2,1)} %get-tuple-element.74.own_ref) | copy-start | bytes 3538948
  122.2 23.3 %collective-permute-start.26 = (bf16[13,72,256]{2,1,0:T(8,128)(2,1)S(1)}, bf16[13,72,256]{2,1,0:T(8,128)(2,1)S(1)}, u32[]{:S(2)}, u32[]{:S(2)}) collective-permute-start(bf16[13,72,256]{2,1,0:T(8,128)(2,1)S(1)} %get-tuple-element.76), channel_id=1, source_target_pairs={{0,192},{8,128},{16,0},{24,64},{128,8},{136,72},{144,200},{152,136... | collective-permute-start | bytes 1437704 | tf_op jit(solution)/shard_map/ppermute | solution.py:294
  124.5 6.2 %copy-start.6 = (bf16[256,2304]{1,0:T(8,128)(2,1)S(1)}, bf16[256,2304]{1,0:T(8,128)(2,1)}, u32[]{:S(2)}) copy-start(bf16[256,2304]{1,0:T(8,128)(2,1)} %get-tuple-element.73.own_ref) | copy-start | bytes 3538948
  130.7 5.6 %copy-start.5 = (bf16[256,2304]{1,0:T(8,128)(2,1)S(1)}, bf16[256,2304]{1,0:T(8,128)(2,1)}, u32[]{:S(2)}) copy-start(bf16[256,2304]{1,0:T(8,128)(2,1)} %get-tuple-element.67.own_ref) | copy-start | bytes 3538948
  137.2 9.8 %collective-permute-start.25 = (f32[256,256]{1,0:T(8,128)S(1)}, f32[256,256]{1,0:T(8,128)S(1)}, u32[]{:S(2)}, u32[]{:S(2)}) collective-permute-start(f32[256,256]{1,0:T(8,128)S(1)} %slice.9), channel_id=1, source_target_pairs={{0,64},{64,0},{1,65},{65,1},{2,66},{66,2},{3,67},{67,3},{4,68},{68... | collective-permute-start | bytes 786440 | tf_op jit(solution)/shard_map/ppermute | solution.py:300

commit v4 on v3

--- a/solution.py
+++ b/solution.py
@@ -58,12 +58,13 @@
     return signs.astype(F32) / math.sqrt(128.0)
 
 
-def call(kernel, out_shape, scratch=(), in_specs=None):
+def call(kernel, out_shape, scratch=(), in_specs=None, grid=()):
     options = {} if in_specs is None else {"in_specs": in_specs}
     return pl.pallas_call(
         kernel,
         out_shape=out_shape,
         scratch_shapes=scratch,
+        grid=grid,
         compiler_params=pltpu.CompilerParams(vmem_limit_bytes=16 << 20),
         cost_estimate=pl.CostEstimate(flops=1000, bytes_accessed=1000, transcendentals=0),
         **options,
@@ -89,15 +90,16 @@
 
     def kernel(own_ref, other_ref, cot_own_ref, cot_other_ref, *refs):
         for i in range(0, size, 384):
-            part = pl.ds(rows.start + i, 384)
+            part = pl.ds(i, 384)
             term = lax.dot_general(own_ref[:, part], cot_own_ref[...], contract, preferred_element_type=F32)
             term += lax.dot_general(other_ref[:, part], cot_other_ref[...], contract, preferred_element_type=F32)
             for ref in refs[: len(added)]:
                 term += ref[pl.ds(i, 384), :].astype(F32)
             refs[-1][pl.ds(i, 384), :] = term.astype(dtype)
 
-    specs = [VMEM] * (4 + len(added)) + [ANY] * len(behind)
-    return call(kernel, shaped((size, 256), dtype), (), specs)(own, other, cot_own, cot_other, *added, *behind)
+    columns = pl.BlockSpec((256, size), lambda i: (0, rows.start // size))
+    specs = [columns] * 2 + [VMEM] * (2 + len(added)) + [ANY] * len(behind)
+    return call(kernel, shaped((size, 256), dtype), (), specs, (1,))(own, other, cot_own, cot_other, *added, *behind)
 
 
 def sum_and_split(total, upper, lower, q):

time: 148 us -> 148 us (level)
  no operation moved by 1% of the time
where the time goes in v4:
time: 148 us
  waiting for transfers between devices  53 us (36%)
  starting transfers between devices  41.9 us (28%)
  Pallas kernels  19.7 us (13%)
  local copies, waits for them, and re-layouts  17.8 us (12%)
  blocking collectives  13.2 us (9%)
    ppermute x12, waiting for transfers between devices, pass_on(): return lax.ppermute(rows, PLANE, line_pairs(True, step))  21.3 us
    ppermute x12, starting transfers between devices, pass_on(): return lax.ppermute(rows, PLANE, line_pairs(True, step))  19.6 us
    dynamic_slice x3, local copies, waits for them, and re-layouts, taken(): lax.dynamic_slice(tokens, (0, after(place, *behind) * 2304), (256, 2304))  13.6 us
    all_to_all x1, blocking collectives, per_device(): slab = lax.all_to_all(copies, 'z', 0, 0, tiled=True)  13.2 us
    ppermute x3, waiting for transfers between devices, per_device(): lax.ppermute(slab, PLANE, line_pairs(False, step))  11.6 us
    pallas_call x7, Pallas kernels, gradient_rows(): call(kernel, shaped((size, 256), dtype), (), specs, (1,))  9.58 us
    ppermute x3, waiting for transfers between devices, per_device(): lax.ppermute(pieces[step - 1], PLANE, line_pairs(False, step))  8.44 us
    all_to_all x1, starting transfers between devices, per_device(): grad = lax.all_to_all(grad, 'z', 0, 0, tiled=True)  7.86 us
  transfers between devices with their start and end apart: 28, of which 15 were waited for; matrix products, arithmetic and copies ran while one was open for 11% of the time, Pallas kernels for 11%

profile of v4, /device:TPU:24, one launch (start us, length us, event | category | flops | bytes accessed | tf_op | source)
XLA Modules:
  0.0 147.7 jit_solution(6788009742855626998)
XLA Ops:
  0.6 0.1 collective-permute-start.2
  0.8 2.4 %constant_dynamic-slice_fusion.11 = bf16[256,2304]{1,0:T(8,128)(2,1)} fusion(bf16[256,18432]{1,0:T(8,128)(2,1)} %param.6, s32[]{:T(128)S(6)} %select_n.112), kind=kLoop, calls=%fused_computation.19 | loop fusion | bytes 2359300 | tf_op jit(solution)/shard_map/dynamic_slice | solution.py:235
  3.1 0.5 collective-permute-start.4
  3.6 6.7 %constant_dynamic-slice_fusion.4 = (bf16[256,2304]{1,0:T(8,128)(2,1)}, bf16[256,2304]{1,0:T(8,128)(2,1)}, bf16[256,2304]{1,0:T(8,128)(2,1)}, bf16[256,2304]{1,0:...) fusion(bf16[256,18432]{1,0:T(8,128)(2,1)} %param.6, ...), kind=kLoop, calls=%fused_computation.12 | loop fusion | bytes 16515100 | tf_op jit(solution)/shard_map/dynamic_slice | solution.py:235
  10.4 0.5 collective-permute-start.7
  10.9 1.3 copy-done.1
  12.1 1.4 shard_map.102
  13.5 1.5 %collective-permute-start.5 = (bf16[1152,256]{1,0:T(8,128)(2,1)}, bf16[1152,256]{1,0:T(8,128)(2,1)}, u32[]{:S(2)}, u32[]{:S(2)}) collective-permute-start(bf16[1152,256]{1,0:T(8,128)(2,1)} %shard_map.102), channel_id=1, source_target_pairs={{0,128},{8,136},{16,144},{24,152},{64,72},{72,80},{80,88},{88,64},... | collective-permute-start | bytes 1769480 | tf_op jit(solution)/shard_map/ppermute | solution.py:247
  15.0 0.5 shard_map.106
  15.5 1.8 %collective-permute-start.10 = (bf16[1152,256]{1,0:T(8,128)(2,1)S(1)}, bf16[1152,256]{1,0:T(8,128)(2,1)}, u32[]{:S(2)}, u32[]{:S(2)}) collective-permute-start(bf16[1152,256]{1,0:T(8,128)(2,1)S(1)} %shard_map.106), channel_id=1, source_target_pairs={{0,160},{8,168},{16,176},{24,184},{64,88},{72,64},{80,72},{88,80},... | collective-permute-start | bytes 1769480 | tf_op jit(solution)/shard_map/ppermute | solution.py:247
  17.4 0.1 copy.11
  17.6 0.8 dynamic-slice_bitcast_fusion
  18.4 2.3 %collective-permute-start = (bf16[4,72,256]{2,1,0:T(8,128)(2,1)S(1)}, bf16[4,72,256]{2,1,0:T(8,128)(2,1)S(1)}, u32[]{:S(2)}, u32[]{:S(2)}) collective-permute-start(bf16[4,72,256]{2,1,0:T(8,128)(2,1)S(1)} %pad_maximum_fusion), channel_id=1, source_target_pairs={{192,0},{128,8},{0,16},{64,24},{8,128},{72,136},{200,144},{136,152... | collective-permute-start | bytes 442376 | tf_op jit(solution)/shard_map/ppermute | solution.py:265
  20.7 1.3 copy-done.3
  22.0 0.5 shard_map.105
  22.5 0.4 collective-permute-start.9
  23.0 1.6 %shard_map.104 = bf16[1152,256]{1,0:T(8,128)(2,1)S(1)} custom-call(bf16[256,2304]{1,0:T(8,128)(2,1)S(1)} %copy-done.2, bf16[256,2304]{1,0:T(8,128)(2,1)} %collective-permute-done.7.other_ref, bf16[256,256]{1,0:T(8,128)(2,1)S(1)} %copy-done.4, bf16[256,256]{1,0:T(8,128)(2,1)S(1)} %collective-permute-done.2.cot_other_ref), custom_call_target="tpu_custom_call" | custom-call | flops 1000 | bytes 1000 | tf_op jit(solution)/shard_map/pallas_call | solution.py:102
  24.6 1.9 %collective-permute-done.5.refs_0_ = bf16[1152,256]{1,0:T(8,128)(2,1)} collective-permute-done((bf16[1152,256]{1,0:T(8,128)(2,1)}, bf16[1152,256]{1,0:T(8,128)(2,1)}, u32[]{:S(2)}, u32[]{:S(2)}) %collective-permute-start.5) | collective-permute-done | bytes 589856 | tf_op jit(solution)/shard_map/ppermute | solution.py:247
  26.5 1.1 collective-permute-start.8
  27.6 1.7 %shard_map.103 = bf16[1152,256]{1,0:T(8,128)(2,1)S(1)} custom-call(bf16[256,2304]{1,0:T(8,128)(2,1)S(1)} %copy-done.3, bf16[256,2304]{1,0:T(8,128)(2,1)S(1)} %collective-permute-done.3.other_ref, bf16[256,256]{1,0:T(8,128)(2,1)S(1)} %copy-done.4, bf16[256,256]{1,0:T(8,128)(2,1)S(1)} %collective-permute-done.2.cot_other_ref, ...), custom_call_target="tpu_custom_call" | custom-call | flops 1000 | bytes 1000 | tf_op jit(solution)/shard_map/pallas_call | solution.py:102
  29.2 0.2 collective-permute-done.10.refs_0_
  29.5 0.8 collective-permute-start.6
  30.3 1.8 %shard_map.107 = bf16[1152,256]{1,0:T(8,128)(2,1)S(1)} custom-call(bf16[256,2304]{1,0:T(8,128)(2,1)S(1)} %copy-done.2, bf16[256,2304]{1,0:T(8,128)(2,1)} %collective-permute-done.7.other_ref, bf16[256,256]{1,0:T(8,128)(2,1)S(1)} %copy-done.4, bf16[256,256]{1,0:T(8,128)(2,1)S(1)} %collective-permute-done.2.cot_other_ref, ...), custom_call_target="tpu_custom_call" | custom-call | flops 1000 | bytes 1000 | tf_op jit(solution)/shard_map/pallas_call | solution.py:102
  32.1 3.3 %collective-permute-start.11 = (bf16[1152,256]{1,0:T(8,128)(2,1)S(1)}, bf16[1152,256]{1,0:T(8,128)(2,1)S(1)}, u32[]{:S(2)}, u32[]{:S(2)}) collective-permute-start(bf16[1152,256]{1,0:T(8,128)(2,1)S(1)} %shard_map.107), channel_id=1, source_target_pairs={{0,160},{8,168},{16,176},{24,184},{64,88},{72,64},{80,72},{88,80},... | collective-permute-start | bytes 1769480 | tf_op jit(solution)/shard_map/ppermute | solution.py:247
  35.4 2.1 %shard_map.101.total_ref = f32[2304,256]{1,0:T(8,128)S(1)} custom-call(bf16[256,2304]{1,0:T(8,128)(2,1)S(1)} %copy-done.9, bf16[256,2304]{1,0:T(8,128)(2,1)} %collective-permute-done.1.other_ref, bf16[256,256]{1,0:T(8,128)(2,1)S(1)} %copy-done.4, bf16[256,256]{1,0:T(8,128)(2,1)S(1)} %collective-permute-done.2.cot_other_ref, ...), custom_call_target="tpu_custom_call" | custom-call | flops 1000 | bytes 1000 | tf_op jit(solution)/shard_map/pallas_call | solution.py:102
  37.5 3.6 %collective-permute-done.6.a_ref = bf16[1152,256]{1,0:T(8,128)(2,1)S(1)} collective-permute-done((bf16[1152,256]{1,0:T(8,128)(2,1)S(1)}, bf16[1152,256]{1,0:T(8,128)(2,1)S(1)}, u32[]{:S(2)}, u32[]{:S(2)}) %collective-permute-start.6) | collective-permute-done | bytes 589856 | tf_op jit(solution)/shard_map/ppermute | solution.py:247
  41.1 2.6 %collective-permute-done.11.e_ref = bf16[1152,256]{1,0:T(8,128)(2,1)S(1)} collective-permute-done((bf16[1152,256]{1,0:T(8,128)(2,1)S(1)}, bf16[1152,256]{1,0:T(8,128)(2,1)S(1)}, u32[]{:S(2)}, u32[]{:S(2)}) %collective-permute-start.11) | collective-permute-done | bytes 589856 | tf_op jit(solution)/shard_map/ppermute | solution.py:247
  43.7 0.5 shard_map.108
  44.3 1.0 collective-permute-start.12
  45.3 1.1 collective-permute-start.13
  46.4 1.6 %collective-permute-start.14 = (bf16[8,72,256]{2,1,0:T(8,128)(2,1)S(1)}, bf16[8,72,256]{2,1,0:T(8,128)(2,1)S(1)}, u32[]{:S(2)}, u32[]{:S(2)}) collective-permute-start(bf16[8,72,256]{2,1,0:T(8,128)(2,1)S(1)} %get-tuple-element.62), channel_id=1, source_target_pairs={{0,16},{8,24},{16,0},{24,8},{64,96},{72,104},{80,112},{88,120},{12... | collective-permute-start | bytes 884744 | tf_op jit(solution)/shard_map/ppermute | solution.py:279
  48.0 3.1 %collective-permute-done.12.a_ref = bf16[8,72,256]{2,1,0:T(8,128)(2,1)S(1)} collective-permute-done((bf16[8,72,256]{2,1,0:T(8,128)(2,1)S(1)}, bf16[8,72,256]{2,1,0:T(8,128)(2,1)S(1)}, u32[]{:S(2)}, u32[]{:S(2)}) %collective-permute-start.12) | collective-permute-done | bytes 294944 | tf_op jit(solution)/shard_map/ppermute | solution.py:279
  51.1 5.3 %collective-permute-done.13.b_ref = bf16[8,72,256]{2,1,0:T(8,128)(2,1)S(1)} collective-permute-done((bf16[8,72,256]{2,1,0:T(8,128)(2,1)S(1)}, bf16[8,72,256]{2,1,0:T(8,128)(2,1)S(1)}, u32[]{:S(2)}, u32[]{:S(2)}) %collective-permute-start.13) | collective-permute-done | bytes 294944 | tf_op jit(solution)/shard_map/ppermute | solution.py:279
  56.4 0.8 shard_map.109
  57.2 7.9 %all-to-all-start = ((bf16[8,72,256]{2,1,0:T(8,128)(2,1)}), bf16[8,72,256]{2,1,0:T(8,128)(2,1)S(1)}, u32[]{:S(2)}, u32[]{:S(2)}) async-start(bf16[8,72,256]{2,1,0:T(8,128)(2,1)} %shard_map.109), calls=%async_computation | async-start | bytes 589824 | tf_op jit(solution)/shard_map/all_to_all | solution.py:282
  65.1 0.2 convert_multiply_fusion.table_ref
  65.3 4.5 %constant_dynamic-slice_fusion = (bf16[256,2304]{1,0:T(8,128)(2,1)}, bf16[256,2304]{1,0:T(8,128)(2,1)}, bf16[256,2304]{1,0:T(8,128)(2,1)}, bf16[256,2304]{1,0:T(8,128)(2,1)}) fusion(bf16[256,18432]{1,0:T(8,128)(2,1)} %param.6, s32[]{:T(128)S(6)} %select_n.132, s32[]{:T(128)S(6)} %select_n.130, s32[]{:T(128)S(6)} %select_n.129, s32[]{:T(128)S(6)} %select_n.131), kind=kLoop, calls=%fused_computation.8 | loop fusion | bytes 9437200 | tf_op jit(solution)/shard_map/dynamic_slice | solution.py:235
  69.9 6.1 %all-to-all-done.terms_ref = bf16[8,72,256]{2,1,0:T(8,128)(2,1)S(1)} async-done(((bf16[8,72,256]{2,1,0:T(8,128)(2,1)}), bf16[8,72,256]{2,1,0:T(8,128)(2,1)S(1)}, u32[]{:S(2)}, u32[]{:S(2)}) %all-to-all-start) | async-done | bytes 294944 | tf_op jit(solution)/shard_map/all_to_all | solution.py:282
  75.9 0.7 shard_map.110
  76.7 13.2 %all_to_all.10.slab_ref = bf16[8,72,256]{2,1,0:T(8,128)(2,1)S(1)} all-to-all(bf16[8,72,256]{2,1,0:T(8,128)(2,1)S(1)} %get-tuple-element.69), channel_id=1, replica_groups=mesh['xl'=2,'c'=2,'xh'=2,'y'=4,'z'=8] {'z'}, dimensions={0} | all-to-all | bytes 589824 | tf_op jit(solution)/shard_map/all_to_all | solution.py:286
  89.9 1.2 collective-permute-start.17
  91.1 1.2 collective-permute-start.16
  92.3 1.1 collective-permute-start.15
  93.3 4.5 %collective-permute-done.17.refs_0_.e_ref = bf16[11,72,256]{2,1,0:T(8,128)(2,1)S(1)} collective-permute-done((bf16[11,72,256]{2,1,0:T(8,128)(2,1)S(1)}, bf16[11,72,256]{2,1,0:T(8,128)(2,1)S(1)}, u32[]{:S(2)}, u32[]{:S(2)}) %collective-permute-start.17) | collective-permute-done | bytes 405536 | tf_op jit(solution)/shard_map/ppermute | solution.py:288
  97.9 2.8 %collective-permute-done.16.refs_2_.d_ref = bf16[11,72,256]{2,1,0:T(8,128)(2,1)} collective-permute-done((bf16[11,72,256]{2,1,0:T(8,128)(2,1)S(1)}, bf16[11,72,256]{2,1,0:T(8,128)(2,1)}, u32[]{:S(2)}, u32[]{:S(2)}) %collective-permute-start.16) | collective-permute-done | bytes 405536 | tf_op jit(solution)/shard_map/ppermute | solution.py:288
  100.7 4.2 %collective-permute-done.15.refs_1_.b_ref = bf16[11,72,256]{2,1,0:T(8,128)(2,1)} collective-permute-done((bf16[11,72,256]{2,1,0:T(8,128)(2,1)S(1)}, bf16[11,72,256]{2,1,0:T(8,128)(2,1)}, u32[]{:S(2)}, u32[]{:S(2)}) %collective-permute-start.15) | collective-permute-done | bytes 405536 | tf_op jit(solution)/shard_map/ppermute | solution.py:288
  105.0 1.1 collective-permute-done.18.ready_ref
  106.1 1.3 shard_map.113
  107.4 3.8 %collective-permute-start.21 = (bf16[1152,256]{1,0:T(8,128)(2,1)S(1)}, bf16[1152,256]{1,0:T(8,128)(2,1)S(1)}, u32[]{:S(2)}, u32[]{:S(2)}) collective-permute-start(bf16[1152,256]{1,0:T(8,128)(2,1)S(1)} %bitcast.18), channel_id=1, source_target_pairs={{0,160},{8,168},{16,176},{24,184},{64,88},{72,64},{80,72},{88,80},... | collective-permute-start | bytes 1769480 | tf_op jit(solution)/shard_map/ppermute | solution.py:247
  111.1 3.3 %collective-permute-start.23 = (bf16[1152,256]{1,0:T(8,128)(2,1)S(1)}, bf16[1152,256]{1,0:T(8,128)(2,1)S(1)}, u32[]{:S(2)}, u32[]{:S(2)}) collective-permute-start(bf16[1152,256]{1,0:T(8,128)(2,1)S(1)} %bitcast.16), channel_id=1, source_target_pairs={{0,160},{8,168},{16,176},{24,184},{64,88},{72,64},{80,72},{88,80},... | collective-permute-start | bytes 1769480 | tf_op jit(solution)/shard_map/ppermute | solution.py:247
  114.4 4.1 %collective-permute-done.21.lower_ref = bf16[1152,256]{1,0:T(8,128)(2,1)S(1)} collective-permute-done((bf16[1152,256]{1,0:T(8,128)(2,1)S(1)}, bf16[1152,256]{1,0:T(8,128)(2,1)S(1)}, u32[]{:S(2)}, u32[]{:S(2)}) %collective-permute-start.21) | collective-permute-done | bytes 589856 | tf_op jit(solution)/shard_map/ppermute | solution.py:247
  118.5 3.7 %collective-permute-start.22 = (bf16[1152,256]{1,0:T(8,128)(2,1)S(1)}, bf16[1152,256]{1,0:T(8,128)(2,1)S(1)}, u32[]{:S(2)}, u32[]{:S(2)}) collective-permute-start(bf16[1152,256]{1,0:T(8,128)(2,1)S(1)} %collective-permute-done.21.lower_ref), channel_id=1, source_target_pairs={{0,160},{8,168},{16,176},{24,184},{64,88},{72,64},{80,72},{88,80},... | collective-permute-start | bytes 1769480 | tf_op jit(solution)/shard_map/ppermute | solution.py:247
  122.2 0.1 collective-permute-start.26
  122.3 2.2 %shard_map.114.refs_0_ = f32[512,256]{1,0:T(8,128)S(1)} custom-call(bf16[256,2304]{1,0:T(8,128)(2,1)S(1)} %copy-done.8, bf16[256,2304]{1,0:T(8,128)(2,1)} %collective-permute-done.1.other_ref, bf16[1152,256]{1,0:T(8,128)(2,1)S(1)} %bitcast.17, bf16[1152,256]{1,0:T(8,128)(2,1)S(1)} %bitcast.20), custom_call_target="tpu_custom_call" | custom-call | flops 1000 | bytes 1000 | tf_op jit(solution)/shard_map/pallas_call | solution.py:221
  124.5 4.0 %collective-permute-done.24.lower_ref = bf16[1152,256]{1,0:T(8,128)(2,1)S(1)} collective-permute-done((bf16[1152,256]{1,0:T(8,128)(2,1)S(1)}, bf16[1152,256]{1,0:T(8,128)(2,1)S(1)}, u32[]{:S(2)}, u32[]{:S(2)}) %collective-permute-start.24) | collective-permute-done | bytes 589856 | tf_op jit(solution)/shard_map/ppermute | solution.py:247
  128.5 2.1 %shard_map.115.refs_0_ = f32[512,256]{1,0:T(8,128)S(1)} custom-call(bf16[256,2304]{1,0:T(8,128)(2,1)S(1)} %copy-done.7, bf16[256,2304]{1,0:T(8,128)(2,1)} %collective-permute-done.7.other_ref, bf16[1152,256]{1,0:T(8,128)(2,1)S(1)} %collective-permute-done.19.upper_ref, bf16[1152,256]{1,0:T(8,128)(2,1)S(1)} %collective-permute-done.24.lower_ref, ...), custom_call_target="tpu_custom_call" | custom-call | flops 1000 | bytes 1000 | tf_op jit(solution)/shard_map/pallas_call | solution.py:221
  130.7 0.8 shard_map.116.refs_0_
  131.5 4.8 %collective-permute-done.22.lower_ref = bf16[1152,256]{1,0:T(8,128)(2,1)S(1)} collective-permute-done((bf16[1152,256]{1,0:T(8,128)(2,1)S(1)}, bf16[1152,256]{1,0:T(8,128)(2,1)S(1)}, u32[]{:S(2)}, u32[]{:S(2)}) %collective-permute-start.22) | collective-permute-done | bytes 589856 | tf_op jit(solution)/shard_map/ppermute | solution.py:247
  136.3 0.8 shard_map.117
  137.2 3.8 %collective-permute-start.25 = (f32[256,256]{1,0:T(8,128)S(1)}, f32[256,256]{1,0:T(8,128)S(1)}, u32[]{:S(2)}, u32[]{:S(2)}) collective-permute-start(f32[256,256]{1,0:T(8,128)S(1)} %slice.9), channel_id=1, source_target_pairs={{0,64},{64,0},{1,65},{65,1},{2,66},{66,2},{3,67},{67,3},{4,68},{68... | collective-permute-start | bytes 786440 | tf_op jit(solution)/shard_map/ppermute | solution.py:302
  141.0 4.6 %collective-permute-done.26.home_ref = bf16[13,72,256]{2,1,0:T(8,128)(2,1)S(1)} collective-permute-done((bf16[13,72,256]{2,1,0:T(8,128)(2,1)S(1)}, bf16[13,72,256]{2,1,0:T(8,128)(2,1)S(1)}, u32[]{:S(2)}, u32[]{:S(2)}) %collective-permute-start.26) | collective-permute-done | bytes 479264 | tf_op jit(solution)/shard_map/ppermute | solution.py:296
  145.6 0.8 shard_map.118
  146.3 0.7 copy.12
  147.0 0.7 fusion
  (50 shorter events, 0.5 us)
Async XLA Ops:
  0.6 16.9 %copy-start = (bf16[288,256]{1,0:T(8,128)(2,1)S(1)}, bf16[288,256]{1,0:T(8,128)(2,1)}, u32[]{:S(2)}) copy-start(bf16[288,256]{1,0:T(8,128)(2,1)} %param.8) | copy-start | bytes 442372
  0.6 2.5 %collective-permute-start.2 = (bf16[256,256]{1,0:T(8,128)(2,1)}, bf16[256,256]{1,0:T(8,128)(2,1)S(1)}, u32[]{:S(2)}, u32[]{:S(2)}) collective-permute-start(bf16[256,256]{1,0:T(8,128)(2,1)} %cot_own_ref.13), channel_id=1, source_target_pairs={{0,64},{64,0},{1,65},{65,1},{2,66},{66,2},{3,67},{67,3},{4,68},{68... | collective-permute-start | bytes 393224 | tf_op jit(solution)/shard_map/ppermute | solution.py:244
  3.1 7.7 %copy-start.4 = (bf16[256,256]{1,0:T(8,128)(2,1)S(1)}, bf16[256,256]{1,0:T(8,128)(2,1)}, u32[]{:S(2)}) copy-start(bf16[256,256]{1,0:T(8,128)(2,1)} %cot_own_ref.13) | copy-start | bytes 393220
  3.1 7.7 %collective-permute-start.4 = (bf16[256,2304]{1,0:T(8,128)(2,1)}, bf16[256,2304]{1,0:T(8,128)(2,1)S(1)}, u32[]{:S(2)}, u32[]{:S(2)}) collective-permute-start(bf16[256,2304]{1,0:T(8,128)(2,1)} %constant_dynamic-slice_fusion.11), channel_id=1, source_target_pairs={{0,64},{64,0},{1,65},{65,1},{2,66},{66,2},{3,67},{67,3},{4,68},{68... | collective-permute-start | bytes 3538952 | tf_op jit(solution)/shard_map/ppermute | solution.py:244
  10.3 8.1 %collective-permute-start.3 = (bf16[256,2304]{1,0:T(8,128)(2,1)}, bf16[256,2304]{1,0:T(8,128)(2,1)S(1)}, u32[]{:S(2)}, u32[]{:S(2)}) collective-permute-start(bf16[256,2304]{1,0:T(8,128)(2,1)} %get-tuple-element.54), channel_id=1, source_target_pairs={{0,64},{64,0},{1,65},{65,1},{2,66},{66,2},{3,67},{67,3},{4,68},{68... | collective-permute-start | bytes 3538952 | tf_op jit(solution)/shard_map/ppermute | solution.py:244
  10.4 12.2 %collective-permute-start.7 = (bf16[256,2304]{1,0:T(8,128)(2,1)}, bf16[256,2304]{1,0:T(8,128)(2,1)}, u32[]{:S(2)}, u32[]{:S(2)}) collective-permute-start(bf16[256,2304]{1,0:T(8,128)(2,1)} %get-tuple-element.58), channel_id=1, source_target_pairs={{0,64},{64,0},{1,65},{65,1},{2,66},{66,2},{3,67},{67,3},{4,68},{68... | collective-permute-start | bytes 3538952 | tf_op jit(solution)/shard_map/ppermute | solution.py:244
  10.8 24.6 %collective-permute-start.1 = (bf16[256,2304]{1,0:T(8,128)(2,1)}, bf16[256,2304]{1,0:T(8,128)(2,1)}, u32[]{:S(2)}, u32[]{:S(2)}) collective-permute-start(bf16[256,2304]{1,0:T(8,128)(2,1)} %get-tuple-element.52), channel_id=1, source_target_pairs={{0,64},{64,0},{1,65},{65,1},{2,66},{66,2},{3,67},{67,3},{4,68},{68... | collective-permute-start | bytes 3538952 | tf_op jit(solution)/shard_map/ppermute | solution.py:244
  10.9 1.3 copy-start.1
  13.5 3.8 %copy-start.10 = (bf16[288,2]{0,1:T(2,128)(2,1)S(1)}, bf16[288,2]{0,1:T(2,128)(2,1)}, u32[]{:S(2)}) copy-start(bf16[288,2]{0,1:T(2,128)(2,1)} %param.10) | copy-start | bytes 3460
  13.5 13.0 %collective-permute-start.5 = (bf16[1152,256]{1,0:T(8,128)(2,1)}, bf16[1152,256]{1,0:T(8,128)(2,1)}, u32[]{:S(2)}, u32[]{:S(2)}) collective-permute-start(bf16[1152,256]{1,0:T(8,128)(2,1)} %shard_map.102), channel_id=1, source_target_pairs={{0,128},{8,136},{16,144},{24,152},{64,72},{72,80},{80,88},{88,64},... | collective-permute-start | bytes 1769480 | tf_op jit(solution)/shard_map/ppermute | solution.py:247
  15.5 14.0 %collective-permute-start.10 = (bf16[1152,256]{1,0:T(8,128)(2,1)S(1)}, bf16[1152,256]{1,0:T(8,128)(2,1)}, u32[]{:S(2)}, u32[]{:S(2)}) collective-permute-start(bf16[1152,256]{1,0:T(8,128)(2,1)S(1)} %shard_map.106), channel_id=1, source_target_pairs={{0,160},{8,168},{16,176},{24,184},{64,88},{72,64},{80,72},{88,80},... | collective-permute-start | bytes 1769480 | tf_op jit(solution)/shard_map/ppermute | solution.py:247
  18.4 4.6 %copy-start.2 = (bf16[256,2304]{1,0:T(8,128)(2,1)S(1)}, bf16[256,2304]{1,0:T(8,128)(2,1)}, u32[]{:S(2)}) copy-start(bf16[256,2304]{1,0:T(8,128)(2,1)} %get-tuple-element.57.own_ref) | copy-start | bytes 3538948
  18.4 13.7 %collective-permute-start = (bf16[4,72,256]{2,1,0:T(8,128)(2,1)S(1)}, bf16[4,72,256]{2,1,0:T(8,128)(2,1)S(1)}, u32[]{:S(2)}, u32[]{:S(2)}) collective-permute-start(bf16[4,72,256]{2,1,0:T(8,128)(2,1)S(1)} %pad_maximum_fusion), channel_id=1, source_target_pairs={{192,0},{128,8},{0,16},{64,24},{8,128},{72,136},{200,144},{136,152... | collective-permute-start | bytes 442376 | tf_op jit(solution)/shard_map/ppermute | solution.py:265
  20.7 1.3 copy-start.3
  22.5 15.0 %collective-permute-start.9 = (bf16[1152,256]{1,0:T(8,128)(2,1)S(1)}, bf16[1152,256]{1,0:T(8,128)(2,1)S(1)}, u32[]{:S(2)}, u32[]{:S(2)}) collective-permute-start(bf16[1152,256]{1,0:T(8,128)(2,1)S(1)} %shard_map.105), channel_id=1, source_target_pairs={{0,128},{8,136},{16,144},{24,152},{64,72},{72,80},{80,88},{88,64},... | collective-permute-start | bytes 1769480 | tf_op jit(solution)/shard_map/ppermute | solution.py:247
  26.5 11.0 %collective-permute-start.8 = (bf16[1152,256]{1,0:T(8,128)(2,1)S(1)}, bf16[1152,256]{1,0:T(8,128)(2,1)S(1)}, u32[]{:S(2)}, u32[]{:S(2)}) collective-permute-start(bf16[1152,256]{1,0:T(8,128)(2,1)S(1)} %shard_map.104), channel_id=1, source_target_pairs={{0,160},{8,168},{16,176},{24,184},{64,88},{72,64},{80,72},{88,80},... | collective-permute-start | bytes 1769480 | tf_op jit(solution)/shard_map/ppermute | solution.py:247
  29.2 6.1 %copy-start.9 = (bf16[256,2304]{1,0:T(8,128)(2,1)S(1)}, bf16[256,2304]{1,0:T(8,128)(2,1)}, u32[]{:S(2)}) copy-start(bf16[256,2304]{1,0:T(8,128)(2,1)} %get-tuple-element.51.own_ref) | copy-start | bytes 3538948
  29.5 11.7 %collective-permute-start.6 = (bf16[1152,256]{1,0:T(8,128)(2,1)S(1)}, bf16[1152,256]{1,0:T(8,128)(2,1)S(1)}, u32[]{:S(2)}, u32[]{:S(2)}) collective-permute-start(bf16[1152,256]{1,0:T(8,128)(2,1)S(1)} %shard_map.103), channel_id=1, source_target_pairs={{0,128},{8,136},{16,144},{24,152},{64,72},{72,80},{80,88},{88,64},... | collective-permute-start | bytes 1769480 | tf_op jit(solution)/shard_map/ppermute | solution.py:247
  32.1 11.6 %collective-permute-start.11 = (bf16[1152,256]{1,0:T(8,128)(2,1)S(1)}, bf16[1152,256]{1,0:T(8,128)(2,1)S(1)}, u32[]{:S(2)}, u32[]{:S(2)}) collective-permute-start(bf16[1152,256]{1,0:T(8,128)(2,1)S(1)} %shard_map.107), channel_id=1, source_target_pairs={{0,160},{8,168},{16,176},{24,184},{64,88},{72,64},{80,72},{88,80},... | collective-permute-start | bytes 1769480 | tf_op jit(solution)/shard_map/ppermute | solution.py:247
  44.3 6.8 %collective-permute-start.12 = (bf16[8,72,256]{2,1,0:T(8,128)(2,1)S(1)}, bf16[8,72,256]{2,1,0:T(8,128)(2,1)S(1)}, u32[]{:S(2)}, u32[]{:S(2)}) collective-permute-start(bf16[8,72,256]{2,1,0:T(8,128)(2,1)S(1)} %get-tuple-element.60), channel_id=1, source_target_pairs={{0,8},{8,16},{16,24},{24,0},{64,192},{72,200},{80,208},{88,216},{1... | collective-permute-start | bytes 884744 | tf_op jit(solution)/shard_map/ppermute | solution.py:279
  45.3 11.1 %collective-permute-start.13 = (bf16[8,72,256]{2,1,0:T(8,128)(2,1)S(1)}, bf16[8,72,256]{2,1,0:T(8,128)(2,1)S(1)}, u32[]{:S(2)}, u32[]{:S(2)}) collective-permute-start(bf16[8,72,256]{2,1,0:T(8,128)(2,1)S(1)} %get-tuple-element.61), channel_id=1, source_target_pairs={{0,24},{8,0},{16,8},{24,16},{64,224},{72,232},{80,240},{88,248},{1... | collective-permute-start | bytes 884744 | tf_op jit(solution)/shard_map/ppermute | solution.py:279
  46.4 10.0 %collective-permute-start.14 = (bf16[8,72,256]{2,1,0:T(8,128)(2,1)S(1)}, bf16[8,72,256]{2,1,0:T(8,128)(2,1)S(1)}, u32[]{:S(2)}, u32[]{:S(2)}) collective-permute-start(bf16[8,72,256]{2,1,0:T(8,128)(2,1)S(1)} %get-tuple-element.62), channel_id=1, source_target_pairs={{0,16},{8,24},{16,0},{24,8},{64,96},{72,104},{80,112},{88,120},{12... | collective-permute-start | bytes 884744 | tf_op jit(solution)/shard_map/ppermute | solution.py:279
  57.2 18.7 %all-to-all-start = ((bf16[8,72,256]{2,1,0:T(8,128)(2,1)}), bf16[8,72,256]{2,1,0:T(8,128)(2,1)S(1)}, u32[]{:S(2)}, u32[]{:S(2)}) async-start(bf16[8,72,256]{2,1,0:T(8,128)(2,1)} %shard_map.109), calls=%async_computation | async-start | bytes 589824 | tf_op jit(solution)/shard_map/all_to_all | solution.py:282
  89.9 8.0 %collective-permute-start.17 = (bf16[11,72,256]{2,1,0:T(8,128)(2,1)S(1)}, bf16[11,72,256]{2,1,0:T(8,128)(2,1)S(1)}, u32[]{:S(2)}, u32[]{:S(2)}) collective-permute-start(bf16[11,72,256]{2,1,0:T(8,128)(2,1)S(1)} %shard_map.111.a_ref), channel_id=1, source_target_pairs={{0,8},{8,16},{16,24},{24,0},{64,192},{72,200},{80,208},{88,216},{1... | collective-permute-start | bytes 1216520 | tf_op jit(solution)/shard_map/ppermute | solution.py:288
  91.1 9.6 %collective-permute-start.16 = (bf16[11,72,256]{2,1,0:T(8,128)(2,1)S(1)}, bf16[11,72,256]{2,1,0:T(8,128)(2,1)}, u32[]{:S(2)}, u32[]{:S(2)}) collective-permute-start(bf16[11,72,256]{2,1,0:T(8,128)(2,1)S(1)} %shard_map.111.a_ref), channel_id=1, source_target_pairs={{0,16},{8,24},{16,0},{24,8},{64,96},{72,104},{80,112},{88,120},{12... | collective-permute-start | bytes 1216520 | tf_op jit(solution)/shard_map/ppermute | solution.py:288
  92.3 12.6 %collective-permute-start.15 = (bf16[11,72,256]{2,1,0:T(8,128)(2,1)S(1)}, bf16[11,72,256]{2,1,0:T(8,128)(2,1)}, u32[]{:S(2)}, u32[]{:S(2)}) collective-permute-start(bf16[11,72,256]{2,1,0:T(8,128)(2,1)S(1)} %shard_map.111.a_ref), channel_id=1, source_target_pairs={{0,24},{8,0},{16,8},{24,16},{64,224},{72,232},{80,240},{88,248},{1... | collective-permute-start | bytes 1216520 | tf_op jit(solution)/shard_map/ppermute | solution.py:288
  93.3 29.0 %copy-start.8 = (bf16[256,2304]{1,0:T(8,128)(2,1)S(1)}, bf16[256,2304]{1,0:T(8,128)(2,1)}, u32[]{:S(2)}) copy-start(bf16[256,2304]{1,0:T(8,128)(2,1)} %get-tuple-element.75.own_ref) | copy-start | bytes 3538948
  104.9 1.2 collective-permute-start.18
  107.4 11.2 %collective-permute-start.21 = (bf16[1152,256]{1,0:T(8,128)(2,1)S(1)}, bf16[1152,256]{1,0:T(8,128)(2,1)S(1)}, u32[]{:S(2)}, u32[]{:S(2)}) collective-permute-start(bf16[1152,256]{1,0:T(8,128)(2,1)S(1)} %bitcast.18), channel_id=1, source_target_pairs={{0,160},{8,168},{16,176},{24,184},{64,88},{72,64},{80,72},{88,80},... | collective-permute-start | bytes 1769480 | tf_op jit(solution)/shard_map/ppermute | solution.py:247
  111.1 11.1 %collective-permute-start.19 = (bf16[1152,256]{1,0:T(8,128)(2,1)S(1)}, bf16[1152,256]{1,0:T(8,128)(2,1)S(1)}, u32[]{:S(2)}, u32[]{:S(2)}) collective-permute-start(bf16[1152,256]{1,0:T(8,128)(2,1)S(1)} %bitcast.15), channel_id=1, source_target_pairs={{0,128},{8,136},{16,144},{24,152},{64,72},{72,80},{80,88},{88,64},... | collective-permute-start | bytes 1769480 | tf_op jit(solution)/shard_map/ppermute | solution.py:247
  111.1 17.4 %collective-permute-start.24 = (bf16[1152,256]{1,0:T(8,128)(2,1)S(1)}, bf16[1152,256]{1,0:T(8,128)(2,1)S(1)}, u32[]{:S(2)}, u32[]{:S(2)}) collective-permute-start(bf16[1152,256]{1,0:T(8,128)(2,1)S(1)} %bitcast.19), channel_id=1, source_target_pairs={{0,128},{8,136},{16,144},{24,152},{64,72},{72,80},{80,88},{88,64},... | collective-permute-start | bytes 1769480 | tf_op jit(solution)/shard_map/ppermute | solution.py:247
  111.1 19.5 %collective-permute-start.23 = (bf16[1152,256]{1,0:T(8,128)(2,1)S(1)}, bf16[1152,256]{1,0:T(8,128)(2,1)S(1)}, u32[]{:S(2)}, u32[]{:S(2)}) collective-permute-start(bf16[1152,256]{1,0:T(8,128)(2,1)S(1)} %bitcast.16), channel_id=1, source_target_pairs={{0,160},{8,168},{16,176},{24,184},{64,88},{72,64},{80,72},{88,80},... | collective-permute-start | bytes 1769480 | tf_op jit(solution)/shard_map/ppermute | solution.py:247
  118.5 17.8 %collective-permute-start.22 = (bf16[1152,256]{1,0:T(8,128)(2,1)S(1)}, bf16[1152,256]{1,0:T(8,128)(2,1)S(1)}, u32[]{:S(2)}, u32[]{:S(2)}) collective-permute-start(bf16[1152,256]{1,0:T(8,128)(2,1)S(1)} %collective-permute-done.21.lower_ref), channel_id=1, source_target_pairs={{0,160},{8,168},{16,176},{24,184},{64,88},{72,64},{80,72},{88,80},... | collective-permute-start | bytes 1769480 | tf_op jit(solution)/shard_map/ppermute | solution.py:247
  122.2 14.1 %collective-permute-start.20 = (bf16[1152,256]{1,0:T(8,128)(2,1)S(1)}, bf16[1152,256]{1,0:T(8,128)(2,1)S(1)}, u32[]{:S(2)}, u32[]{:S(2)}) collective-permute-start(bf16[1152,256]{1,0:T(8,128)(2,1)S(1)} %collective-permute-done.19.upper_ref), channel_id=1, source_target_pairs={{0,128},{8,136},{16,144},{24,152},{64,72},{72,80},{80,88},{88,64},... | collective-permute-start | bytes 1769480 | tf_op jit(solution)/shard_map/ppermute | solution.py:247
  122.2 6.3 %copy-start.7 = (bf16[256,2304]{1,0:T(8,128)(2,1)S(1)}, bf16[256,2304]{1,0:T(8,128)(2,1)}, u32[]{:S(2)}) copy-start(bf16[256,2304]{1,0:T(8,128)(2,1)} %get-tuple-element.74.own_ref) | copy-start | bytes 3538948
  122.2 23.3 %collective-permute-start.26 = (bf16[13,72,256]{2,1,0:T(8,128)(2,1)S(1)}, bf16[13,72,256]{2,1,0:T(8,128)(2,1)S(1)}, u32[]{:S(2)}, u32[]{:S(2)}) collective-permute-start(bf16[13,72,256]{2,1,0:T(8,128)(2,1)S(1)} %get-tuple-element.76), channel_id=1, source_target_pairs={{0,192},{8,128},{16,0},{24,64},{128,8},{136,72},{144,200},{152,136... | collective-permute-start | bytes 1437704 | tf_op jit(solution)/shard_map/ppermute | solution.py:296
  124.5 6.2 %copy-start.6 = (bf16[256,2304]{1,0:T(8,128)(2,1)S(1)}, bf16[256,2304]{1,0:T(8,128)(2,1)}, u32[]{:S(2)}) copy-start(bf16[256,2304]{1,0:T(8,128)(2,1)} %get-tuple-element.73.own_ref) | copy-start | bytes 3538948
  130.7 5.6 %copy-start.5 = (bf16[256,2304]{1,0:T(8,128)(2,1)S(1)}, bf16[256,2304]{1,0:T(8,128)(2,1)}, u32[]{:S(2)}) copy-start(bf16[256,2304]{1,0:T(8,128)(2,1)} %get-tuple-element.67.own_ref) | copy-start | bytes 3538948
  137.2 9.8 %collective-permute-start.25 = (f32[256,256]{1,0:T(8,128)S(1)}, f32[256,256]{1,0:T(8,128)S(1)}, u32[]{:S(2)}, u32[]{:S(2)}) collective-permute-start(f32[256,256]{1,0:T(8,128)S(1)} %slice.9), channel_id=1, source_target_pairs={{0,64},{64,0},{1,65},{65,1},{2,66},{66,2},{3,67},{67,3},{4,68},{68... | collective-permute-start | bytes 786440 | tf_op jit(solution)/shard_map/ppermute | solution.py:302
